TPU v7x, 256 devices: a whole 4x4x8 slice. The times are simulated.
256 devices in a mesh: fsdp: 64 (over x, z, core), rep: 4 (over y).
Axes of the slice: x: 4, y: 4, z: 8, core: 2. Of those that a mesh axis runs over, the one named last changes fastest.
Arguments:
- gate_shards: bfloat16 [4, 7168, 2048], P(None, 'fsdp', 'rep'), may hold values from -6 to 6
- up_shards: bfloat16 [4, 7168, 2048], P(None, 'fsdp', 'rep'), may hold values from -6 to 6
- norm_gain: float32 [7168], P('fsdp'), may hold values from 0.1 to 1.9
- matching: int32 [64], replicated, may hold values from 0 to 63, each once
- replica_slots: int32 [4, 4], replicated, may hold values from 0 to 7, as said below
- replica_count: int32 [4], replicated, may hold values from 1 to 4, as said below
Outputs:
- joined: bfloat16 [64, 7168, 512], P('fsdp')
Inputs may be any that keep to these rules, and one draw needn't show every extreme that they name: `replica_slots`: every physical slot 0 to 7 appears exactly once among the first replica_count[e] entries of the rows e together; those entries of a row are ascending; the remaining entries of a row are arbitrary slots. `replica_count`: the counts sum to 8 and stay at or below 4; one expert has exactly 4 replicas in every draw. `matching`: each rank appears once.
All inputs are finite; a program needn't handle non-finite values.
Results may differ from a plain program's by a relative error of at most 0.001.
Values may be sent and summed in bfloat16 or wider, within the bound.
No kernel may reach another device: no remote copies, remote signals or barrier semaphores. Data moves between devices by JAX's collectives and lax.ppermute only.
A program may use at most 64 MiB of HBM per device.

v0:
```python
import jax
import jax.numpy as jnp
from jax import lax
from jax.sharding import PartitionSpec as P


def slot_owner(replica_slots, replica_count, slots):
    live = jnp.arange(replica_slots.shape[1])[None, :] < replica_count[:, None]
    hits = live[:, :, None] & (replica_slots[:, :, None] == jnp.arange(slots)[None, None, :])
    owners = jnp.arange(replica_slots.shape[0], dtype=jnp.int32)[:, None, None] * hits.astype(
        jnp.int32
    )
    return jnp.sum(owners, axis=(0, 1))


def inverse_order(matching):
    count = matching.shape[0]
    match_grid = matching[None, :] == jnp.arange(count, dtype=jnp.int32)[:, None]
    ranks = jnp.where(match_grid, jnp.arange(count, dtype=jnp.int32)[None, :], 0)
    return jnp.sum(ranks, axis=1)


def fold_rows(weights, gain_rows):
    return (weights.astype(jnp.float32) * gain_rows[:, None]).astype(jnp.bfloat16)


def pick_units(weights, expert_pick, block_pick, block_count):
    experts, rows, units = weights.shape
    return weights.reshape(experts, rows, units // block_count, block_count)[
        expert_pick, :, :, block_pick
    ]


def alternate(gate_part, up_part):
    shape = gate_part.shape
    return jnp.stack((gate_part, up_part), axis=-1).reshape(shape[:-1] + (2 * shape[-1],))


def local(gate_shards, up_shards, norm_gain, matching, replica_slots, replica_count):
    devices = lax.axis_size("fsdp")
    block_count = min(8, devices // 8)
    rows = gate_shards.shape[1]
    owners = slot_owner(replica_slots, replica_count, devices // block_count)
    targets = jnp.arange(devices, dtype=jnp.int32)
    expert_pick = owners[targets // block_count]
    block_pick = targets % block_count
    inverse = inverse_order(matching)
    gate_all, up_all = (
        lax.all_gather(gate_shards, "rep", axis=2, tiled=True),
        lax.all_gather(up_shards, "rep", axis=2, tiled=True),
    )
    outgoing = alternate(
        pick_units(gate_all, expert_pick, block_pick, block_count),
        pick_units(up_all, expert_pick, block_pick, block_count),
    )
    received = lax.all_to_all(outgoing, "fsdp", split_axis=0, concat_axis=0, tiled=True)
    portion = received[inverse].reshape(devices * rows, received.shape[2])
    gain_all = lax.all_gather(norm_gain, "fsdp", axis=0, tiled=True)
    gain_model = gain_all.reshape(devices, rows)[inverse].reshape(devices * rows)
    portion = fold_rows(portion, gain_model)
    return portion[None]


def solution(mesh):
    return jax.shard_map(
        local,
        mesh=mesh,
        in_specs=(P(None, "fsdp", "rep"), P(None, "fsdp", "rep"), P("fsdp"), P(), P(), P()),
        out_specs=P("fsdp", None, None),
        check_vma=False,
    )
```

profile of v0, /device:TPU:64, one launch (start us, length us, event | category | flops | bytes accessed | tf_op | source)
XLA Modules:
  0.0 544.2 jit_solution(16833138758784412576)
XLA Ops:
  6.5 0.0 all-gather.3.cloned.1.call-start
  6.5 0.7 all-gather.3.cloned.1.call-update
  7.3 0.0 all-gather.5.cloned.1.call-start
  7.3 0.7 all-gather.5.cloned.1.call-update
  8.0 0.7 iota_compare_fusion.2
  8.7 0.8 select_reduce_fusion.1
  9.5 0.7 fusion.11
  10.2 5.0 fusion.5
  15.2 27.5 %all-gather.3.cloned.1.call-done = bf16[4,112,2048]{2,1,0:T(8,128)(2,1)} async-done(((bf16[4,112,512]{2,1,0:T(8,128)(2,1)}), bf16[4,112,2048]{2,1,0:T(8,128)(2,1)}) %all-gather.3.cloned.1.call-update) | async-done | bytes 1835024 | tf_op jit(solution)/shard_map/all_gather | solution.py:49
  42.7 3.8 copy.19
  46.5 3.0 copy.20
  49.6 26.2 %all-gather.5.cloned.1.call-done = bf16[4,112,2048]{2,1,0:T(8,128)(2,1)} async-done(((bf16[4,112,512]{2,1,0:T(8,128)(2,1)}), bf16[4,112,2048]{2,1,0:T(8,128)(2,1)}) %all-gather.5.cloned.1.call-update) | async-done | bytes 1835024 | tf_op jit(solution)/shard_map/all_gather | solution.py:50
  75.8 3.8 copy.21
  79.6 4.3 copy.22
  83.9 2.6 gather_fusion
  86.5 4.1 gather_fusion.1
  90.6 6.9 %pad_maximum_fusion = bf16[64,112,256,2]{2,1,0,3:T(8,128)(2,1)} fusion(bf16[64,112,256,1]{2,1,0,3:T(8,128)(2,1)} %bitcast.63, bf16[64,112,256,1]{2,1,0,3:T(8,128)(2,1)} %bitcast.62), kind=kLoop, calls=%fused_computation.6 | loop fusion | flops 3670016 | bytes 14680064 | tf_op jit(solution)/shard_map/stack | solution.py:36
  97.5 11.8 %copy.23 = bf16[64,112,256,2]{1,0,3,2:T(8,128)(2,1)} copy(bf16[64,112,256,2]{2,1,0,3:T(8,128)(2,1)} %pad_maximum_fusion) | data formatting | bytes 14680064 | tf_op jit(solution)/shard_map/stack | solution.py:36
  109.2 12.1 %copy.24 = bf16[64,112,512]{2,1,0:T(8,128)(2,1)} copy(bf16[64,112,512]{1,0,2:T(8,128)(2,1)} %bitcast.60) | data formatting | bytes 14680064 | tf_op jit(solution)/shard_map/reshape | solution.py:36
  121.3 0.0 copy-start.2
  121.3 0.0 copy-start
  121.3 0.0 copy-start.1
  121.3 10.7 %all-to-all-start = ((bf16[64,112,512]{2,1,0:T(8,128)(2,1)}), bf16[64,112,512]{2,1,0:T(8,128)(2,1)}, u32[]{:S(2)}, u32[]{:S(2)}) async-start(bf16[64,112,512]{2,1,0:T(8,128)(2,1)} %copy.24), calls=%async_computation | async-start | bytes 14680064 | tf_op jit(solution)/shard_map/all_to_all | solution.py:56
  132.0 0.0 copy-done.2
  132.0 0.7 dynamic-slice
  133.3 0.0 copy-done
  133.3 0.3 dynamic-update-slice
  133.6 387.9 %all-reduce = f32[7168]{0:T(1024)S(1)} all-reduce(f32[7168]{0:T(1024)S(1)} %dynamic-update-slice), channel_id=1, replica_groups=mesh['fsdp'=64,'rep'=4] {'fsdp'}, use_global_device_ids=true, to_apply=%add | all-reduce | flops 7168 | bytes 57344
  521.5 0.1 reshape.180
  521.5 0.0 copy-done.1
  521.5 0.1 select_reduce_fusion
  521.7 0.6 gather_fusion.3
  522.3 0.1 mul.27
  522.4 0.0 all-to-all-done
  522.4 7.1 %gather_fusion.2 = bf16[64,112,512]{2,1,0:T(8,128)(2,1)} fusion(bf16[64,112,512]{2,1,0:T(8,128)(2,1)} %all-to-all-done, s32[1024]{0:T(1024)S(1)} %pad_clamp_fusion), kind=kCustom, calls=%fused_computation.2 | custom fusion | bytes 14680320 | tf_op jit(solution)/shard_map/gather | solution.py:57
  529.5 7.9 %fusion = bf16[1,7168,512]{2,1,0:T(8,128)(2,1)} fusion(f32[7168]{0:T(1024)S(1)} %mul.27, bf16[1,7168,512]{2,1,0:T(8,128)(2,1)} %bitcast.61), kind=kLoop, calls=%fused_computation.5 | loop fusion | flops 11010048 | bytes 14708736 | tf_op jit(solution)/shard_map/convert_element_type | solution.py:24
  (3 shorter events, 0.0 us)
Async XLA Ops:
  6.5 36.2 %all-gather.3.cloned.1.call-start = ((), (), s32[]{:S(2)}) async-start(), calls=%async_computation.1 | async-start | bytes 2293760 | tf_op jit(solution)/shard_map/all_gather | solution.py:49
  7.3 68.5 %all-gather.5.cloned.1.call-start = ((), (), s32[]{:S(2)}) async-start(), calls=%async_computation.2 | async-start | bytes 2293760 | tf_op jit(solution)/shard_map/all_gather | solution.py:50
  121.3 10.7 %copy-start.2 = (u32[256]{0:T(256)S(1)}, u32[256]{0:T(256)}, u32[]{:S(2)}) copy-start(u32[256]{0:T(256)} %constant.78) | copy-start | bytes 3076
  121.3 12.0 %copy-start = (f32[112]{0:T(128)S(1)}, f32[112]{0:T(128)}, u32[]{:S(2)}) copy-start(f32[112]{0:T(128)} %param.8) | copy-start | bytes 1348
  121.3 400.2 %copy-start.1 = (s32[64]{0:T(128)S(1)}, s32[64]{0:T(128)}, u32[]{:S(2)}) copy-start(s32[64]{0:T(128)} %param.9) | copy-start | bytes 772
  121.3 401.1 %all-to-all-start = ((bf16[64,112,512]{2,1,0:T(8,128)(2,1)}), bf16[64,112,512]{2,1,0:T(8,128)(2,1)}, u32[]{:S(2)}, u32[]{:S(2)}) async-start(bf16[64,112,512]{2,1,0:T(8,128)(2,1)} %copy.24), calls=%async_computation | async-start | bytes 14680064 | tf_op jit(solution)/shard_map/all_to_all | solution.py:56
Sparse Core Ops, SparseCore 0:
  9.2 33.4 all-gather.2
  44.5 31.2 all-gather.4
where the time goes:
time: 555 us; the launch traced here: 544 us
  blocking collectives  388 us (70%)
  waiting for transfers between devices  55.1 us (10%)
  local copies, waits for them, and re-layouts  55.1 us (10%)
  other arithmetic  21.4 us (4%)
  between operations  14.1 us (3%)
  starting transfers between devices  10.7 us (2%)
    unnamed x1, blocking collectives  388 us
    all_gather x1, waiting for transfers between devices, local(): lax.all_gather(gate_shards, 'rep', axis=2, tiled=True)  27.5 us
    all_gather x1, waiting for transfers between devices, local(): lax.all_gather(up_shards, 'rep', axis=2, tiled=True)  26.2 us
    reshape x1, local copies, waits for them, and re-layouts, alternate(): jnp.stack((gate_part, up_part), axis=-1)  12.1 us
    another operation x1, local copies, waits for them, and re-layouts, alternate(): jnp.stack((gate_part, up_part), axis=-1)  11.8 us
  transfers between devices with their start and end apart: 3, of which 2 were waited for; matrix products, arithmetic and copies ran while one was open for 3% of the time, Pallas kernels for 0%

commit v1 on v0

v1 whole, which is shorter than its diff:
```python
import functools

import jax
import jax.numpy as jnp
from jax import lax
from jax.experimental import pallas as pl
from jax.experimental.pallas import tpu as pltpu
from jax.sharding import PartitionSpec as P

NX, NZ, NY = 4, 8, 4
SLOTS, BLOCKS = 8, 8
GROUPS = ((0,), (1, 7), (2, 6, 3, 5, 4))
CLASSES = ((0,), (1, 7), (2, 6), (3, 5), (4,))
BF16 = jnp.bfloat16


def place():
    me = lax.axis_index("fsdp")
    return me // (2 * NZ), (me // 2) % NZ, me % 2


def pick_matrix(core):
    unit = lax.broadcasted_iota(jnp.int32, (1024, 512), 0)
    column = lax.broadcasted_iota(jnp.int32, (1024, 512), 1)
    lane = column % 128
    wanted = (lane % 2) * 512 + 8 * (lane // 2) + 2 * (column // 128) + core
    return (unit == wanted).astype(BF16)


def prepare_kernel(slots_ref, count_ref, gate, up, gate_far, up_far, gain, gain_far, matrix, *rest):
    outs, (picked, owner) = rest[:-2], rest[-2:]
    experts, rows = gate.shape[:2]
    x, z, _ = place()
    for e in range(experts):
        for k in range(slots_ref.shape[1]):
            @pl.when(k < count_ref[e])
            def _():
                owner[slots_ref[e, k]] = e
    for side, (g, u, scale) in enumerate(((gate, up, gain), (gate_far, up_far, gain_far))):
        for e in range(experts):
            got = jnp.dot(g[e], matrix[:512, :], preferred_element_type=jnp.float32)
            got += jnp.dot(u[e], matrix[512:, :], preferred_element_type=jnp.float32)
            got = (got * scale[...]).astype(BF16)
            for zl in range(4):
                picked[e * 4 + zl, side] = got[:, zl * 128 : (zl + 1) * 128]
    for g, group in enumerate(GROUPS):
        for k, dz in enumerate(group):
            zt = (z + dz) % NZ
            for dx in range(NX):
                xt = (x + dx) % NX
                source = owner[xt * 2 + zt // 4] * 4 + zt % 4
                outs[g * NX + dx][k] = picked[source]


def prepare(gate, up, gain, matrix, replica_slots, replica_count):
    rows = gate.shape[1]
    flip = [(i, i ^ 1) for i in range(2 * NX * NZ)]
    gate_far = lax.ppermute(gate, "fsdp", flip)
    up_far = lax.ppermute(up, "fsdp", flip)
    gain_far = lax.ppermute(gain, "fsdp", flip)
    shapes = [
        jax.ShapeDtypeStruct((len(group), 2, rows, 128), BF16) for group in GROUPS for _ in range(NX)
    ]
    vmem = pl.BlockSpec(memory_space=pltpu.VMEM)
    smem = pl.BlockSpec(memory_space=pltpu.SMEM)
    outs = pl.pallas_call(
        prepare_kernel,
        out_shape=shapes,
        in_specs=[smem, smem] + [vmem] * 7,
        out_specs=[vmem] * len(shapes),
        scratch_shapes=[pltpu.VMEM((16, 2, rows, 128), BF16), pltpu.SMEM((SLOTS,), jnp.int32)],
        compiler_params=pltpu.CompilerParams(vmem_limit_bytes=32 * 1024 * 1024),
        name="prepare",
    )(
        replica_slots, replica_count, gate, up, gate_far, up_far,
        gain.reshape(rows, 1), gain_far.reshape(rows, 1), matrix,
    )
    return [outs[g * NX : (g + 1) * NX] for g in range(len(GROUPS))]


def place_kernel(dzs, base, matching, *refs):
    n = len(dzs)
    own, (left, right, far_left, far_right) = refs[:n], refs[n : n + 4]
    out, held, built, load_sems, save_sems = refs[-5:]
    count, rows = 8 * n, own[0].shape[1]
    half = count // 2
    x, z, core = place()
    y = lax.axis_index("rep")
    sources = [(0, 8 * k, ref.at[pl.ds(0, 8)]) for k, ref in enumerate(own)]
    sources += [
        (3, 0, left.at[pl.ds(0, count)]),
        (1, 0, right.at[pl.ds(0, count)]),
        (2, 0, far_left.at[pl.ds(base, half)]),
        (2, half, far_right.at[pl.ds(base, half)]),
    ]
    loads = []
    for step, at, ref in sources:
        load = pltpu.make_async_copy(
            ref, held.at[step, pl.ds(at, ref.shape[0])], load_sems.at[len(loads)]
        )
        load.start()
        loads.append(load)
    for load in loads:
        load.wait()
    saves = []
    for k, dz in enumerate(dzs):
        for dx in range(NX):
            for side in range(2):
                at = (k * NX + dx) * 2 + side
                for step in range(NY):
                    column = pl.multiple_of(((y + step) % NY) * 128, 128)
                    built[at, :, pl.ds(column, 128)] = held[step, at]
                block = matching[(((x - dx) % NX) * NZ + (z - dz) % NZ) * 2 + (core ^ side)]
                row = pl.multiple_of(block * rows, 16)
                save = pltpu.make_async_copy(built.at[at], out.at[pl.ds(row, rows)], save_sems.at[at])
                save.start()
                saves.append(save)
    for save in saves:
        save.wait()


def place_class(dzs, base, out, matching, own, left, right, far_left, far_right, devices):
    rows = own[0].shape[1]
    n = len(dzs)
    anywhere = pl.BlockSpec(memory_space=pl.ANY)
    args = [matching, *own, left, right, far_left, far_right] + ([] if out is None else [out])
    return pl.pallas_call(
        functools.partial(place_kernel, dzs, base),
        out_shape=jax.ShapeDtypeStruct((devices * rows, 512), BF16),
        in_specs=[pl.BlockSpec(memory_space=pltpu.SMEM)] + [anywhere] * (len(args) - 1),
        out_specs=anywhere,
        scratch_shapes=[
            pltpu.VMEM((NY, 8 * n, rows, 128), BF16),
            pltpu.VMEM((8 * n, rows, 512), BF16),
            pltpu.SemaphoreType.DMA((n + 4,)),
            pltpu.SemaphoreType.DMA((8 * n,)),
        ],
        input_output_aliases={} if out is None else {len(args) - 1: 0},
        compiler_params=pltpu.CompilerParams(vmem_limit_bytes=16 * 1024 * 1024),
        name="place",
    )(*args)


def local(gate, up, norm_gain, matching, replica_slots, replica_count):
    devices = lax.axis_size("fsdp")
    rows = gate.shape[1]
    _, _, core = place()
    matrix = pick_matrix(core)
    parts = prepare(gate, up, norm_gain, matrix, replica_slots, replica_count)

    def along_x(dx):
        return [(i, ((i // 16 + dx) % NX) * 16 + i % 16) for i in range(devices)]

    def along_z(dz):
        return [(i, (i // 16) * 16 + ((i // 2 + dz) % NZ) * 2 + i % 2) for i in range(devices)]

    def along_y(dy):
        return [(i, (i + dy) % NY) for i in range(NY)]

    ready = {}
    for group, pieces in zip(GROUPS, parts):
        arrived = [pieces[0]] + [lax.ppermute(pieces[dx], "fsdp", along_x(dx)) for dx in range(1, NX)]
        for k, dz in enumerate(group):
            own = jnp.stack([a[k] for a in arrived]).reshape(8, rows, 128)
            ready[dz] = lax.ppermute(own, "fsdp", along_z(dz)) if dz else own

    out = None
    left, right, owns = [], [], []
    for step in range(len(CLASSES) + 2):
        to_right, to_left = [], []
        if step < len(CLASSES):
            owns.append([ready[dz] for dz in CLASSES[step]])
            to_right += owns[step]
            to_left += owns[step]
        base = sum(p.shape[0] for p in to_right)
        if step >= 2:
            count = 8 * len(CLASSES[step - 2])
            to_right.append(left[step - 2][: count // 2])
            to_left.append(right[step - 2][count // 2 : count])
        left.append(lax.ppermute(jnp.concatenate(to_right), "rep", along_y(1)))
        right.append(lax.ppermute(jnp.concatenate(to_left), "rep", along_y(-1)))
        if step >= 2:
            k = step - 2
            out = place_class(
                CLASSES[k], base, out, matching, owns[k], left[k], right[k], left[step], right[step], devices
            )
    return out[None]


def solution(mesh):
    return jax.shard_map(
        local,
        mesh=mesh,
        in_specs=(P(None, "fsdp", "rep"), P(None, "fsdp", "rep"), P("fsdp"), P(), P(), P()),
        out_specs=P("fsdp", None, None),
        check_vma=False,
    )
```

time: 555 us -> 134 us (0.24)
  the two profiles are of different devices: /device:TPU:64 before, /device:TPU:66 now
where the time goes in v1:
time: 134 us
  starting transfers between devices  62 us (46%)
  waiting for transfers between devices  47.1 us (35%)
  Pallas kernels  18.9 us (14%)
  local copies, waits for them, and re-layouts  4.54 us (3%)
    ppermute x7, starting transfers between devices, local(): right.append(lax.ppermute(jnp.concatenate(to_left), 'rep', along_y(-1)))  22.3 us
    ppermute x7, waiting for transfers between devices, local(): left.append(lax.ppermute(jnp.concatenate(to_right), 'rep', along_y(1)))  20.5 us
    ppermute x7, starting transfers between devices, local(): ready[dz] = lax.ppermute(own, 'fsdp', along_z(dz)) if dz else own  19.2 us
    ppermute x9, starting transfers between devices, local(): lax.ppermute(pieces[dx], 'fsdp', along_x(dx))  17.5 us
    pallas_call x5, Pallas kernels, place_class(): pl.pallas_call(functools.partial(place_kernel, dzs, base), out_shape=jax....  16.8 us
    ppermute x7, waiting for transfers between devices, local(): ready[dz] = lax.ppermute(own, 'fsdp', along_z(dz)) if dz else own  14 us
    ppermute x9, waiting for transfers between devices, local(): lax.ppermute(pieces[dx], 'fsdp', along_x(dx))  11.5 us
    unnamed x11, local copies, waits for them, and re-layouts  3.39 us
  transfers between devices with their start and end apart: 33, of which 10 were waited for; matrix products, arithmetic and copies ran while one was open for 2% of the time, Pallas kernels for 10%

profile of v1, /device:TPU:66, one launch (start us, length us, event | category | flops | bytes accessed | tf_op | source)
XLA Modules:
  0.0 134.0 jit_solution(3530084204812255636)
XLA Ops:
  0.0 0.5 collective-permute-start.1
  0.5 0.0 collective-permute-start.2
  0.5 0.4 fusion.10.matrix
  0.9 0.8 copy.11.gain
  1.7 1.0 collective-permute-done.2
  2.7 0.1 copy.12.gain_far
  2.8 0.0 collective-permute-done.gate_far
  2.8 0.0 copy-start
  2.8 1.0 copy-done
  3.8 1.0 copy-done.1
  4.9 0.7 copy-done.3
  5.5 0.7 copy-done.4
  6.2 2.1 %prepare.1 = (bf16[1,2,112,128]{3,2,1,0:T(8,128)(2,1)S(1)}, bf16[1,2,112,128]{3,2,1,0:T(8,128)(2,1)S(1)}, bf16[1,2,112,128]{3,2,1,0:T(8,128)(2,1)S(1)}, bf16[1,2...) custom-call(s32[4,4]{1,0:T(4,128)S(1)} %copy-done.3, ...), custom_call_target="tpu_custom_call" | custom-call | tf_op jit(solution)/shard_map/prepare/pallas_call | solution.py:66
  8.3 1.6 %collective-permute-start.3 = (bf16[5,2,112,128]{3,2,1,0:T(8,128)(2,1)S(1)}, bf16[5,2,112,128]{3,2,1,0:T(8,128)(2,1)S(1)}, u32[]{:S(2)}, u32[]{:S(2)}) collective-permute-start(bf16[5,2,112,128]{3,2,1,0:T(8,128)(2,1)S(1)} %get-tuple-element.18), channel_id=1, source_target_pairs={{0,64},{4,68},{8,72},{12,76},{16,80},{20,84},{24,88},{28,92},{32,9... | collective-permute-start | bytes 860168 | tf_op jit(solution)/shard_map/ppermute | solution.py:162
  9.8 1.1 collective-permute-start.4
  11.0 2.5 %collective-permute-start.10 = (bf16[1,2,112,128]{3,2,1,0:T(8,128)(2,1)S(1)}, bf16[1,2,112,128]{3,2,1,0:T(8,128)(2,1)S(1)}, u32[]{:S(2)}, u32[]{:S(2)}) collective-permute-start(bf16[1,2,112,128]{3,2,1,0:T(8,128)(2,1)S(1)} %get-tuple-element.23), channel_id=1, source_target_pairs={{0,128},{4,132},{8,136},{12,140},{16,144},{20,148},{24,152},{28,15... | collective-permute-start | bytes 172040 | tf_op jit(solution)/shard_map/ppermute | solution.py:162
  13.5 0.5 collective-permute-start.11
  14.0 1.5 %collective-permute-start.9 = (bf16[1,2,112,128]{3,2,1,0:T(8,128)(2,1)S(1)}, bf16[1,2,112,128]{3,2,1,0:T(8,128)(2,1)S(1)}, u32[]{:S(2)}, u32[]{:S(2)}) collective-permute-start(bf16[1,2,112,128]{3,2,1,0:T(8,128)(2,1)S(1)} %get-tuple-element.22), channel_id=1, source_target_pairs={{0,64},{4,68},{8,72},{12,76},{16,80},{20,84},{24,88},{28,92},{32,9... | collective-permute-start | bytes 172040 | tf_op jit(solution)/shard_map/ppermute | solution.py:162
  15.5 6.4 %collective-permute-done.10 = bf16[1,2,112,128]{3,2,1,0:T(8,128)(2,1)S(1)} collective-permute-done((bf16[1,2,112,128]{3,2,1,0:T(8,128)(2,1)S(1)}, bf16[1,2,112,128]{3,2,1,0:T(8,128)(2,1)S(1)}, u32[]{:S(2)}, u32[]{:S(2)}) %collective-permute-start.10) | collective-permute-done | bytes 57376 | tf_op jit(solution)/shard_map/ppermute | solution.py:162
  21.9 6.1 %collective-permute-start.5 = (bf16[5,2,112,128]{3,2,1,0:T(8,128)(2,1)S(1)}, bf16[5,2,112,128]{3,2,1,0:T(8,128)(2,1)S(1)}, u32[]{:S(2)}, u32[]{:S(2)}) collective-permute-start(bf16[5,2,112,128]{3,2,1,0:T(8,128)(2,1)S(1)} %get-tuple-element.20), channel_id=1, source_target_pairs={{0,192},{4,196},{8,200},{12,204},{16,208},{20,212},{24,216},{28,22... | collective-permute-start | bytes 860168 | tf_op jit(solution)/shard_map/ppermute | solution.py:162
  28.0 2.1 %collective-permute-start.23 = (bf16[2,2,112,128]{3,2,1,0:T(8,128)(2,1)S(1)}, bf16[2,2,112,128]{3,2,1,0:T(8,128)(2,1)S(1)}, u32[]{:S(2)}, u32[]{:S(2)}) collective-permute-start(bf16[2,2,112,128]{3,2,1,0:T(8,128)(2,1)S(1)} %get-tuple-element.27), channel_id=1, source_target_pairs={{0,128},{4,132},{8,136},{12,140},{16,144},{20,148},{24,152},{28,15... | collective-permute-start | bytes 344072 | tf_op jit(solution)/shard_map/ppermute | solution.py:162
  30.1 2.7 %collective-permute-done.22 = bf16[2,2,112,128]{3,2,1,0:T(8,128)(2,1)S(1)} collective-permute-done((bf16[2,2,112,128]{3,2,1,0:T(8,128)(2,1)S(1)}, bf16[2,2,112,128]{3,2,1,0:T(8,128)(2,1)S(1)}, u32[]{:S(2)}, u32[]{:S(2)}) %collective-permute-start.22) | collective-permute-done | bytes 114720 | tf_op jit(solution)/shard_map/ppermute | solution.py:162
  32.7 2.1 %collective-permute-start.24 = (bf16[2,2,112,128]{3,2,1,0:T(8,128)(2,1)S(1)}, bf16[2,2,112,128]{3,2,1,0:T(8,128)(2,1)S(1)}, u32[]{:S(2)}, u32[]{:S(2)}) collective-permute-start(bf16[2,2,112,128]{3,2,1,0:T(8,128)(2,1)S(1)} %get-tuple-element.28), channel_id=1, source_target_pairs={{0,192},{4,196},{8,200},{12,204},{16,208},{20,212},{24,216},{28,22... | collective-permute-start | bytes 344072 | tf_op jit(solution)/shard_map/ppermute | solution.py:162
  34.9 2.5 %collective-permute-done.23 = bf16[2,2,112,128]{3,2,1,0:T(8,128)(2,1)S(1)} collective-permute-done((bf16[2,2,112,128]{3,2,1,0:T(8,128)(2,1)S(1)}, bf16[2,2,112,128]{3,2,1,0:T(8,128)(2,1)S(1)}, u32[]{:S(2)}, u32[]{:S(2)}) %collective-permute-start.23) | collective-permute-done | bytes 114720 | tf_op jit(solution)/shard_map/ppermute | solution.py:162
  37.3 1.6 %collective-permute-start.12 = (bf16[8,112,128]{2,1,0:T(8,128)(2,1)S(1)}, bf16[8,112,128]{2,1,0:T(8,128)(2,1)S(1)}, u32[]{:S(2)}, u32[]{:S(2)}) collective-permute-start(bf16[8,112,128]{2,1,0:T(8,128)(2,1)S(1)} %bitcast.11), channel_id=1, source_target_pairs={{0,1},{1,2},{2,3},{3,0},{4,5},{5,6},{6,7},{7,4},{8,9},{9,10},{10,1... | collective-permute-start | bytes 688136 | tf_op jit(solution)/shard_map/ppermute | solution.py:180
  39.0 2.5 %collective-permute-start.15 = (bf16[8,112,128]{2,1,0:T(8,128)(2,1)S(1)}, bf16[8,112,128]{2,1,0:T(8,128)(2,1)S(1)}, u32[]{:S(2)}, u32[]{:S(2)}) collective-permute-start(bf16[8,112,128]{2,1,0:T(8,128)(2,1)S(1)} %bitcast.12), channel_id=1, source_target_pairs={{0,3},{1,0},{2,1},{3,2},{4,7},{5,4},{6,5},{7,6},{8,11},{9,8},{10,9... | collective-permute-start | bytes 688136 | tf_op jit(solution)/shard_map/ppermute | solution.py:181
  41.6 0.2 collective-permute-start.26
  41.8 0.0 collective-permute-done.4
  41.8 2.1 %collective-permute-start.25 = (bf16[8,112,128]{2,1,0:T(8,128)(2,1)S(1)}, bf16[8,112,128]{2,1,0:T(8,128)(2,1)S(1)}, u32[]{:S(2)}, u32[]{:S(2)}) collective-permute-start(bf16[8,112,128]{2,1,0:T(8,128)(2,1)S(1)} %bitcast.18), channel_id=1, source_target_pairs={{0,8},{4,12},{8,16},{12,20},{16,24},{20,28},{24,32},{28,36},{32,40... | collective-permute-start | bytes 688136 | tf_op jit(solution)/shard_map/ppermute | solution.py:165
  44.0 0.0 collective-permute-done.5
  44.1 4.6 %collective-permute-start.7 = (bf16[8,112,128]{2,1,0:T(8,128)(2,1)S(1)}, bf16[8,112,128]{2,1,0:T(8,128)(2,1)S(1)}, u32[]{:S(2)}, u32[]{:S(2)}) collective-permute-start(bf16[8,112,128]{2,1,0:T(8,128)(2,1)S(1)} %bitcast.16), channel_id=1, source_target_pairs={{0,16},{4,20},{8,24},{12,28},{16,32},{20,36},{24,40},{28,44},{32,4... | collective-permute-start | bytes 688136 | tf_op jit(solution)/shard_map/ppermute | solution.py:165
  48.7 4.2 %collective-permute-done.25.refs_0_ = bf16[8,112,128]{2,1,0:T(8,128)(2,1)S(1)} collective-permute-done((bf16[8,112,128]{2,1,0:T(8,128)(2,1)S(1)}, bf16[8,112,128]{2,1,0:T(8,128)(2,1)S(1)}, u32[]{:S(2)}, u32[]{:S(2)}) %collective-permute-start.25) | collective-permute-done | bytes 229408 | tf_op jit(solution)/shard_map/ppermute | solution.py:165
  52.9 0.0 collective-permute-done.26.refs_1_
  52.9 0.1 collective-permute-start.27
  53.1 7.0 %collective-permute-start.8 = (bf16[8,112,128]{2,1,0:T(8,128)(2,1)S(1)}, bf16[8,112,128]{2,1,0:T(8,128)(2,1)S(1)}, u32[]{:S(2)}, u32[]{:S(2)}) collective-permute-start(bf16[8,112,128]{2,1,0:T(8,128)(2,1)S(1)} %bitcast.20), channel_id=1, source_target_pairs={{0,48},{4,52},{8,56},{12,60},{16,0},{20,4},{24,8},{28,12},{32,16},... | collective-permute-start | bytes 688136 | tf_op jit(solution)/shard_map/ppermute | solution.py:165
  60.1 0.0 collective-permute-done.12.refs_1_
  60.1 0.1 collective-permute-start.21
  60.2 3.3 %collective-permute-start.29 = (bf16[16,112,128]{2,1,0:T(8,128)(2,1)S(1)}, bf16[16,112,128]{2,1,0:T(8,128)(2,1)S(1)}, u32[]{:S(2)}, u32[]{:S(2)}) collective-permute-start(bf16[16,112,128]{2,1,0:T(8,128)(2,1)S(1)} %constant_dynamic-update-slice_fusion), channel_id=1, source_target_pairs={{0,3},{1,0},{2,1},{3,2},{4,7},{5,4},{6,5},{7,6},{8,11},{9,8},{10,9... | collective-permute-start | bytes 1376264 | tf_op jit(solution)/shard_map/ppermute | solution.py:181
  63.6 5.1 %collective-permute-start.20 = (bf16[8,112,128]{2,1,0:T(8,128)(2,1)S(1)}, bf16[8,112,128]{2,1,0:T(8,128)(2,1)S(1)}, u32[]{:S(2)}, u32[]{:S(2)}) collective-permute-start(bf16[8,112,128]{2,1,0:T(8,128)(2,1)S(1)} %bitcast.17), channel_id=1, source_target_pairs={{0,24},{4,28},{8,32},{12,36},{16,40},{20,44},{24,48},{28,52},{32,5... | collective-permute-start | bytes 688136 | tf_op jit(solution)/shard_map/ppermute | solution.py:165
  68.7 8.0 %collective-permute-done.8.refs_1_ = bf16[8,112,128]{2,1,0:T(8,128)(2,1)S(1)} collective-permute-done((bf16[8,112,128]{2,1,0:T(8,128)(2,1)S(1)}, bf16[8,112,128]{2,1,0:T(8,128)(2,1)S(1)}, u32[]{:S(2)}, u32[]{:S(2)}) %collective-permute-start.8) | collective-permute-done | bytes 229408 | tf_op jit(solution)/shard_map/ppermute | solution.py:165
  76.7 0.1 pad_maximum_fusion.5
  76.7 0.1 collective-permute-start.13
  76.8 3.2 %collective-permute-start.16 = (bf16[20,112,128]{2,1,0:T(8,128)(2,1)S(1)}, bf16[20,112,128]{2,1,0:T(8,128)(2,1)S(1)}, u32[]{:S(2)}, u32[]{:S(2)}) collective-permute-start(bf16[20,112,128]{2,1,0:T(8,128)(2,1)S(1)} %get-tuple-element.31), channel_id=1, source_target_pairs={{0,3},{1,0},{2,1},{3,2},{4,7},{5,4},{6,5},{7,6},{8,11},{9,8},{10,9... | collective-permute-start | bytes 1720328 | tf_op jit(solution)/shard_map/ppermute | solution.py:181
  80.1 0.1 collective-permute-start.6
  80.3 1.8 %collective-permute-done.21.refs_1_ = bf16[8,112,128]{2,1,0:T(8,128)(2,1)S(1)} collective-permute-done((bf16[8,112,128]{2,1,0:T(8,128)(2,1)S(1)}, bf16[8,112,128]{2,1,0:T(8,128)(2,1)S(1)}, u32[]{:S(2)}, u32[]{:S(2)}) %collective-permute-start.21) | collective-permute-done | bytes 229408 | tf_op jit(solution)/shard_map/ppermute | solution.py:165
  82.1 0.1 pad_maximum_fusion.2
  82.2 0.0 copy-start.2
  82.2 0.4 collective-permute-start.28
  82.6 3.2 %collective-permute-start.30 = (bf16[24,112,128]{2,1,0:T(8,128)(2,1)S(1)}, bf16[24,112,128]{2,1,0:T(8,128)(2,1)S(1)}, u32[]{:S(2)}, u32[]{:S(2)}) collective-permute-start(bf16[24,112,128]{2,1,0:T(8,128)(2,1)S(1)} %get-tuple-element.29), channel_id=1, source_target_pairs={{0,3},{1,0},{2,1},{3,2},{4,7},{5,4},{6,5},{7,6},{8,11},{9,8},{10,9... | collective-permute-start | bytes 2064392 | tf_op jit(solution)/shard_map/ppermute | solution.py:181
  85.9 8.1 %collective-permute-done.13.refs_3_.refs_2_ = bf16[20,112,128]{2,1,0:T(8,128)(2,1)S(1)} collective-permute-done((bf16[20,112,128]{2,1,0:T(8,128)(2,1)S(1)}, bf16[20,112,128]{2,1,0:T(8,128)(2,1)S(1)}, u32[]{:S(2)}, u32[]{:S(2)}) %collective-permute-start.13) | collective-permute-done | bytes 573472 | tf_op jit(solution)/shard_map/ppermute | solution.py:180
  94.0 0.1 pad_maximum_fusion.6
  94.1 0.1 collective-permute-start.14
  94.2 3.3 %collective-permute-start.17 = (bf16[16,112,128]{2,1,0:T(8,128)(2,1)S(1)}, bf16[16,112,128]{2,1,0:T(8,128)(2,1)S(1)}, u32[]{:S(2)}, u32[]{:S(2)}) collective-permute-start(bf16[16,112,128]{2,1,0:T(8,128)(2,1)S(1)} %get-tuple-element.53), channel_id=1, source_target_pairs={{0,3},{1,0},{2,1},{3,2},{4,7},{5,4},{6,5},{7,6},{8,11},{9,8},{10,9... | collective-permute-start | bytes 1376264 | tf_op jit(solution)/shard_map/ppermute | solution.py:181
  97.5 11.2 %collective-permute-done.28.refs_4_.refs_2_ = bf16[24,112,128]{2,1,0:T(8,128)(2,1)S(1)} collective-permute-done((bf16[24,112,128]{2,1,0:T(8,128)(2,1)S(1)}, bf16[24,112,128]{2,1,0:T(8,128)(2,1)S(1)}, u32[]{:S(2)}, u32[]{:S(2)}) %collective-permute-start.28) | collective-permute-done | bytes 688160 | tf_op jit(solution)/shard_map/ppermute | solution.py:180
  108.6 0.1 collective-permute-start.31
  108.8 3.5 %collective-permute-start.32 = (bf16[8,112,128]{2,1,0:T(8,128)(2,1)S(1)}, bf16[8,112,128]{2,1,0:T(8,128)(2,1)S(1)}, u32[]{:S(2)}, u32[]{:S(2)}) collective-permute-start(bf16[8,112,128]{2,1,0:T(8,128)(2,1)S(1)} %slice.182), channel_id=1, source_target_pairs={{0,3},{1,0},{2,1},{3,2},{4,7},{5,4},{6,5},{7,6},{8,11},{9,8},{10,9... | collective-permute-start | bytes 688136 | tf_op jit(solution)/shard_map/ppermute | solution.py:181
  112.3 1.3 collective-permute-done.14.refs_4_.refs_1_
  113.6 0.1 collective-permute-start.18
  113.7 3.3 %collective-permute-start.19 = (bf16[4,112,128]{2,1,0:T(8,128)(2,1)S(1)}, bf16[4,112,128]{2,1,0:T(8,128)(2,1)S(1)}, u32[]{:S(2)}, u32[]{:S(2)}) collective-permute-start(bf16[4,112,128]{2,1,0:T(8,128)(2,1)S(1)} %slice.166), channel_id=1, source_target_pairs={{0,3},{1,0},{2,1},{3,2},{4,7},{5,4},{6,5},{7,6},{8,11},{9,8},{10,9... | collective-permute-start | bytes 344072 | tf_op jit(solution)/shard_map/ppermute | solution.py:181
  117.0 2.8 %place.5.refs_6_ = bf16[7168,512]{1,0:T(8,128)(2,1)} custom-call(s32[64]{0:T(128)S(1)} %copy-done.2, bf16[8,112,128]{2,1,0:T(8,128)(2,1)S(1)} %bitcast.13, bf16[8,112,128]{2,1,0:T(8,128)(2,1)S(1)} %collective-permute-done.12.refs_1_, bf16[8,112,128]{2,1,0:T(8,128)(2,1)S(1)} %collective-permute-done.15.refs_2_, ...), custom_call_target="tpu_custom_call" | custom-call | tf_op jit(solution)/shard_map/place/pallas_call | solution.py:127
  119.8 3.7 %place.6.refs_6_ = bf16[7168,512]{1,0:T(8,128)(2,1)} custom-call(s32[64]{0:T(128)S(1)} %copy-done.2, bf16[8,112,128]{2,1,0:T(8,128)(2,1)S(1)} %collective-permute-done.25.refs_0_, bf16[8,112,128]{2,1,0:T(8,128)(2,1)S(1)} %collective-permute-done.26.refs_1_, ...), custom_call_target="tpu_custom_call", output_to_operand_aliasing={{}: (7, {})} | custom-call | tf_op jit(solution)/shard_map/place/pallas_call | solution.py:127
  123.5 3.7 %place.7.refs_6_ = bf16[7168,512]{1,0:T(8,128)(2,1)} custom-call(s32[64]{0:T(128)S(1)} %copy-done.2, bf16[8,112,128]{2,1,0:T(8,128)(2,1)S(1)} %collective-permute-done.7.refs_0_, bf16[8,112,128]{2,1,0:T(8,128)(2,1)S(1)} %collective-permute-done.8.refs_1_, ...), custom_call_target="tpu_custom_call", output_to_operand_aliasing={{}: (7, {})} | custom-call | tf_op jit(solution)/shard_map/place/pallas_call | solution.py:127
  127.3 3.7 %place.8.refs_5_ = bf16[7168,512]{1,0:T(8,128)(2,1)} custom-call(s32[64]{0:T(128)S(1)} %copy-done.2, bf16[8,112,128]{2,1,0:T(8,128)(2,1)S(1)} %collective-permute-done.20.refs_0_, bf16[8,112,128]{2,1,0:T(8,128)(2,1)S(1)} %collective-permute-done.21.refs_1_, ...), custom_call_target="tpu_custom_call", output_to_operand_aliasing={{}: (7, {})} | custom-call | tf_op jit(solution)/shard_map/place/pallas_call | solution.py:127
  131.1 2.8 %place.9 = bf16[7168,512]{1,0:T(8,128)(2,1)} custom-call(s32[64]{0:T(128)S(1)} %copy-done.2, bf16[8,112,128]{2,1,0:T(8,128)(2,1)S(1)} %collective-permute-done.6.refs_0_, bf16[16,112,128]{2,1,0:T(8,128)(2,1)S(1)} %collective-permute-done.14.refs_4_.refs_1_, ...), custom_call_target="tpu_custom_call", output_to_operand_aliasing={{}: (6, {})} | custom-call | tf_op jit(solution)/shard_map/place/pallas_call | solution.py:127
  (55 shorter events, 0.6 us)
Async XLA Ops:
  0.0 2.8 %collective-permute-start = (bf16[4,112,512]{2,1,0:T(8,128)(2,1)}, bf16[4,112,512]{2,1,0:T(8,128)(2,1)S(1)}, u32[]{:S(2)}, u32[]{:S(2)}) collective-permute-start(bf16[4,112,512]{2,1,0:T(8,128)(2,1)} %gate.1), channel_id=1, source_target_pairs={{0,4},{4,0},{8,12},{12,8},{16,20},{20,16},{24,28},{28,24},{32,36},... | collective-permute-start | bytes 1376264 | tf_op jit(solution)/shard_map/ppermute | solution.py:58
  0.0 2.8 %collective-permute-start.1 = (bf16[4,112,512]{2,1,0:T(8,128)(2,1)}, bf16[4,112,512]{2,1,0:T(8,128)(2,1)S(1)}, u32[]{:S(2)}, u32[]{:S(2)}) collective-permute-start(bf16[4,112,512]{2,1,0:T(8,128)(2,1)} %up.1), channel_id=1, source_target_pairs={{0,4},{4,0},{8,12},{12,8},{16,20},{20,16},{24,28},{28,24},{32,36},... | collective-permute-start | bytes 1376264 | tf_op jit(solution)/shard_map/ppermute | solution.py:59
  0.5 2.2 %collective-permute-start.2 = (f32[112]{0:T(128)}, f32[112]{0:T(128)S(1)}, u32[]{:S(2)}, u32[]{:S(2)}) collective-permute-start(f32[112]{0:T(128)} %param.8), channel_id=1, source_target_pairs={{0,4},{4,0},{8,12},{12,8},{16,20},{20,16},{24,28},{28,24},{32,36},... | collective-permute-start | bytes 1352 | tf_op jit(solution)/shard_map/ppermute | solution.py:60
  2.8 1.0 copy-start
  3.8 1.0 copy-start.1
  4.8 0.7 copy-start.3
  5.5 0.7 copy-start.4
  8.3 33.3 %collective-permute-start.3 = (bf16[5,2,112,128]{3,2,1,0:T(8,128)(2,1)S(1)}, bf16[5,2,112,128]{3,2,1,0:T(8,128)(2,1)S(1)}, u32[]{:S(2)}, u32[]{:S(2)}) collective-permute-start(bf16[5,2,112,128]{3,2,1,0:T(8,128)(2,1)S(1)} %get-tuple-element.18), channel_id=1, source_target_pairs={{0,64},{4,68},{8,72},{12,76},{16,80},{20,84},{24,88},{28,92},{32,9... | collective-permute-start | bytes 860168 | tf_op jit(solution)/shard_map/ppermute | solution.py:162
  9.8 32.0 %collective-permute-start.4 = (bf16[5,2,112,128]{3,2,1,0:T(8,128)(2,1)S(1)}, bf16[5,2,112,128]{3,2,1,0:T(8,128)(2,1)S(1)}, u32[]{:S(2)}, u32[]{:S(2)}) collective-permute-start(bf16[5,2,112,128]{3,2,1,0:T(8,128)(2,1)S(1)} %get-tuple-element.19), channel_id=1, source_target_pairs={{0,128},{4,132},{8,136},{12,140},{16,144},{20,148},{24,152},{28,15... | collective-permute-start | bytes 860168 | tf_op jit(solution)/shard_map/ppermute | solution.py:162
  11.0 10.9 %collective-permute-start.10 = (bf16[1,2,112,128]{3,2,1,0:T(8,128)(2,1)S(1)}, bf16[1,2,112,128]{3,2,1,0:T(8,128)(2,1)S(1)}, u32[]{:S(2)}, u32[]{:S(2)}) collective-permute-start(bf16[1,2,112,128]{3,2,1,0:T(8,128)(2,1)S(1)} %get-tuple-element.23), channel_id=1, source_target_pairs={{0,128},{4,132},{8,136},{12,140},{16,144},{20,148},{24,152},{28,15... | collective-permute-start | bytes 172040 | tf_op jit(solution)/shard_map/ppermute | solution.py:162
  13.5 14.5 %collective-permute-start.11 = (bf16[1,2,112,128]{3,2,1,0:T(8,128)(2,1)S(1)}, bf16[1,2,112,128]{3,2,1,0:T(8,128)(2,1)S(1)}, u32[]{:S(2)}, u32[]{:S(2)}) collective-permute-start(bf16[1,2,112,128]{3,2,1,0:T(8,128)(2,1)S(1)} %get-tuple-element.24), channel_id=1, source_target_pairs={{0,192},{4,196},{8,200},{12,204},{16,208},{20,212},{24,216},{28,22... | collective-permute-start | bytes 172040 | tf_op jit(solution)/shard_map/ppermute | solution.py:162
  14.0 14.0 %collective-permute-start.9 = (bf16[1,2,112,128]{3,2,1,0:T(8,128)(2,1)S(1)}, bf16[1,2,112,128]{3,2,1,0:T(8,128)(2,1)S(1)}, u32[]{:S(2)}, u32[]{:S(2)}) collective-permute-start(bf16[1,2,112,128]{3,2,1,0:T(8,128)(2,1)S(1)} %get-tuple-element.22), channel_id=1, source_target_pairs={{0,64},{4,68},{8,72},{12,76},{16,80},{20,84},{24,88},{28,92},{32,9... | collective-permute-start | bytes 172040 | tf_op jit(solution)/shard_map/ppermute | solution.py:162
  21.9 22.1 %collective-permute-start.5 = (bf16[5,2,112,128]{3,2,1,0:T(8,128)(2,1)S(1)}, bf16[5,2,112,128]{3,2,1,0:T(8,128)(2,1)S(1)}, u32[]{:S(2)}, u32[]{:S(2)}) collective-permute-start(bf16[5,2,112,128]{3,2,1,0:T(8,128)(2,1)S(1)} %get-tuple-element.20), channel_id=1, source_target_pairs={{0,192},{4,196},{8,200},{12,204},{16,208},{20,212},{24,216},{28,22... | collective-permute-start | bytes 860168 | tf_op jit(solution)/shard_map/ppermute | solution.py:162
  28.0 4.8 %collective-permute-start.22 = (bf16[2,2,112,128]{3,2,1,0:T(8,128)(2,1)S(1)}, bf16[2,2,112,128]{3,2,1,0:T(8,128)(2,1)S(1)}, u32[]{:S(2)}, u32[]{:S(2)}) collective-permute-start(bf16[2,2,112,128]{3,2,1,0:T(8,128)(2,1)S(1)} %get-tuple-element.26), channel_id=1, source_target_pairs={{0,64},{4,68},{8,72},{12,76},{16,80},{20,84},{24,88},{28,92},{32,9... | collective-permute-start | bytes 344072 | tf_op jit(solution)/shard_map/ppermute | solution.py:162
  28.0 9.4 %collective-permute-start.23 = (bf16[2,2,112,128]{3,2,1,0:T(8,128)(2,1)S(1)}, bf16[2,2,112,128]{3,2,1,0:T(8,128)(2,1)S(1)}, u32[]{:S(2)}, u32[]{:S(2)}) collective-permute-start(bf16[2,2,112,128]{3,2,1,0:T(8,128)(2,1)S(1)} %get-tuple-element.27), channel_id=1, source_target_pairs={{0,128},{4,132},{8,136},{12,140},{16,144},{20,148},{24,152},{28,15... | collective-permute-start | bytes 344072 | tf_op jit(solution)/shard_map/ppermute | solution.py:162
  32.7 6.2 %collective-permute-start.24 = (bf16[2,2,112,128]{3,2,1,0:T(8,128)(2,1)S(1)}, bf16[2,2,112,128]{3,2,1,0:T(8,128)(2,1)S(1)}, u32[]{:S(2)}, u32[]{:S(2)}) collective-permute-start(bf16[2,2,112,128]{3,2,1,0:T(8,128)(2,1)S(1)} %get-tuple-element.28), channel_id=1, source_target_pairs={{0,192},{4,196},{8,200},{12,204},{16,208},{20,212},{24,216},{28,22... | collective-permute-start | bytes 344072 | tf_op jit(solution)/shard_map/ppermute | solution.py:162
  37.3 22.8 %collective-permute-start.12 = (bf16[8,112,128]{2,1,0:T(8,128)(2,1)S(1)}, bf16[8,112,128]{2,1,0:T(8,128)(2,1)S(1)}, u32[]{:S(2)}, u32[]{:S(2)}) collective-permute-start(bf16[8,112,128]{2,1,0:T(8,128)(2,1)S(1)} %bitcast.11), channel_id=1, source_target_pairs={{0,1},{1,2},{2,3},{3,0},{4,5},{5,6},{6,7},{7,4},{8,9},{9,10},{10,1... | collective-permute-start | bytes 688136 | tf_op jit(solution)/shard_map/ppermute | solution.py:180
  39.0 21.3 %collective-permute-start.15 = (bf16[8,112,128]{2,1,0:T(8,128)(2,1)S(1)}, bf16[8,112,128]{2,1,0:T(8,128)(2,1)S(1)}, u32[]{:S(2)}, u32[]{:S(2)}) collective-permute-start(bf16[8,112,128]{2,1,0:T(8,128)(2,1)S(1)} %bitcast.12), channel_id=1, source_target_pairs={{0,3},{1,0},{2,1},{3,2},{4,7},{5,4},{6,5},{7,6},{8,11},{9,8},{10,9... | collective-permute-start | bytes 688136 | tf_op jit(solution)/shard_map/ppermute | solution.py:181
  41.6 11.3 %collective-permute-start.26 = (bf16[8,112,128]{2,1,0:T(8,128)(2,1)S(1)}, bf16[8,112,128]{2,1,0:T(8,128)(2,1)S(1)}, u32[]{:S(2)}, u32[]{:S(2)}) collective-permute-start(bf16[8,112,128]{2,1,0:T(8,128)(2,1)S(1)} %bitcast.15), channel_id=1, source_target_pairs={{0,56},{4,60},{8,0},{12,4},{16,8},{20,12},{24,16},{28,20},{32,24},... | collective-permute-start | bytes 688136 | tf_op jit(solution)/shard_map/ppermute | solution.py:165
  41.8 11.1 %collective-permute-start.25 = (bf16[8,112,128]{2,1,0:T(8,128)(2,1)S(1)}, bf16[8,112,128]{2,1,0:T(8,128)(2,1)S(1)}, u32[]{:S(2)}, u32[]{:S(2)}) collective-permute-start(bf16[8,112,128]{2,1,0:T(8,128)(2,1)S(1)} %bitcast.18), channel_id=1, source_target_pairs={{0,8},{4,12},{8,16},{12,20},{16,24},{20,28},{24,32},{28,36},{32,40... | collective-permute-start | bytes 688136 | tf_op jit(solution)/shard_map/ppermute | solution.py:165
  44.1 19.5 %collective-permute-start.7 = (bf16[8,112,128]{2,1,0:T(8,128)(2,1)S(1)}, bf16[8,112,128]{2,1,0:T(8,128)(2,1)S(1)}, u32[]{:S(2)}, u32[]{:S(2)}) collective-permute-start(bf16[8,112,128]{2,1,0:T(8,128)(2,1)S(1)} %bitcast.16), channel_id=1, source_target_pairs={{0,16},{4,20},{8,24},{12,28},{16,32},{20,36},{24,40},{28,44},{32,4... | collective-permute-start | bytes 688136 | tf_op jit(solution)/shard_map/ppermute | solution.py:165
  52.9 23.9 %collective-permute-start.27 = (bf16[16,112,128]{2,1,0:T(8,128)(2,1)S(1)}, bf16[16,112,128]{2,1,0:T(8,128)(2,1)S(1)}, u32[]{:S(2)}, u32[]{:S(2)}) collective-permute-start(bf16[16,112,128]{2,1,0:T(8,128)(2,1)S(1)} %constant_dynamic-update-slice_fusion), channel_id=1, source_target_pairs={{0,1},{1,2},{2,3},{3,0},{4,5},{5,6},{6,7},{7,4},{8,9},{9,10},{10,1... | collective-permute-start | bytes 1376264 | tf_op jit(solution)/shard_map/ppermute | solution.py:180
  53.1 23.6 %collective-permute-start.8 = (bf16[8,112,128]{2,1,0:T(8,128)(2,1)S(1)}, bf16[8,112,128]{2,1,0:T(8,128)(2,1)S(1)}, u32[]{:S(2)}, u32[]{:S(2)}) collective-permute-start(bf16[8,112,128]{2,1,0:T(8,128)(2,1)S(1)} %bitcast.20), channel_id=1, source_target_pairs={{0,48},{4,52},{8,56},{12,60},{16,0},{20,4},{24,8},{28,12},{32,16},... | collective-permute-start | bytes 688136 | tf_op jit(solution)/shard_map/ppermute | solution.py:165
  60.1 21.9 %collective-permute-start.21 = (bf16[8,112,128]{2,1,0:T(8,128)(2,1)S(1)}, bf16[8,112,128]{2,1,0:T(8,128)(2,1)S(1)}, u32[]{:S(2)}, u32[]{:S(2)}) collective-permute-start(bf16[8,112,128]{2,1,0:T(8,128)(2,1)S(1)} %bitcast.14), channel_id=1, source_target_pairs={{0,40},{4,44},{8,48},{12,52},{16,56},{20,60},{24,0},{28,4},{32,8},... | collective-permute-start | bytes 688136 | tf_op jit(solution)/shard_map/ppermute | solution.py:165
  60.2 19.9 %collective-permute-start.29 = (bf16[16,112,128]{2,1,0:T(8,128)(2,1)S(1)}, bf16[16,112,128]{2,1,0:T(8,128)(2,1)S(1)}, u32[]{:S(2)}, u32[]{:S(2)}) collective-permute-start(bf16[16,112,128]{2,1,0:T(8,128)(2,1)S(1)} %constant_dynamic-update-slice_fusion), channel_id=1, source_target_pairs={{0,3},{1,0},{2,1},{3,2},{4,7},{5,4},{6,5},{7,6},{8,11},{9,8},{10,9... | collective-permute-start | bytes 1376264 | tf_op jit(solution)/shard_map/ppermute | solution.py:181
  63.6 18.5 %collective-permute-start.20 = (bf16[8,112,128]{2,1,0:T(8,128)(2,1)S(1)}, bf16[8,112,128]{2,1,0:T(8,128)(2,1)S(1)}, u32[]{:S(2)}, u32[]{:S(2)}) collective-permute-start(bf16[8,112,128]{2,1,0:T(8,128)(2,1)S(1)} %bitcast.17), channel_id=1, source_target_pairs={{0,24},{4,28},{8,32},{12,36},{16,40},{20,44},{24,48},{28,52},{32,5... | collective-permute-start | bytes 688136 | tf_op jit(solution)/shard_map/ppermute | solution.py:165
  76.7 17.2 %collective-permute-start.13 = (bf16[20,112,128]{2,1,0:T(8,128)(2,1)S(1)}, bf16[20,112,128]{2,1,0:T(8,128)(2,1)S(1)}, u32[]{:S(2)}, u32[]{:S(2)}) collective-permute-start(bf16[20,112,128]{2,1,0:T(8,128)(2,1)S(1)} %get-tuple-element.32), channel_id=1, source_target_pairs={{0,1},{1,2},{2,3},{3,0},{4,5},{5,6},{6,7},{7,4},{8,9},{9,10},{10,1... | collective-permute-start | bytes 1720328 | tf_op jit(solution)/shard_map/ppermute | solution.py:180
  76.8 17.1 %collective-permute-start.16 = (bf16[20,112,128]{2,1,0:T(8,128)(2,1)S(1)}, bf16[20,112,128]{2,1,0:T(8,128)(2,1)S(1)}, u32[]{:S(2)}, u32[]{:S(2)}) collective-permute-start(bf16[20,112,128]{2,1,0:T(8,128)(2,1)S(1)} %get-tuple-element.31), channel_id=1, source_target_pairs={{0,3},{1,0},{2,1},{3,2},{4,7},{5,4},{6,5},{7,6},{8,11},{9,8},{10,9... | collective-permute-start | bytes 1720328 | tf_op jit(solution)/shard_map/ppermute | solution.py:181
  80.1 13.9 %collective-permute-start.6 = (bf16[8,112,128]{2,1,0:T(8,128)(2,1)S(1)}, bf16[8,112,128]{2,1,0:T(8,128)(2,1)S(1)}, u32[]{:S(2)}, u32[]{:S(2)}) collective-permute-start(bf16[8,112,128]{2,1,0:T(8,128)(2,1)S(1)} %bitcast.19), channel_id=1, source_target_pairs={{0,32},{4,36},{8,40},{12,44},{16,48},{20,52},{24,56},{28,60},{32,0... | collective-permute-start | bytes 688136 | tf_op jit(solution)/shard_map/ppermute | solution.py:165
  82.2 34.8 %copy-start.2 = (s32[64]{0:T(128)S(1)}, s32[64]{0:T(128)}, u32[]{:S(2)}) copy-start(s32[64]{0:T(128)} %matching.9) | copy-start | bytes 772
  82.2 26.4 %collective-permute-start.28 = (bf16[24,112,128]{2,1,0:T(8,128)(2,1)S(1)}, bf16[24,112,128]{2,1,0:T(8,128)(2,1)S(1)}, u32[]{:S(2)}, u32[]{:S(2)}) collective-permute-start(bf16[24,112,128]{2,1,0:T(8,128)(2,1)S(1)} %get-tuple-element.30), channel_id=1, source_target_pairs={{0,1},{1,2},{2,3},{3,0},{4,5},{5,6},{6,7},{7,4},{8,9},{9,10},{10,1... | collective-permute-start | bytes 2064392 | tf_op jit(solution)/shard_map/ppermute | solution.py:180
  82.6 26.1 %collective-permute-start.30 = (bf16[24,112,128]{2,1,0:T(8,128)(2,1)S(1)}, bf16[24,112,128]{2,1,0:T(8,128)(2,1)S(1)}, u32[]{:S(2)}, u32[]{:S(2)}) collective-permute-start(bf16[24,112,128]{2,1,0:T(8,128)(2,1)S(1)} %get-tuple-element.29), channel_id=1, source_target_pairs={{0,3},{1,0},{2,1},{3,2},{4,7},{5,4},{6,5},{7,6},{8,11},{9,8},{10,9... | collective-permute-start | bytes 2064392 | tf_op jit(solution)/shard_map/ppermute | solution.py:181
  94.1 19.5 %collective-permute-start.14 = (bf16[16,112,128]{2,1,0:T(8,128)(2,1)S(1)}, bf16[16,112,128]{2,1,0:T(8,128)(2,1)S(1)}, u32[]{:S(2)}, u32[]{:S(2)}) collective-permute-start(bf16[16,112,128]{2,1,0:T(8,128)(2,1)S(1)} %get-tuple-element.54), channel_id=1, source_target_pairs={{0,1},{1,2},{2,3},{3,0},{4,5},{5,6},{6,7},{7,4},{8,9},{9,10},{10,1... | collective-permute-start | bytes 1376264 | tf_op jit(solution)/shard_map/ppermute | solution.py:180
  94.2 19.5 %collective-permute-start.17 = (bf16[16,112,128]{2,1,0:T(8,128)(2,1)S(1)}, bf16[16,112,128]{2,1,0:T(8,128)(2,1)S(1)}, u32[]{:S(2)}, u32[]{:S(2)}) collective-permute-start(bf16[16,112,128]{2,1,0:T(8,128)(2,1)S(1)} %get-tuple-element.53), channel_id=1, source_target_pairs={{0,3},{1,0},{2,1},{3,2},{4,7},{5,4},{6,5},{7,6},{8,11},{9,8},{10,9... | collective-permute-start | bytes 1376264 | tf_op jit(solution)/shard_map/ppermute | solution.py:181
  108.6 18.6 %collective-permute-start.31 = (bf16[8,112,128]{2,1,0:T(8,128)(2,1)S(1)}, bf16[8,112,128]{2,1,0:T(8,128)(2,1)S(1)}, u32[]{:S(2)}, u32[]{:S(2)}) collective-permute-start(bf16[8,112,128]{2,1,0:T(8,128)(2,1)S(1)} %slice.181), channel_id=1, source_target_pairs={{0,1},{1,2},{2,3},{3,0},{4,5},{5,6},{6,7},{7,4},{8,9},{9,10},{10,1... | collective-permute-start | bytes 688136 | tf_op jit(solution)/shard_map/ppermute | solution.py:180
  108.8 18.5 %collective-permute-start.32 = (bf16[8,112,128]{2,1,0:T(8,128)(2,1)S(1)}, bf16[8,112,128]{2,1,0:T(8,128)(2,1)S(1)}, u32[]{:S(2)}, u32[]{:S(2)}) collective-permute-start(bf16[8,112,128]{2,1,0:T(8,128)(2,1)S(1)} %slice.182), channel_id=1, source_target_pairs={{0,3},{1,0},{2,1},{3,2},{4,7},{5,4},{6,5},{7,6},{8,11},{9,8},{10,9... | collective-permute-start | bytes 688136 | tf_op jit(solution)/shard_map/ppermute | solution.py:181
  113.6 17.5 %collective-permute-start.18 = (bf16[4,112,128]{2,1,0:T(8,128)(2,1)S(1)}, bf16[4,112,128]{2,1,0:T(8,128)(2,1)S(1)}, u32[]{:S(2)}, u32[]{:S(2)}) collective-permute-start(bf16[4,112,128]{2,1,0:T(8,128)(2,1)S(1)} %slice.165), channel_id=1, source_target_pairs={{0,1},{1,2},{2,3},{3,0},{4,5},{5,6},{6,7},{7,4},{8,9},{9,10},{10,1... | collective-permute-start | bytes 344072 | tf_op jit(solution)/shard_map/ppermute | solution.py:180
  113.7 17.4 %collective-permute-start.19 = (bf16[4,112,128]{2,1,0:T(8,128)(2,1)S(1)}, bf16[4,112,128]{2,1,0:T(8,128)(2,1)S(1)}, u32[]{:S(2)}, u32[]{:S(2)}) collective-permute-start(bf16[4,112,128]{2,1,0:T(8,128)(2,1)S(1)} %slice.166), channel_id=1, source_target_pairs={{0,3},{1,0},{2,1},{3,2},{4,7},{5,4},{6,5},{7,6},{8,11},{9,8},{10,9... | collective-permute-start | bytes 344072 | tf_op jit(solution)/shard_map/ppermute | solution.py:181

commit v2 on v1

v2 whole, which is shorter than its diff:
```python
import functools

import jax
import jax.numpy as jnp
from jax import lax
from jax.experimental import pallas as pl
from jax.experimental.pallas import tpu as pltpu
from jax.sharding import PartitionSpec as P

NX, NZ, NY = 4, 8, 4
SLOTS, BLOCKS = 8, 8
GROUPS = ((1, 7), (3, 5))
BF16 = jnp.bfloat16


def place():
    me = lax.axis_index("fsdp")
    return me // (2 * NZ), (me // 2) % NZ, me % 2


def after(arrays, *done):
    return lax.optimization_barrier((list(arrays), done))[0]


def pick_matrix(core):
    unit = lax.broadcasted_iota(jnp.int32, (1024, 512), 0)
    column = lax.broadcasted_iota(jnp.int32, (1024, 512), 1)
    lane = column % 128
    wanted = (lane % 2) * 512 + 8 * (lane // 2) + 2 * (column // 128) + core
    return (unit == wanted).astype(BF16)


def prepare_kernel(tables, *refs):
    sources, (gain, gain_far, matrix), outs = refs[:4], refs[4:7], refs[7:-2]
    picked, owner = refs[-2:]
    experts, rows = sources[0].shape[:2]
    x, z, _ = place()
    for e in range(experts):
        for k in range(4):
            @pl.when(k < tables[16 + e])
            def _():
                owner[tables[4 * e + k]] = e
    for side, scale in enumerate((gain, gain_far)):
        for e in range(experts):
            got = jnp.dot(sources[2 * side][e], matrix[:512, :], preferred_element_type=jnp.float32)
            got += jnp.dot(sources[2 * side + 1][e], matrix[512:, :], preferred_element_type=jnp.float32)
            got = (got * scale[...]).astype(BF16)
            for zl in range(4):
                picked[e * 4 + zl, side] = got[:, zl * 128 : (zl + 1) * 128]
    for g, group in enumerate(GROUPS):
        for k, dz in enumerate(group):
            zt = (z + dz) % NZ
            for dx in range(NX):
                xt = (x + dx) % NX
                source = owner[xt * 2 + zt // 4] * 4 + zt % 4
                outs[g * NX + dx][k] = picked[source]
    for xt in range(NX):
        for k in range(NZ // 2):
            zt = 2 * k + z % 2
            outs[-1][xt * (NZ // 2) + k] = picked[owner[xt * 2 + zt // 4] * 4 + zt % 4]


def prepare(gate, up, gain, matrix, tables):
    rows = gate.shape[1]
    flip = [(i, i ^ 1) for i in range(2 * NX * NZ)]
    gate_far = lax.ppermute(gate, "fsdp", flip)
    up_far = lax.ppermute(up, "fsdp", flip)
    gain_far = lax.ppermute(gain, "fsdp", flip)
    shapes = [
        jax.ShapeDtypeStruct((len(group), 2, rows, 128), BF16) for group in GROUPS for _ in range(NX)
    ] + [jax.ShapeDtypeStruct((NX * NZ // 2, 2, rows, 128), BF16)]
    vmem = pl.BlockSpec(memory_space=pltpu.VMEM)
    smem = pl.BlockSpec(memory_space=pltpu.SMEM)
    outs = pl.pallas_call(
        prepare_kernel,
        out_shape=shapes,
        in_specs=[smem] + [vmem] * 7,
        out_specs=[vmem] * len(shapes),
        scratch_shapes=[
            pltpu.VMEM((16, 2, rows, 128), BF16),
            pltpu.SMEM((SLOTS,), jnp.int32),
        ],
        compiler_params=pltpu.CompilerParams(vmem_limit_bytes=16 * 1024 * 1024),
        name="prepare",
    )(
        tables, gate, up, gate_far, up_far,
        gain.reshape(rows, 1), gain_far.reshape(rows, 1), matrix,
    )
    return [outs[g * NX : (g + 1) * NX] for g in range(len(GROUPS))], outs[-1]


def place_kernel(blocks, sizes, relative, tables, *refs):
    held = refs[-len(sizes) - 3 : -3]
    built, load_sems, save_sems = refs[-3:]
    out, rows = refs[-len(sizes) - 4], built.shape[1]
    x, z, core = place()
    y = lax.axis_index("rep")
    loads = [
        pltpu.make_async_copy(refs[k].at[pl.ds(at, size)], held[k], load_sems.at[k])
        for k, (at, size) in enumerate(sizes)
    ]
    for load in loads:
        load.start()
    for load in loads:
        load.wait()
    saves = []
    for at, (dz, dx, side, parts) in enumerate(blocks):
        for step, (k, index) in enumerate(parts):
            group = (y + step) % NY if relative else step
            built[at, :, pl.ds(pl.multiple_of(group * 128, 128), 128)] = held[k][index]
        xs, zs = ((x - dx) % NX, (z - dz) % NZ) if dz is not None else (dx // 4, 2 * (dx % 4) + z % 2)
        block = tables[20 + (xs * NZ + zs) * 2 + (core ^ side)]
        row = pl.multiple_of(block * rows, 16)
        save = pltpu.make_async_copy(built.at[at], out.at[pl.ds(row, rows)], save_sems.at[at])
        save.start()
        saves.append(save)
    for save in saves:
        save.wait()


def place_blocks(out, tables, devices, arrays, blocks, relative=True):
    rows = arrays[0][0].shape[1]
    anywhere = pl.BlockSpec(memory_space=pl.ANY)
    sizes = [(at, size) for _, at, size in arrays]
    args = [tables] + [array for array, _, _ in arrays] + ([] if out is None else [out])
    total = len(blocks) * rows * 512 * 2
    return pl.pallas_call(
        functools.partial(place_kernel, blocks, sizes, relative),
        out_shape=jax.ShapeDtypeStruct((devices * rows, 512), BF16),
        in_specs=[pl.BlockSpec(memory_space=pltpu.SMEM)] + [anywhere] * (len(args) - 1),
        out_specs=anywhere,
        scratch_shapes=[pltpu.VMEM((size, rows, 128), BF16) for _, size in sizes]
        + [
            pltpu.VMEM((len(blocks), rows, 512), BF16),
            pltpu.SemaphoreType.DMA((len(sizes),)),
            pltpu.SemaphoreType.DMA((len(blocks),)),
        ],
        input_output_aliases={} if out is None else {len(args) - 1: 0},
        compiler_params=pltpu.CompilerParams(vmem_limit_bytes=16 * 1024 * 1024),
        cost_estimate=pl.CostEstimate(flops=0, bytes_accessed=2 * total, transcendentals=0),
        name="place",
    )(*args)


def local(gate, up, norm_gain, matching, replica_slots, replica_count):
    devices = lax.axis_size("fsdp")
    rows = gate.shape[1]
    _, _, core = place()
    matrix = pick_matrix(core)
    tables = jnp.concatenate([replica_slots.reshape(16), replica_count, matching])
    parts, even = prepare(gate, up, norm_gain, matrix, tables)

    def along_x(dx):
        return [(i, ((i // 16 + dx) % NX) * 16 + i % 16) for i in range(devices)]

    def along_z(dz):
        return [(i, (i // 16) * 16 + ((i // 2 + dz) % NZ) * 2 + i % 2) for i in range(devices)]

    def along_y(dy):
        return [(i, (i + dy) % NY) for i in range(NY)]

    same_parity = [
        [(x * NZ + 2 * k + odd) * 2 + c for x in range(NX) for k in range(NZ // 2)]
        for odd in range(2) for c in range(2)
    ]

    def cross_x(g, *done):
        pieces = after(parts[g], *done)
        got = [pieces[0]] + [lax.ppermute(pieces[dx], "fsdp", along_x(dx)) for dx in range(1, NX)]
        return [jnp.stack([a[k] for a in got]).reshape(8, rows, 128) for k in range(len(GROUPS[g]))]

    def cross_z(dzs, pieces, *done):
        pieces = after(pieces, *done)
        return [lax.ppermute(p, "fsdp", along_z(dz)) for dz, p in zip(dzs, pieces)]

    def cross_y(to_right, to_left, *done):
        pair = after([jnp.concatenate(to_right), jnp.concatenate(to_left)], *done)
        return lax.ppermute(pair[0], "rep", along_y(1)), lax.ppermute(pair[1], "rep", along_y(-1))

    def ring_blocks(dzs):
        n, count = len(dzs), 8 * len(dzs)
        blocks = []
        for at in range(count):
            dz, dx, side = dzs[at // 8], at % 8 // 2, at % 2
            far = (n + 2, at) if at < count // 2 else (n + 3, at - count // 2)
            blocks.append((dz, dx, side, ((at // 8, at % 8), (n + 1, at), far, (n, at))))
        return blocks

    def finish(out, dzs, own, left, right, far_left, far_right, base):
        count = 8 * len(dzs)
        arrays = [(a, 0, 8) for a in own]
        arrays += [(left, 0, count), (right, 0, count)]
        arrays += [(far_left, base, count // 2), (far_right, base, count // 2)]
        return place_blocks(out, tables, devices, arrays, ring_blocks(dzs))

    own1 = cross_z((1, 7), [jnp.concatenate([piece[k] for piece in parts[0]]) for k in range(2)])
    own = lax.all_to_all(even, "fsdp", 0, 0, tiled=True, axis_index_groups=same_parity)
    own = own.reshape(32, rows, 128)
    l1, r1 = cross_y(own1, own1)
    h1 = cross_y([l1[:8]], [r1[8:16]])
    le, re = cross_y([own], [own], *h1)
    bundles = []
    for dx in range(NX):
        here = [slice(8 * k + 2 * dx, 8 * k + 2 * dx + 2) for k in range(2)]
        bundle = [own1[k][here[0]] for k in range(2)] + [r1[h] for h in here]
        bundle += [h1[0][here[0]], h1[1][here[0]]] + [l1[h] for h in here]
        bundle = jnp.concatenate(bundle)
        bundles.append(lax.ppermute(bundle, "fsdp", along_x(dx)) if dx else bundle)
    own3 = cross_z((3, 5), cross_x(1, *own1))
    l3, r3 = cross_y(own3 + [le[:16]], own3 + [re[16:]])
    late = [
        (dz, dx, side, tuple((dx, step * 4 + 2 * k + side) for step in range(NY)))
        for dx in range(NX) for k, dz in enumerate(GROUPS[0]) for side in range(2)
    ]
    out = place_blocks(None, tables, devices, [(b, 0, 16) for b in bundles], late)
    l4, r4 = cross_y([l3[:8]], [r3[8:16]])
    evens = [
        (None, at // 2, at % 2, ((0, at), (2, at), (3, at) if at < 16 else (4, at - 16), (1, at)))
        for at in range(32)
    ]
    arrays = [(own, 0, 32), (le, 0, 32), (re, 0, 32), (l3, 16, 16), (r3, 16, 16)]
    out = place_blocks(out, tables, devices, arrays, evens)
    out = finish(out, (3, 5), own3, l3, r3, l4, r4, 0)
    return out[None]


def solution(mesh):
    return jax.shard_map(
        local,
        mesh=mesh,
        in_specs=(P(None, "fsdp", "rep"), P(None, "fsdp", "rep"), P("fsdp"), P(), P(), P()),
        out_specs=P("fsdp", None, None),
        check_vma=False,
    )
```

time: 134 us -> 109 us (0.81)
  the two profiles are of different devices: /device:TPU:66 before, /device:TPU:64 now
where the time goes in v2:
time: 109 us; the launch traced here: 108 us
  starting transfers between devices  45 us (41%)
  waiting for transfers between devices  40.3 us (37%)
  Pallas kernels  13.7 us (13%)
  local copies, waits for them, and re-layouts  7.37 us (7%)
  other arithmetic  1.45 us (1%)
    ppermute x5, waiting for transfers between devices, cross_y(): lax.ppermute(pair[0], 'rep', along_y(1))  37.9 us
    ppermute x5, starting transfers between devices, cross_y(): lax.ppermute(pair[1], 'rep', along_y(-1))  12.1 us
    all_to_all x1, starting transfers between devices, local(): lax.all_to_all(even, 'fsdp', 0, 0, tiled=True, axis_index_groups=same_par...  11.8 us
    pallas_call x3, Pallas kernels, place_blocks(): pl.pallas_call(functools.partial(place_kernel, blocks, sizes, relative),...  10.8 us
    ppermute x4, starting transfers between devices, cross_z(): return [lax.ppermute(p, 'fsdp', along_z(dz)) for dz, p in zip(dzs, pieces)]  7.21 us
    ppermute x3, starting transfers between devices, cross_x(): lax.ppermute(pieces[dx], 'fsdp', along_x(dx))  5.6 us
    unnamed x17, local copies, waits for them, and re-layouts  5.5 us
    ppermute x5, starting transfers between devices, cross_y(): lax.ppermute(pair[0], 'rep', along_y(1))  4.16 us
  transfers between devices with their start and end apart: 24, of which 7 were waited for; matrix products, arithmetic and copies ran while one was open for 6% of the time, Pallas kernels for 6%

profile of v2, /device:TPU:64, one launch (start us, length us, event | category | flops | bytes accessed | tf_op | source)
XLA Modules:
  0.0 108.3 jit_solution(3397061581766801792)
XLA Ops:
  0.0 0.0 collective-permute-start
  0.0 0.5 collective-permute-start.1
  0.5 0.0 collective-permute-start.2
  0.5 0.8 reshape.18
  1.3 0.4 fusion.10.refs_6_
  1.7 0.8 pad_add_fusion.tables
  2.4 0.8 copy.9.refs_4_
  3.2 0.0 collective-permute-done.2
  3.2 0.1 copy.10.refs_5_
  3.3 0.0 collective-permute-done.refs_2_
  3.3 0.0 collective-permute-done.1.refs_3_
  3.3 0.0 copy-start
  3.3 1.0 copy-done
  4.3 1.0 copy-done.1
  5.4 3.0 %prepare.1 = (bf16[2,2,112,128]{3,2,1,0:T(8,128)(2,1)S(1)}, bf16[2,2,112,128]{3,2,1,0:T(8,128)(2,1)S(1)}, bf16[2,2,112,128]{3,2,1,0:T(8,128)(2,1)S(1)}, bf16[2,2...) custom-call(s32[84]{0:T(128)S(1)} %pad_add_fusion.tables, ...), custom_call_target="tpu_custom_call" | custom-call | tf_op jit(solution)/shard_map/prepare/pallas_call | solution.py:74
  8.5 2.0 %collective-permute-start.3 = (bf16[8,112,128]{2,1,0:T(8,128)(2,1)S(1)}, bf16[8,112,128]{2,1,0:T(8,128)(2,1)S(1)}, u32[]{:S(2)}, u32[]{:S(2)}) collective-permute-start(bf16[8,112,128]{2,1,0:T(8,128)(2,1)S(1)} %pad_maximum_fusion.4), channel_id=1, source_target_pairs={{0,8},{4,12},{8,16},{12,20},{16,24},{20,28},{24,32},{28,36},{32,40... | collective-permute-start | bytes 688136 | tf_op jit(solution)/shard_map/ppermute | solution.py:174
  10.5 0.1 collective-permute-start.4
  10.6 11.8 %all-to-all-start = ((bf16[16,2,112,128]{3,2,1,0:T(8,128)(2,1)}), bf16[16,2,112,128]{3,2,1,0:T(8,128)(2,1)S(1)}, u32[]{:S(2)}, u32[]{:S(2)}) async-start(bf16[16,2,112,128]{3,2,1,0:T(8,128)(2,1)} %get-tuple-element.48), calls=%async_computation | async-start | bytes 1835008 | tf_op jit(solution)/shard_map/all_to_all | solution.py:197
  22.4 0.0 collective-permute-done.3
  22.4 0.0 collective-permute-done.4
  22.5 3.1 %collective-permute-start.11 = (bf16[16,112,128]{2,1,0:T(8,128)(2,1)S(1)}, bf16[16,112,128]{2,1,0:T(8,128)(2,1)S(1)}, u32[]{:S(2)}, u32[]{:S(2)}) collective-permute-start(bf16[16,112,128]{2,1,0:T(8,128)(2,1)S(1)} %pad_maximum_fusion.3), channel_id=1, source_target_pairs={{0,3},{1,0},{2,1},{3,2},{4,7},{5,4},{6,5},{7,6},{8,11},{9,8},{10,9... | collective-permute-start | bytes 1376264 | tf_op jit(solution)/shard_map/ppermute | solution.py:178
  25.6 0.0 collective-permute-start.10
  25.6 1.5 %collective-permute-start.5 = (bf16[2,2,112,128]{3,2,1,0:T(8,128)(2,1)S(1)}, bf16[2,2,112,128]{3,2,1,0:T(8,128)(2,1)S(1)}, u32[]{:S(2)}, u32[]{:S(2)}) collective-permute-start(bf16[2,2,112,128]{3,2,1,0:T(8,128)(2,1)S(1)} %get-tuple-element.43), channel_id=1, source_target_pairs={{0,64},{4,68},{8,72},{12,76},{16,80},{20,84},{24,88},{28,92},{32,9... | collective-permute-start | bytes 344072 | tf_op jit(solution)/shard_map/ppermute | solution.py:169
  27.0 2.7 %collective-permute-start.6 = (bf16[2,2,112,128]{3,2,1,0:T(8,128)(2,1)S(1)}, bf16[2,2,112,128]{3,2,1,0:T(8,128)(2,1)S(1)}, u32[]{:S(2)}, u32[]{:S(2)}) collective-permute-start(bf16[2,2,112,128]{3,2,1,0:T(8,128)(2,1)S(1)} %get-tuple-element.44), channel_id=1, source_target_pairs={{0,128},{4,132},{8,136},{12,140},{16,144},{20,148},{24,152},{28,15... | collective-permute-start | bytes 344072 | tf_op jit(solution)/shard_map/ppermute | solution.py:169
  29.7 1.5 %collective-permute-start.7 = (bf16[2,2,112,128]{3,2,1,0:T(8,128)(2,1)S(1)}, bf16[2,2,112,128]{3,2,1,0:T(8,128)(2,1)S(1)}, u32[]{:S(2)}, u32[]{:S(2)}) collective-permute-start(bf16[2,2,112,128]{3,2,1,0:T(8,128)(2,1)S(1)} %get-tuple-element.45), channel_id=1, source_target_pairs={{0,192},{4,196},{8,200},{12,204},{16,208},{20,212},{24,216},{28,22... | collective-permute-start | bytes 344072 | tf_op jit(solution)/shard_map/ppermute | solution.py:169
  31.2 0.7 constant_dynamic-update-slice_fusion.31
  31.9 0.7 constant_dynamic-update-slice_fusion.30
  32.5 0.3 collective-permute-done.5
  32.9 5.4 %collective-permute-done.10 = bf16[16,112,128]{2,1,0:T(8,128)(2,1)S(1)} collective-permute-done((bf16[16,112,128]{2,1,0:T(8,128)(2,1)S(1)}, bf16[16,112,128]{2,1,0:T(8,128)(2,1)S(1)}, u32[]{:S(2)}, u32[]{:S(2)}) %collective-permute-start.10) | collective-permute-done | bytes 458784 | tf_op jit(solution)/shard_map/ppermute | solution.py:178
  38.3 0.0 collective-permute-done.11
  38.4 0.1 collective-permute-start.12
  38.4 3.2 %collective-permute-start.13 = (bf16[8,112,128]{2,1,0:T(8,128)(2,1)S(1)}, bf16[8,112,128]{2,1,0:T(8,128)(2,1)S(1)}, u32[]{:S(2)}, u32[]{:S(2)}) collective-permute-start(bf16[8,112,128]{2,1,0:T(8,128)(2,1)S(1)} %slice.223), channel_id=1, source_target_pairs={{0,3},{1,0},{2,1},{3,2},{4,7},{5,4},{6,5},{7,6},{8,11},{9,8},{10,9... | collective-permute-start | bytes 688136 | tf_op jit(solution)/shard_map/ppermute | solution.py:178
  41.7 0.0 collective-permute-done.6
  41.7 4.0 %collective-permute-done.12 = bf16[8,112,128]{2,1,0:T(8,128)(2,1)S(1)} collective-permute-done((bf16[8,112,128]{2,1,0:T(8,128)(2,1)S(1)}, bf16[8,112,128]{2,1,0:T(8,128)(2,1)S(1)}, u32[]{:S(2)}, u32[]{:S(2)}) %collective-permute-start.12) | collective-permute-done | bytes 229408 | tf_op jit(solution)/shard_map/ppermute | solution.py:178
  45.7 0.0 collective-permute-done.13
  45.7 1.9 %all-to-all-done = bf16[16,2,112,128]{3,2,1,0:T(8,128)(2,1)S(1)} async-done(((bf16[16,2,112,128]{3,2,1,0:T(8,128)(2,1)}), bf16[16,2,112,128]{3,2,1,0:T(8,128)(2,1)S(1)}, u32[]{:S(2)}, u32[]{:S(2)}) %all-to-all-start) | async-done | bytes 917536 | tf_op jit(solution)/shard_map/all_to_all | solution.py:197
  47.6 1.5 %collective-permute-start.14 = (bf16[32,112,128]{2,1,0:T(8,128)(2,1)S(1)}, bf16[32,112,128]{2,1,0:T(8,128)(2,1)S(1)}, u32[]{:S(2)}, u32[]{:S(2)}) collective-permute-start(bf16[32,112,128]{2,1,0:T(8,128)(2,1)S(1)} %bitcast.22), channel_id=1, source_target_pairs={{0,1},{1,2},{2,3},{3,0},{4,5},{5,6},{6,7},{7,4},{8,9},{9,10},{10,1... | collective-permute-start | bytes 2752520 | tf_op jit(solution)/shard_map/ppermute | solution.py:178
  49.1 1.7 %collective-permute-start.15 = (bf16[32,112,128]{2,1,0:T(8,128)(2,1)S(1)}, bf16[32,112,128]{2,1,0:T(8,128)(2,1)S(1)}, u32[]{:S(2)}, u32[]{:S(2)}) collective-permute-start(bf16[32,112,128]{2,1,0:T(8,128)(2,1)S(1)} %bitcast.23), channel_id=1, source_target_pairs={{0,3},{1,0},{2,1},{3,2},{4,7},{5,4},{6,5},{7,6},{8,11},{9,8},{10,9... | collective-permute-start | bytes 2752520 | tf_op jit(solution)/shard_map/ppermute | solution.py:178
  50.9 2.1 %collective-permute-start.8 = (bf16[8,112,128]{2,1,0:T(8,128)(2,1)S(1)}, bf16[8,112,128]{2,1,0:T(8,128)(2,1)S(1)}, u32[]{:S(2)}, u32[]{:S(2)}) collective-permute-start(bf16[8,112,128]{2,1,0:T(8,128)(2,1)S(1)} %bitcast.26), channel_id=1, source_target_pairs={{0,24},{4,28},{8,32},{12,36},{16,40},{20,44},{24,48},{28,52},{32,5... | collective-permute-start | bytes 688136 | tf_op jit(solution)/shard_map/ppermute | solution.py:174
  53.0 3.0 %collective-permute-start.9 = (bf16[8,112,128]{2,1,0:T(8,128)(2,1)S(1)}, bf16[8,112,128]{2,1,0:T(8,128)(2,1)S(1)}, u32[]{:S(2)}, u32[]{:S(2)}) collective-permute-start(bf16[8,112,128]{2,1,0:T(8,128)(2,1)S(1)} %bitcast.25), channel_id=1, source_target_pairs={{0,40},{4,44},{8,48},{12,52},{16,56},{20,60},{24,0},{28,4},{32,8},... | collective-permute-start | bytes 688136 | tf_op jit(solution)/shard_map/ppermute | solution.py:174
  56.0 0.7 constant_dynamic-update-slice_fusion.29
  56.7 0.7 constant_dynamic-update-slice_fusion.28
  57.3 0.7 constant_dynamic-update-slice_fusion.27
  58.0 12.9 %collective-permute-done.14.refs_1_ = bf16[32,112,128]{2,1,0:T(8,128)(2,1)S(1)} collective-permute-done((bf16[32,112,128]{2,1,0:T(8,128)(2,1)S(1)}, bf16[32,112,128]{2,1,0:T(8,128)(2,1)S(1)}, u32[]{:S(2)}, u32[]{:S(2)}) %collective-permute-start.14) | collective-permute-done | bytes 917536 | tf_op jit(solution)/shard_map/ppermute | solution.py:178
  71.0 0.0 collective-permute-done.15.refs_2_
  71.1 0.0 collective-permute-done.8.refs_0_
  71.1 0.0 collective-permute-done.9.refs_1_
  71.1 0.1 pad_maximum_fusion.2
  71.2 1.6 %collective-permute-start.16 = (bf16[32,112,128]{2,1,0:T(8,128)(2,1)S(1)}, bf16[32,112,128]{2,1,0:T(8,128)(2,1)S(1)}, u32[]{:S(2)}, u32[]{:S(2)}) collective-permute-start(bf16[32,112,128]{2,1,0:T(8,128)(2,1)S(1)} %get-tuple-element.55), channel_id=1, source_target_pairs={{0,1},{1,2},{2,3},{3,0},{4,5},{5,6},{6,7},{7,4},{8,9},{9,10},{10,1... | collective-permute-start | bytes 2752520 | tf_op jit(solution)/shard_map/ppermute | solution.py:178
  72.8 1.8 %collective-permute-start.17 = (bf16[32,112,128]{2,1,0:T(8,128)(2,1)S(1)}, bf16[32,112,128]{2,1,0:T(8,128)(2,1)S(1)}, u32[]{:S(2)}, u32[]{:S(2)}) collective-permute-start(bf16[32,112,128]{2,1,0:T(8,128)(2,1)S(1)} %get-tuple-element.56), channel_id=1, source_target_pairs={{0,3},{1,0},{2,1},{3,2},{4,7},{5,4},{6,5},{7,6},{8,11},{9,8},{10,9... | collective-permute-start | bytes 2752520 | tf_op jit(solution)/shard_map/ppermute | solution.py:178
  74.7 0.1 collective-permute-start.20
  74.8 2.3 %collective-permute-start.21 = (bf16[16,112,128]{2,1,0:T(8,128)(2,1)S(1)}, bf16[16,112,128]{2,1,0:T(8,128)(2,1)S(1)}, u32[]{:S(2)}, u32[]{:S(2)}) collective-permute-start(bf16[16,112,128]{2,1,0:T(8,128)(2,1)S(1)} %get-tuple-element.60), channel_id=1, source_target_pairs={{0,128},{4,132},{8,136},{12,140},{16,144},{20,148},{24,152},{28,15... | collective-permute-start | bytes 1376264 | tf_op jit(solution)/shard_map/ppermute | solution.py:208
  77.1 1.2 %collective-permute-start.22 = (bf16[16,112,128]{2,1,0:T(8,128)(2,1)S(1)}, bf16[16,112,128]{2,1,0:T(8,128)(2,1)S(1)}, u32[]{:S(2)}, u32[]{:S(2)}) collective-permute-start(bf16[16,112,128]{2,1,0:T(8,128)(2,1)S(1)} %get-tuple-element.59), channel_id=1, source_target_pairs={{0,192},{4,196},{8,200},{12,204},{16,208},{20,212},{24,216},{28,22... | collective-permute-start | bytes 1376264 | tf_op jit(solution)/shard_map/ppermute | solution.py:208
  78.3 15.6 %collective-permute-done.16.refs_3_.refs_2_ = bf16[32,112,128]{2,1,0:T(8,128)(2,1)S(1)} collective-permute-done((bf16[32,112,128]{2,1,0:T(8,128)(2,1)S(1)}, bf16[32,112,128]{2,1,0:T(8,128)(2,1)S(1)}, u32[]{:S(2)}, u32[]{:S(2)}) %collective-permute-start.16) | collective-permute-done | bytes 917536 | tf_op jit(solution)/shard_map/ppermute | solution.py:178
  93.9 0.0 collective-permute-done.17.refs_4_.refs_3_
  93.9 1.0 collective-permute-start.18
  94.9 2.3 %collective-permute-start.19 = (bf16[8,112,128]{2,1,0:T(8,128)(2,1)S(1)}, bf16[8,112,128]{2,1,0:T(8,128)(2,1)S(1)}, u32[]{:S(2)}, u32[]{:S(2)}) collective-permute-start(bf16[8,112,128]{2,1,0:T(8,128)(2,1)S(1)} %slice.227), channel_id=1, source_target_pairs={{0,3},{1,0},{2,1},{3,2},{4,7},{5,4},{6,5},{7,6},{8,11},{9,8},{10,9... | collective-permute-start | bytes 688136 | tf_op jit(solution)/shard_map/ppermute | solution.py:178
  97.2 0.0 collective-permute-done.20.refs_1_
  97.2 0.0 collective-permute-done.21.refs_2_
  97.2 0.1 collective-permute-done.22.refs_3_
  97.4 3.1 %place.3.refs_5_ = bf16[7168,512]{1,0:T(8,128)(2,1)} custom-call(s32[84]{0:T(128)S(1)} %pad_add_fusion.tables, bf16[16,112,128]{2,1,0:T(8,128)(2,1)S(1)} %get-tuple-element.62.refs_0_, bf16[16,112,128]{2,1,0:T(8,128)(2,1)S(1)} %collective-permute-done.20.refs_1_, bf16[16,112,128]{2,1,0:T(8,128)(2,1)S(1)} %collective-permute-done.21.refs_2_, ...), custom_call_target="tpu_custom_call" | custom-call | bytes 3670016 | tf_op jit(solution)/shard_map/place/pallas_call | solution.py:127
  100.4 4.0 %place.4.refs_6_ = bf16[7168,512]{1,0:T(8,128)(2,1)} custom-call(s32[84]{0:T(128)S(1)} %pad_add_fusion.tables, bf16[32,112,128]{2,1,0:T(8,128)(2,1)S(1)} %bitcast.24, bf16[32,112,128]{2,1,0:T(8,128)(2,1)S(1)} %collective-permute-done.14.refs_1_, bf16[32,112,128]{2,1,0:T(8,128)(2,1)S(1)} %collective-permute-done.15.refs_2_, ...), custom_call_target="tpu_custom_call", output_to_operand_aliasing={{}: (6, {})} | custom-call | bytes 7340032 | tf_op jit(solution)/shard_map/place/pallas_call | solution.py:127
  104.4 0.0 collective-permute-done.19.refs_5_
  104.4 3.7 %place.5 = bf16[7168,512]{1,0:T(8,128)(2,1)} custom-call(s32[84]{0:T(128)S(1)} %pad_add_fusion.tables, bf16[8,112,128]{2,1,0:T(8,128)(2,1)S(1)} %collective-permute-done.8.refs_0_, bf16[8,112,128]{2,1,0:T(8,128)(2,1)S(1)} %collective-permute-done.9.refs_1_, ...), custom_call_target="tpu_custom_call", output_to_operand_aliasing={{}: (7, {})} | custom-call | bytes 3670016 | tf_op jit(solution)/shard_map/place/pallas_call | solution.py:127
  (34 shorter events, 0.5 us)
Async XLA Ops:
  0.0 3.3 %collective-permute-start = (bf16[4,112,512]{2,1,0:T(8,128)(2,1)}, bf16[4,112,512]{2,1,0:T(8,128)(2,1)S(1)}, u32[]{:S(2)}, u32[]{:S(2)}) collective-permute-start(bf16[4,112,512]{2,1,0:T(8,128)(2,1)} %refs_0_.1), channel_id=1, source_target_pairs={{0,4},{4,0},{8,12},{12,8},{16,20},{20,16},{24,28},{28,24},{32,36},... | collective-permute-start | bytes 1376264 | tf_op jit(solution)/shard_map/ppermute | solution.py:66
  0.0 3.3 %collective-permute-start.1 = (bf16[4,112,512]{2,1,0:T(8,128)(2,1)}, bf16[4,112,512]{2,1,0:T(8,128)(2,1)S(1)}, u32[]{:S(2)}, u32[]{:S(2)}) collective-permute-start(bf16[4,112,512]{2,1,0:T(8,128)(2,1)} %refs_1_.1), channel_id=1, source_target_pairs={{0,4},{4,0},{8,12},{12,8},{16,20},{20,16},{24,28},{28,24},{32,36},... | collective-permute-start | bytes 1376264 | tf_op jit(solution)/shard_map/ppermute | solution.py:67
  0.5 2.7 %collective-permute-start.2 = (f32[112]{0:T(128)}, f32[112]{0:T(128)S(1)}, u32[]{:S(2)}, u32[]{:S(2)}) collective-permute-start(f32[112]{0:T(128)} %param.8), channel_id=1, source_target_pairs={{0,4},{4,0},{8,12},{12,8},{16,20},{20,16},{24,28},{28,24},{32,36},... | collective-permute-start | bytes 1352 | tf_op jit(solution)/shard_map/ppermute | solution.py:68
  3.3 1.0 copy-start
  4.3 1.0 copy-start.1
  8.5 13.9 %collective-permute-start.3 = (bf16[8,112,128]{2,1,0:T(8,128)(2,1)S(1)}, bf16[8,112,128]{2,1,0:T(8,128)(2,1)S(1)}, u32[]{:S(2)}, u32[]{:S(2)}) collective-permute-start(bf16[8,112,128]{2,1,0:T(8,128)(2,1)S(1)} %pad_maximum_fusion.4), channel_id=1, source_target_pairs={{0,8},{4,12},{8,16},{12,20},{16,24},{20,28},{24,32},{28,36},{32,40... | collective-permute-start | bytes 688136 | tf_op jit(solution)/shard_map/ppermute | solution.py:174
  10.5 11.9 %collective-permute-start.4 = (bf16[8,112,128]{2,1,0:T(8,128)(2,1)S(1)}, bf16[8,112,128]{2,1,0:T(8,128)(2,1)S(1)}, u32[]{:S(2)}, u32[]{:S(2)}) collective-permute-start(bf16[8,112,128]{2,1,0:T(8,128)(2,1)S(1)} %pad_maximum_fusion.5), channel_id=1, source_target_pairs={{0,56},{4,60},{8,0},{12,4},{16,8},{20,12},{24,16},{28,20},{32,24},... | collective-permute-start | bytes 688136 | tf_op jit(solution)/shard_map/ppermute | solution.py:174
  10.6 37.0 %all-to-all-start = ((bf16[16,2,112,128]{3,2,1,0:T(8,128)(2,1)}), bf16[16,2,112,128]{3,2,1,0:T(8,128)(2,1)S(1)}, u32[]{:S(2)}, u32[]{:S(2)}) async-start(bf16[16,2,112,128]{3,2,1,0:T(8,128)(2,1)} %get-tuple-element.48), calls=%async_computation | async-start | bytes 1835008 | tf_op jit(solution)/shard_map/all_to_all | solution.py:197
  22.5 15.8 %collective-permute-start.11 = (bf16[16,112,128]{2,1,0:T(8,128)(2,1)S(1)}, bf16[16,112,128]{2,1,0:T(8,128)(2,1)S(1)}, u32[]{:S(2)}, u32[]{:S(2)}) collective-permute-start(bf16[16,112,128]{2,1,0:T(8,128)(2,1)S(1)} %pad_maximum_fusion.3), channel_id=1, source_target_pairs={{0,3},{1,0},{2,1},{3,2},{4,7},{5,4},{6,5},{7,6},{8,11},{9,8},{10,9... | collective-permute-start | bytes 1376264 | tf_op jit(solution)/shard_map/ppermute | solution.py:178
  25.6 12.7 %collective-permute-start.10 = (bf16[16,112,128]{2,1,0:T(8,128)(2,1)S(1)}, bf16[16,112,128]{2,1,0:T(8,128)(2,1)S(1)}, u32[]{:S(2)}, u32[]{:S(2)}) collective-permute-start(bf16[16,112,128]{2,1,0:T(8,128)(2,1)S(1)} %pad_maximum_fusion.3), channel_id=1, source_target_pairs={{0,1},{1,2},{2,3},{3,0},{4,5},{5,6},{6,7},{7,4},{8,9},{9,10},{10,1... | collective-permute-start | bytes 1376264 | tf_op jit(solution)/shard_map/ppermute | solution.py:178
  25.6 7.3 %collective-permute-start.5 = (bf16[2,2,112,128]{3,2,1,0:T(8,128)(2,1)S(1)}, bf16[2,2,112,128]{3,2,1,0:T(8,128)(2,1)S(1)}, u32[]{:S(2)}, u32[]{:S(2)}) collective-permute-start(bf16[2,2,112,128]{3,2,1,0:T(8,128)(2,1)S(1)} %get-tuple-element.43), channel_id=1, source_target_pairs={{0,64},{4,68},{8,72},{12,76},{16,80},{20,84},{24,88},{28,92},{32,9... | collective-permute-start | bytes 344072 | tf_op jit(solution)/shard_map/ppermute | solution.py:169
  27.0 14.6 %collective-permute-start.6 = (bf16[2,2,112,128]{3,2,1,0:T(8,128)(2,1)S(1)}, bf16[2,2,112,128]{3,2,1,0:T(8,128)(2,1)S(1)}, u32[]{:S(2)}, u32[]{:S(2)}) collective-permute-start(bf16[2,2,112,128]{3,2,1,0:T(8,128)(2,1)S(1)} %get-tuple-element.44), channel_id=1, source_target_pairs={{0,128},{4,132},{8,136},{12,140},{16,144},{20,148},{24,152},{28,15... | collective-permute-start | bytes 344072 | tf_op jit(solution)/shard_map/ppermute | solution.py:169
  29.7 12.0 %collective-permute-start.7 = (bf16[2,2,112,128]{3,2,1,0:T(8,128)(2,1)S(1)}, bf16[2,2,112,128]{3,2,1,0:T(8,128)(2,1)S(1)}, u32[]{:S(2)}, u32[]{:S(2)}) collective-permute-start(bf16[2,2,112,128]{3,2,1,0:T(8,128)(2,1)S(1)} %get-tuple-element.45), channel_id=1, source_target_pairs={{0,192},{4,196},{8,200},{12,204},{16,208},{20,212},{24,216},{28,22... | collective-permute-start | bytes 344072 | tf_op jit(solution)/shard_map/ppermute | solution.py:169
  38.4 7.3 %collective-permute-start.12 = (bf16[8,112,128]{2,1,0:T(8,128)(2,1)S(1)}, bf16[8,112,128]{2,1,0:T(8,128)(2,1)S(1)}, u32[]{:S(2)}, u32[]{:S(2)}) collective-permute-start(bf16[8,112,128]{2,1,0:T(8,128)(2,1)S(1)} %slice.222), channel_id=1, source_target_pairs={{0,1},{1,2},{2,3},{3,0},{4,5},{5,6},{6,7},{7,4},{8,9},{9,10},{10,1... | collective-permute-start | bytes 688136 | tf_op jit(solution)/shard_map/ppermute | solution.py:178
  38.4 7.2 %collective-permute-start.13 = (bf16[8,112,128]{2,1,0:T(8,128)(2,1)S(1)}, bf16[8,112,128]{2,1,0:T(8,128)(2,1)S(1)}, u32[]{:S(2)}, u32[]{:S(2)}) collective-permute-start(bf16[8,112,128]{2,1,0:T(8,128)(2,1)S(1)} %slice.223), channel_id=1, source_target_pairs={{0,3},{1,0},{2,1},{3,2},{4,7},{5,4},{6,5},{7,6},{8,11},{9,8},{10,9... | collective-permute-start | bytes 688136 | tf_op jit(solution)/shard_map/ppermute | solution.py:178
  47.6 23.4 %collective-permute-start.14 = (bf16[32,112,128]{2,1,0:T(8,128)(2,1)S(1)}, bf16[32,112,128]{2,1,0:T(8,128)(2,1)S(1)}, u32[]{:S(2)}, u32[]{:S(2)}) collective-permute-start(bf16[32,112,128]{2,1,0:T(8,128)(2,1)S(1)} %bitcast.22), channel_id=1, source_target_pairs={{0,1},{1,2},{2,3},{3,0},{4,5},{5,6},{6,7},{7,4},{8,9},{9,10},{10,1... | collective-permute-start | bytes 2752520 | tf_op jit(solution)/shard_map/ppermute | solution.py:178
  49.1 21.9 %collective-permute-start.15 = (bf16[32,112,128]{2,1,0:T(8,128)(2,1)S(1)}, bf16[32,112,128]{2,1,0:T(8,128)(2,1)S(1)}, u32[]{:S(2)}, u32[]{:S(2)}) collective-permute-start(bf16[32,112,128]{2,1,0:T(8,128)(2,1)S(1)} %bitcast.23), channel_id=1, source_target_pairs={{0,3},{1,0},{2,1},{3,2},{4,7},{5,4},{6,5},{7,6},{8,11},{9,8},{10,9... | collective-permute-start | bytes 2752520 | tf_op jit(solution)/shard_map/ppermute | solution.py:178
  50.9 20.2 %collective-permute-start.8 = (bf16[8,112,128]{2,1,0:T(8,128)(2,1)S(1)}, bf16[8,112,128]{2,1,0:T(8,128)(2,1)S(1)}, u32[]{:S(2)}, u32[]{:S(2)}) collective-permute-start(bf16[8,112,128]{2,1,0:T(8,128)(2,1)S(1)} %bitcast.26), channel_id=1, source_target_pairs={{0,24},{4,28},{8,32},{12,36},{16,40},{20,44},{24,48},{28,52},{32,5... | collective-permute-start | bytes 688136 | tf_op jit(solution)/shard_map/ppermute | solution.py:174
  53.0 18.1 %collective-permute-start.9 = (bf16[8,112,128]{2,1,0:T(8,128)(2,1)S(1)}, bf16[8,112,128]{2,1,0:T(8,128)(2,1)S(1)}, u32[]{:S(2)}, u32[]{:S(2)}) collective-permute-start(bf16[8,112,128]{2,1,0:T(8,128)(2,1)S(1)} %bitcast.25), channel_id=1, source_target_pairs={{0,40},{4,44},{8,48},{12,52},{16,56},{20,60},{24,0},{28,4},{32,8},... | collective-permute-start | bytes 688136 | tf_op jit(solution)/shard_map/ppermute | solution.py:174
  71.0 3.6 %copy-start.2 = (bf16[16,112,128]{2,1,0:T(8,128)(2,1)S(1)}, bf16[16,112,128]{2,1,0:T(8,128)(2,1)}, u32[]{:S(2)}) copy-start(bf16[16,112,128]{2,1,0:T(8,128)(2,1)} %get-tuple-element.81) | copy-start | bytes 1376260
  71.0 3.6 %copy-start.3 = (bf16[16,112,128]{2,1,0:T(8,128)(2,1)S(1)}, bf16[16,112,128]{2,1,0:T(8,128)(2,1)}, u32[]{:S(2)}) copy-start(bf16[16,112,128]{2,1,0:T(8,128)(2,1)} %get-tuple-element.82) | copy-start | bytes 1376260
  71.0 3.5 %copy-start.4 = (bf16[16,112,128]{2,1,0:T(8,128)(2,1)S(1)}, bf16[16,112,128]{2,1,0:T(8,128)(2,1)}, u32[]{:S(2)}) copy-start(bf16[16,112,128]{2,1,0:T(8,128)(2,1)} %get-tuple-element.83) | copy-start | bytes 1376260
  71.2 22.6 %collective-permute-start.16 = (bf16[32,112,128]{2,1,0:T(8,128)(2,1)S(1)}, bf16[32,112,128]{2,1,0:T(8,128)(2,1)S(1)}, u32[]{:S(2)}, u32[]{:S(2)}) collective-permute-start(bf16[32,112,128]{2,1,0:T(8,128)(2,1)S(1)} %get-tuple-element.55), channel_id=1, source_target_pairs={{0,1},{1,2},{2,3},{3,0},{4,5},{5,6},{6,7},{7,4},{8,9},{9,10},{10,1... | collective-permute-start | bytes 2752520 | tf_op jit(solution)/shard_map/ppermute | solution.py:178
  72.8 21.1 %collective-permute-start.17 = (bf16[32,112,128]{2,1,0:T(8,128)(2,1)S(1)}, bf16[32,112,128]{2,1,0:T(8,128)(2,1)S(1)}, u32[]{:S(2)}, u32[]{:S(2)}) collective-permute-start(bf16[32,112,128]{2,1,0:T(8,128)(2,1)S(1)} %get-tuple-element.56), channel_id=1, source_target_pairs={{0,3},{1,0},{2,1},{3,2},{4,7},{5,4},{6,5},{7,6},{8,11},{9,8},{10,9... | collective-permute-start | bytes 2752520 | tf_op jit(solution)/shard_map/ppermute | solution.py:178
  74.7 22.5 %collective-permute-start.20 = (bf16[16,112,128]{2,1,0:T(8,128)(2,1)S(1)}, bf16[16,112,128]{2,1,0:T(8,128)(2,1)S(1)}, u32[]{:S(2)}, u32[]{:S(2)}) collective-permute-start(bf16[16,112,128]{2,1,0:T(8,128)(2,1)S(1)} %get-tuple-element.61), channel_id=1, source_target_pairs={{0,64},{4,68},{8,72},{12,76},{16,80},{20,84},{24,88},{28,92},{32,9... | collective-permute-start | bytes 1376264 | tf_op jit(solution)/shard_map/ppermute | solution.py:208
  74.8 22.5 %collective-permute-start.21 = (bf16[16,112,128]{2,1,0:T(8,128)(2,1)S(1)}, bf16[16,112,128]{2,1,0:T(8,128)(2,1)S(1)}, u32[]{:S(2)}, u32[]{:S(2)}) collective-permute-start(bf16[16,112,128]{2,1,0:T(8,128)(2,1)S(1)} %get-tuple-element.60), channel_id=1, source_target_pairs={{0,128},{4,132},{8,136},{12,140},{16,144},{20,148},{24,152},{28,15... | collective-permute-start | bytes 1376264 | tf_op jit(solution)/shard_map/ppermute | solution.py:208
  77.1 20.3 %collective-permute-start.22 = (bf16[16,112,128]{2,1,0:T(8,128)(2,1)S(1)}, bf16[16,112,128]{2,1,0:T(8,128)(2,1)S(1)}, u32[]{:S(2)}, u32[]{:S(2)}) collective-permute-start(bf16[16,112,128]{2,1,0:T(8,128)(2,1)S(1)} %get-tuple-element.59), channel_id=1, source_target_pairs={{0,192},{4,196},{8,200},{12,204},{16,208},{20,212},{24,216},{28,22... | collective-permute-start | bytes 1376264 | tf_op jit(solution)/shard_map/ppermute | solution.py:208
  93.9 10.5 %collective-permute-start.18 = (bf16[8,112,128]{2,1,0:T(8,128)(2,1)S(1)}, bf16[8,112,128]{2,1,0:T(8,128)(2,1)S(1)}, u32[]{:S(2)}, u32[]{:S(2)}) collective-permute-start(bf16[8,112,128]{2,1,0:T(8,128)(2,1)S(1)} %slice.226), channel_id=1, source_target_pairs={{0,1},{1,2},{2,3},{3,0},{4,5},{5,6},{6,7},{7,4},{8,9},{9,10},{10,1... | collective-permute-start | bytes 688136 | tf_op jit(solution)/shard_map/ppermute | solution.py:178
  94.9 9.5 %collective-permute-start.19 = (bf16[8,112,128]{2,1,0:T(8,128)(2,1)S(1)}, bf16[8,112,128]{2,1,0:T(8,128)(2,1)S(1)}, u32[]{:S(2)}, u32[]{:S(2)}) collective-permute-start(bf16[8,112,128]{2,1,0:T(8,128)(2,1)S(1)} %slice.227), channel_id=1, source_target_pairs={{0,3},{1,0},{2,1},{3,2},{4,7},{5,4},{6,5},{7,6},{8,11},{9,8},{10,9... | collective-permute-start | bytes 688136 | tf_op jit(solution)/shard_map/ppermute | solution.py:178

commit v3 on v2

--- a/solution.py
+++ b/solution.py
@@ -41,12 +41,13 @@
             def _():
                 owner[tables[4 * e + k]] = e
     for side, scale in enumerate((gain, gain_far)):
+        gate, up = (ref[...].reshape(experts * rows, 512) for ref in sources[2 * side : 2 * side + 2])
+        got = jnp.dot(gate, matrix[:512, :], preferred_element_type=jnp.float32)
+        got += jnp.dot(up, matrix[512:, :], preferred_element_type=jnp.float32)
         for e in range(experts):
-            got = jnp.dot(sources[2 * side][e], matrix[:512, :], preferred_element_type=jnp.float32)
-            got += jnp.dot(sources[2 * side + 1][e], matrix[512:, :], preferred_element_type=jnp.float32)
-            got = (got * scale[...]).astype(BF16)
+            part = (got[e * rows : (e + 1) * rows] * scale[...]).astype(BF16)
             for zl in range(4):
-                picked[e * 4 + zl, side] = got[:, zl * 128 : (zl + 1) * 128]
+                picked[e * 4 + zl, side] = part[:, zl * 128 : (zl + 1) * 128]
     for g, group in enumerate(GROUPS):
         for k, dz in enumerate(group):
             zt = (z + dz) % NZ
@@ -89,55 +90,75 @@
     return [outs[g * NX : (g + 1) * NX] for g in range(len(GROUPS))], outs[-1]
 
 
-def place_kernel(blocks, sizes, relative, tables, *refs):
-    held = refs[-len(sizes) - 3 : -3]
-    built, load_sems, save_sems = refs[-3:]
-    out, rows = refs[-len(sizes) - 4], built.shape[1]
+def cost(megabytes):
+    return pl.CostEstimate(flops=0, bytes_accessed=int(megabytes * 1e6), transcendentals=0)
+
+
+def pack_kernel(outs, count, *refs):
+    for out, entries in zip(refs[count:], outs):
+        for at, (k, index) in enumerate(entries):
+            out[at] = refs[k][index]
+
+
+def pack(arrays, outs):
+    vmem = pl.BlockSpec(memory_space=pltpu.VMEM)
+    return pl.pallas_call(
+        functools.partial(pack_kernel, outs, len(arrays)),
+        out_shape=[jax.ShapeDtypeStruct((len(out),) + arrays[0].shape[1:], BF16) for out in outs],
+        in_specs=[vmem] * len(arrays),
+        out_specs=[vmem] * len(outs),
+        compiler_params=pltpu.CompilerParams(vmem_limit_bytes=16 * 1024 * 1024),
+        cost_estimate=cost(1),
+        name="pack",
+    )(*arrays)
+
+
+def blocks_of(array, start, stop):
+    return [(array, index) for index in range(start, stop)]
+
+
+def place_kernel(blocks, arrays, tables, *refs):
+    held = refs[:arrays]
+    out, built, sems = refs[-3:]
+    rows = built.shape[1]
     x, z, core = place()
     y = lax.axis_index("rep")
-    loads = [
-        pltpu.make_async_copy(refs[k].at[pl.ds(at, size)], held[k], load_sems.at[k])
-        for k, (at, size) in enumerate(sizes)
-    ]
-    for load in loads:
-        load.start()
-    for load in loads:
-        load.wait()
     saves = []
-    for at, (dz, dx, side, parts) in enumerate(blocks):
+    for at, (dz, side, xs, dx, parts) in enumerate(blocks):
         for step, (k, index) in enumerate(parts):
-            group = (y + step) % NY if relative else step
-            built[at, :, pl.ds(pl.multiple_of(group * 128, 128), 128)] = held[k][index]
-        xs, zs = ((x - dx) % NX, (z - dz) % NZ) if dz is not None else (dx // 4, 2 * (dx % 4) + z % 2)
-        block = tables[20 + (xs * NZ + zs) * 2 + (core ^ side)]
+            column = pl.multiple_of(((y + step) % NY) * 128, 128)
+            built[at, :, pl.ds(column, 128)] = held[k][index]
+        if dx is None:
+            source = xs * NZ + (2 * dz + z % 2)
+        else:
+            source = (x - dx) % NX * NZ + (z - dz) % NZ
+        block = tables[20 + source * 2 + (core ^ side)]
         row = pl.multiple_of(block * rows, 16)
-        save = pltpu.make_async_copy(built.at[at], out.at[pl.ds(row, rows)], save_sems.at[at])
+        save = pltpu.make_async_copy(built.at[at], out.at[pl.ds(row, rows)], sems.at[at])
         save.start()
         saves.append(save)
     for save in saves:
         save.wait()
 
 
-def place_blocks(out, tables, devices, arrays, blocks, relative=True):
-    rows = arrays[0][0].shape[1]
-    anywhere = pl.BlockSpec(memory_space=pl.ANY)
-    sizes = [(at, size) for _, at, size in arrays]
-    args = [tables] + [array for array, _, _ in arrays] + ([] if out is None else [out])
+def place_blocks(out, tables, devices, arrays, blocks):
+    rows = arrays[0].shape[1]
+    vmem, anywhere = pl.BlockSpec(memory_space=pltpu.VMEM), pl.BlockSpec(memory_space=pl.ANY)
+    args = [tables, *arrays] + ([] if out is None else [out])
     total = len(blocks) * rows * 512 * 2
     return pl.pallas_call(
-        functools.partial(place_kernel, blocks, sizes, relative),
+        functools.partial(place_kernel, blocks, len(arrays)),
         out_shape=jax.ShapeDtypeStruct((devices * rows, 512), BF16),
-        in_specs=[pl.BlockSpec(memory_space=pltpu.SMEM)] + [anywhere] * (len(args) - 1),
+        in_specs=[pl.BlockSpec(memory_space=pltpu.SMEM)] + [vmem] * len(arrays)
+        + ([] if out is None else [anywhere]),
         out_specs=anywhere,
-        scratch_shapes=[pltpu.VMEM((size, rows, 128), BF16) for _, size in sizes]
-        + [
+        scratch_shapes=[
             pltpu.VMEM((len(blocks), rows, 512), BF16),
-            pltpu.SemaphoreType.DMA((len(sizes),)),
             pltpu.SemaphoreType.DMA((len(blocks),)),
         ],
         input_output_aliases={} if out is None else {len(args) - 1: 0},
-        compiler_params=pltpu.CompilerParams(vmem_limit_bytes=16 * 1024 * 1024),
-        cost_estimate=pl.CostEstimate(flops=0, bytes_accessed=2 * total, transcendentals=0),
+        compiler_params=pltpu.CompilerParams(vmem_limit_bytes=24 * 1024 * 1024),
+        cost_estimate=cost(2e-6 * total),
         name="place",
     )(*args)
 
@@ -176,22 +197,6 @@
     def cross_y(to_right, to_left, *done):
         pair = after([jnp.concatenate(to_right), jnp.concatenate(to_left)], *done)
         return lax.ppermute(pair[0], "rep", along_y(1)), lax.ppermute(pair[1], "rep", along_y(-1))
-
-    def ring_blocks(dzs):
-        n, count = len(dzs), 8 * len(dzs)
-        blocks = []
-        for at in range(count):
-            dz, dx, side = dzs[at // 8], at % 8 // 2, at % 2
-            far = (n + 2, at) if at < count // 2 else (n + 3, at - count // 2)
-            blocks.append((dz, dx, side, ((at // 8, at % 8), (n + 1, at), far, (n, at))))
-        return blocks
-
-    def finish(out, dzs, own, left, right, far_left, far_right, base):
-        count = 8 * len(dzs)
-        arrays = [(a, 0, 8) for a in own]
-        arrays += [(left, 0, count), (right, 0, count)]
-        arrays += [(far_left, base, count // 2), (far_right, base, count // 2)]
-        return place_blocks(out, tables, devices, arrays, ring_blocks(dzs))
 
     own1 = cross_z((1, 7), [jnp.concatenate([piece[k] for piece in parts[0]]) for k in range(2)])
     own = lax.all_to_all(even, "fsdp", 0, 0, tiled=True, axis_index_groups=same_parity)
@@ -208,19 +213,23 @@
         bundles.append(lax.ppermute(bundle, "fsdp", along_x(dx)) if dx else bundle)
     own3 = cross_z((3, 5), cross_x(1, *own1))
     l3, r3 = cross_y(own3 + [le[:16]], own3 + [re[16:]])
+    l4, r4 = cross_y([l3[:8]], [r3[8:16]])
     late = [
-        (dz, dx, side, tuple((dx, step * 4 + 2 * k + side) for step in range(NY)))
+        (dz, side, None, dx, tuple((dx, step * 4 + 2 * k + side) for step in range(NY)))
         for dx in range(NX) for k, dz in enumerate(GROUPS[0]) for side in range(2)
     ]
-    out = place_blocks(None, tables, devices, [(b, 0, 16) for b in bundles], late)
-    l4, r4 = cross_y([l3[:8]], [r3[8:16]])
+    out = place_blocks(None, tables, devices, bundles, late)
     evens = [
-        (None, at // 2, at % 2, ((0, at), (2, at), (3, at) if at < 16 else (4, at - 16), (1, at)))
+        (at // 2 % 4, at % 2, at // 8, None, ((0, at), (2, at), (3, 16 + at) if at < 16 else (4, at), (1, at)))
         for at in range(32)
     ]
-    arrays = [(own, 0, 32), (le, 0, 32), (re, 0, 32), (l3, 16, 16), (r3, 16, 16)]
-    out = place_blocks(out, tables, devices, arrays, evens)
-    out = finish(out, (3, 5), own3, l3, r3, l4, r4, 0)
+    out = place_blocks(out, tables, devices, [own, le, re, l3, r3], evens)
+    odds = [
+        (GROUPS[1][at // 8], at % 2, None, at % 8 // 2,
+         ((at // 8, at % 8), (3, at), (4, at) if at < 8 else (5, at - 8), (2, at)))
+        for at in range(16)
+    ]
+    out = place_blocks(out, tables, devices, [*own3, l3, r3, l4, r4], odds)
     return out[None]
 
 

time: 109 us -> 104 us (0.954)
  Pallas kernels: 13.7 us -> 9.28 us
    pallas_call x3, Pallas kernels: 10.8 us -> 6.57 us  [place_blocks(): pl.pallas_call(functools.partial(place_kernel, blocks, len(arrays)), out_...]
  transfers between devices with their start and end apart: 24 -> 24, of which waited for: 7 -> 7; matrix products, arithmetic and copies ran while one was open for 6% -> 6% of each run, Pallas kernels for 6% -> 4%
where the time goes in v3:
time: 104 us
  starting transfers between devices  45.1 us (43%)
  waiting for transfers between devices  40.1 us (39%)
  Pallas kernels  9.28 us (9%)
  local copies, waits for them, and re-layouts  7.37 us (7%)
  other arithmetic  1.45 us (1%)
    ppermute x5, waiting for transfers between devices, cross_y(): lax.ppermute(pair[0], 'rep', along_y(1))  37.8 us
    ppermute x5, starting transfers between devices, cross_y(): lax.ppermute(pair[1], 'rep', along_y(-1))  12.1 us
    all_to_all x1, starting transfers between devices, local(): lax.all_to_all(even, 'fsdp', 0, 0, tiled=True, axis_index_groups=same_par...  11.8 us
    ppermute x4, starting transfers between devices, cross_z(): return [lax.ppermute(p, 'fsdp', along_z(dz)) for dz, p in zip(dzs, pieces)]  7.4 us
    pallas_call x3, Pallas kernels, place_blocks(): pl.pallas_call(functools.partial(place_kernel, blocks, len(arrays)), out_...  6.57 us
    ppermute x3, starting transfers between devices, cross_x(): lax.ppermute(pieces[dx], 'fsdp', along_x(dx))  5.6 us
    unnamed x17, local copies, waits for them, and re-layouts  5.5 us
    ppermute x5, starting transfers between devices, cross_y(): lax.ppermute(pair[0], 'rep', along_y(1))  4.15 us
  transfers between devices with their start and end apart: 24, of which 7 were waited for; matrix products, arithmetic and copies ran while one was open for 6% of the time, Pallas kernels for 4%

profile of v3, /device:TPU:64, one launch (start us, length us, event | category | flops | bytes accessed | tf_op | source)
XLA Modules:
  0.0 103.8 jit_solution(17740918354316427354)
XLA Ops:
  0.0 0.0 collective-permute-start
  0.0 0.5 collective-permute-start.1
  0.5 0.0 collective-permute-start.2
  0.5 0.8 reshape.18
  1.3 0.4 fusion.10.refs_6_
  1.7 0.8 pad_add_fusion.tables
  2.4 0.8 copy.9.refs_4_
  3.2 0.0 collective-permute-done.2
  3.2 0.1 copy.10.refs_5_
  3.3 0.0 collective-permute-done.refs_2_
  3.3 0.0 collective-permute-done.1.refs_3_
  3.3 0.0 copy-start
  3.3 1.0 copy-done
  4.3 1.0 copy-done.1
  5.4 2.7 %prepare.1 = (bf16[2,2,112,128]{3,2,1,0:T(8,128)(2,1)S(1)}, bf16[2,2,112,128]{3,2,1,0:T(8,128)(2,1)S(1)}, bf16[2,2,112,128]{3,2,1,0:T(8,128)(2,1)S(1)}, bf16[2,2...) custom-call(s32[84]{0:T(128)S(1)} %pad_add_fusion.tables, ...), custom_call_target="tpu_custom_call" | custom-call | tf_op jit(solution)/shard_map/prepare/pallas_call | solution.py:75
  8.2 2.0 %collective-permute-start.3 = (bf16[8,112,128]{2,1,0:T(8,128)(2,1)S(1)}, bf16[8,112,128]{2,1,0:T(8,128)(2,1)S(1)}, u32[]{:S(2)}, u32[]{:S(2)}) collective-permute-start(bf16[8,112,128]{2,1,0:T(8,128)(2,1)S(1)} %pad_maximum_fusion.4), channel_id=1, source_target_pairs={{0,8},{4,12},{8,16},{12,20},{16,24},{20,28},{24,32},{28,36},{32,40... | collective-permute-start | bytes 688136 | tf_op jit(solution)/shard_map/ppermute | solution.py:195
  10.2 0.1 collective-permute-start.4
  10.3 11.8 %all-to-all-start = ((bf16[16,2,112,128]{3,2,1,0:T(8,128)(2,1)}), bf16[16,2,112,128]{3,2,1,0:T(8,128)(2,1)S(1)}, u32[]{:S(2)}, u32[]{:S(2)}) async-start(bf16[16,2,112,128]{3,2,1,0:T(8,128)(2,1)} %get-tuple-element.48), calls=%async_computation | async-start | bytes 1835008 | tf_op jit(solution)/shard_map/all_to_all | solution.py:202
  22.1 0.0 collective-permute-done.3
  22.1 0.0 collective-permute-done.4
  22.2 3.1 %collective-permute-start.11 = (bf16[16,112,128]{2,1,0:T(8,128)(2,1)S(1)}, bf16[16,112,128]{2,1,0:T(8,128)(2,1)S(1)}, u32[]{:S(2)}, u32[]{:S(2)}) collective-permute-start(bf16[16,112,128]{2,1,0:T(8,128)(2,1)S(1)} %pad_maximum_fusion.3), channel_id=1, source_target_pairs={{0,3},{1,0},{2,1},{3,2},{4,7},{5,4},{6,5},{7,6},{8,11},{9,8},{10,9... | collective-permute-start | bytes 1376264 | tf_op jit(solution)/shard_map/ppermute | solution.py:199
  25.3 0.0 collective-permute-start.10
  25.3 1.5 %collective-permute-start.5 = (bf16[2,2,112,128]{3,2,1,0:T(8,128)(2,1)S(1)}, bf16[2,2,112,128]{3,2,1,0:T(8,128)(2,1)S(1)}, u32[]{:S(2)}, u32[]{:S(2)}) collective-permute-start(bf16[2,2,112,128]{3,2,1,0:T(8,128)(2,1)S(1)} %get-tuple-element.43), channel_id=1, source_target_pairs={{0,64},{4,68},{8,72},{12,76},{16,80},{20,84},{24,88},{28,92},{32,9... | collective-permute-start | bytes 344072 | tf_op jit(solution)/shard_map/ppermute | solution.py:190
  26.8 2.7 %collective-permute-start.6 = (bf16[2,2,112,128]{3,2,1,0:T(8,128)(2,1)S(1)}, bf16[2,2,112,128]{3,2,1,0:T(8,128)(2,1)S(1)}, u32[]{:S(2)}, u32[]{:S(2)}) collective-permute-start(bf16[2,2,112,128]{3,2,1,0:T(8,128)(2,1)S(1)} %get-tuple-element.44), channel_id=1, source_target_pairs={{0,128},{4,132},{8,136},{12,140},{16,144},{20,148},{24,152},{28,15... | collective-permute-start | bytes 344072 | tf_op jit(solution)/shard_map/ppermute | solution.py:190
  29.4 1.5 %collective-permute-start.7 = (bf16[2,2,112,128]{3,2,1,0:T(8,128)(2,1)S(1)}, bf16[2,2,112,128]{3,2,1,0:T(8,128)(2,1)S(1)}, u32[]{:S(2)}, u32[]{:S(2)}) collective-permute-start(bf16[2,2,112,128]{3,2,1,0:T(8,128)(2,1)S(1)} %get-tuple-element.45), channel_id=1, source_target_pairs={{0,192},{4,196},{8,200},{12,204},{16,208},{20,212},{24,216},{28,22... | collective-permute-start | bytes 344072 | tf_op jit(solution)/shard_map/ppermute | solution.py:190
  30.9 0.7 constant_dynamic-update-slice_fusion.31
  31.6 0.7 constant_dynamic-update-slice_fusion.30
  32.3 0.3 collective-permute-done.5
  32.6 5.4 %collective-permute-done.10 = bf16[16,112,128]{2,1,0:T(8,128)(2,1)S(1)} collective-permute-done((bf16[16,112,128]{2,1,0:T(8,128)(2,1)S(1)}, bf16[16,112,128]{2,1,0:T(8,128)(2,1)S(1)}, u32[]{:S(2)}, u32[]{:S(2)}) %collective-permute-start.10) | collective-permute-done | bytes 458784 | tf_op jit(solution)/shard_map/ppermute | solution.py:199
  38.0 0.0 collective-permute-done.11
  38.1 0.1 collective-permute-start.12
  38.2 3.2 %collective-permute-start.13 = (bf16[8,112,128]{2,1,0:T(8,128)(2,1)S(1)}, bf16[8,112,128]{2,1,0:T(8,128)(2,1)S(1)}, u32[]{:S(2)}, u32[]{:S(2)}) collective-permute-start(bf16[8,112,128]{2,1,0:T(8,128)(2,1)S(1)} %slice.223), channel_id=1, source_target_pairs={{0,3},{1,0},{2,1},{3,2},{4,7},{5,4},{6,5},{7,6},{8,11},{9,8},{10,9... | collective-permute-start | bytes 688136 | tf_op jit(solution)/shard_map/ppermute | solution.py:199
  41.4 0.0 collective-permute-done.7
  41.4 4.0 %collective-permute-done.12 = bf16[8,112,128]{2,1,0:T(8,128)(2,1)S(1)} collective-permute-done((bf16[8,112,128]{2,1,0:T(8,128)(2,1)S(1)}, bf16[8,112,128]{2,1,0:T(8,128)(2,1)S(1)}, u32[]{:S(2)}, u32[]{:S(2)}) %collective-permute-start.12) | collective-permute-done | bytes 229408 | tf_op jit(solution)/shard_map/ppermute | solution.py:199
  45.4 0.0 collective-permute-done.13
  45.4 1.9 %all-to-all-done = bf16[16,2,112,128]{3,2,1,0:T(8,128)(2,1)S(1)} async-done(((bf16[16,2,112,128]{3,2,1,0:T(8,128)(2,1)}), bf16[16,2,112,128]{3,2,1,0:T(8,128)(2,1)S(1)}, u32[]{:S(2)}, u32[]{:S(2)}) %all-to-all-start) | async-done | bytes 917536 | tf_op jit(solution)/shard_map/all_to_all | solution.py:202
  47.3 1.5 %collective-permute-start.14 = (bf16[32,112,128]{2,1,0:T(8,128)(2,1)S(1)}, bf16[32,112,128]{2,1,0:T(8,128)(2,1)S(1)}, u32[]{:S(2)}, u32[]{:S(2)}) collective-permute-start(bf16[32,112,128]{2,1,0:T(8,128)(2,1)S(1)} %bitcast.22), channel_id=1, source_target_pairs={{0,1},{1,2},{2,3},{3,0},{4,5},{5,6},{6,7},{7,4},{8,9},{9,10},{10,1... | collective-permute-start | bytes 2752520 | tf_op jit(solution)/shard_map/ppermute | solution.py:199
  48.8 1.7 %collective-permute-start.15 = (bf16[32,112,128]{2,1,0:T(8,128)(2,1)S(1)}, bf16[32,112,128]{2,1,0:T(8,128)(2,1)S(1)}, u32[]{:S(2)}, u32[]{:S(2)}) collective-permute-start(bf16[32,112,128]{2,1,0:T(8,128)(2,1)S(1)} %bitcast.23), channel_id=1, source_target_pairs={{0,3},{1,0},{2,1},{3,2},{4,7},{5,4},{6,5},{7,6},{8,11},{9,8},{10,9... | collective-permute-start | bytes 2752520 | tf_op jit(solution)/shard_map/ppermute | solution.py:199
  50.6 2.3 %collective-permute-start.8 = (bf16[8,112,128]{2,1,0:T(8,128)(2,1)S(1)}, bf16[8,112,128]{2,1,0:T(8,128)(2,1)S(1)}, u32[]{:S(2)}, u32[]{:S(2)}) collective-permute-start(bf16[8,112,128]{2,1,0:T(8,128)(2,1)S(1)} %bitcast.26), channel_id=1, source_target_pairs={{0,24},{4,28},{8,32},{12,36},{16,40},{20,44},{24,48},{28,52},{32,5... | collective-permute-start | bytes 688136 | tf_op jit(solution)/shard_map/ppermute | solution.py:195
  52.9 3.0 %collective-permute-start.9 = (bf16[8,112,128]{2,1,0:T(8,128)(2,1)S(1)}, bf16[8,112,128]{2,1,0:T(8,128)(2,1)S(1)}, u32[]{:S(2)}, u32[]{:S(2)}) collective-permute-start(bf16[8,112,128]{2,1,0:T(8,128)(2,1)S(1)} %bitcast.25), channel_id=1, source_target_pairs={{0,40},{4,44},{8,48},{12,52},{16,56},{20,60},{24,0},{28,4},{32,8},... | collective-permute-start | bytes 688136 | tf_op jit(solution)/shard_map/ppermute | solution.py:195
  55.9 0.7 constant_dynamic-update-slice_fusion.29
  56.6 0.7 constant_dynamic-update-slice_fusion.28
  57.2 0.7 constant_dynamic-update-slice_fusion.27
  57.9 12.8 %collective-permute-done.14.refs_1_ = bf16[32,112,128]{2,1,0:T(8,128)(2,1)S(1)} collective-permute-done((bf16[32,112,128]{2,1,0:T(8,128)(2,1)S(1)}, bf16[32,112,128]{2,1,0:T(8,128)(2,1)S(1)}, u32[]{:S(2)}, u32[]{:S(2)}) %collective-permute-start.14) | collective-permute-done | bytes 917536 | tf_op jit(solution)/shard_map/ppermute | solution.py:199
  70.8 0.0 collective-permute-done.15.refs_2_
  70.8 0.0 collective-permute-done.8.refs_0_
  70.8 0.0 collective-permute-done.9.refs_1_
  70.8 0.1 pad_maximum_fusion.2
  71.0 1.6 %collective-permute-start.16 = (bf16[32,112,128]{2,1,0:T(8,128)(2,1)S(1)}, bf16[32,112,128]{2,1,0:T(8,128)(2,1)S(1)}, u32[]{:S(2)}, u32[]{:S(2)}) collective-permute-start(bf16[32,112,128]{2,1,0:T(8,128)(2,1)S(1)} %get-tuple-element.55), channel_id=1, source_target_pairs={{0,1},{1,2},{2,3},{3,0},{4,5},{5,6},{6,7},{7,4},{8,9},{9,10},{10,1... | collective-permute-start | bytes 2752520 | tf_op jit(solution)/shard_map/ppermute | solution.py:199
  72.5 1.8 %collective-permute-start.17 = (bf16[32,112,128]{2,1,0:T(8,128)(2,1)S(1)}, bf16[32,112,128]{2,1,0:T(8,128)(2,1)S(1)}, u32[]{:S(2)}, u32[]{:S(2)}) collective-permute-start(bf16[32,112,128]{2,1,0:T(8,128)(2,1)S(1)} %get-tuple-element.56), channel_id=1, source_target_pairs={{0,3},{1,0},{2,1},{3,2},{4,7},{5,4},{6,5},{7,6},{8,11},{9,8},{10,9... | collective-permute-start | bytes 2752520 | tf_op jit(solution)/shard_map/ppermute | solution.py:199
  74.4 0.1 collective-permute-start.20
  74.5 2.3 %collective-permute-start.21 = (bf16[16,112,128]{2,1,0:T(8,128)(2,1)S(1)}, bf16[16,112,128]{2,1,0:T(8,128)(2,1)S(1)}, u32[]{:S(2)}, u32[]{:S(2)}) collective-permute-start(bf16[16,112,128]{2,1,0:T(8,128)(2,1)S(1)} %get-tuple-element.60), channel_id=1, source_target_pairs={{0,128},{4,132},{8,136},{12,140},{16,144},{20,148},{24,152},{28,15... | collective-permute-start | bytes 1376264 | tf_op jit(solution)/shard_map/ppermute | solution.py:213
  76.8 1.2 %collective-permute-start.22 = (bf16[16,112,128]{2,1,0:T(8,128)(2,1)S(1)}, bf16[16,112,128]{2,1,0:T(8,128)(2,1)S(1)}, u32[]{:S(2)}, u32[]{:S(2)}) collective-permute-start(bf16[16,112,128]{2,1,0:T(8,128)(2,1)S(1)} %get-tuple-element.59), channel_id=1, source_target_pairs={{0,192},{4,196},{8,200},{12,204},{16,208},{20,212},{24,216},{28,22... | collective-permute-start | bytes 1376264 | tf_op jit(solution)/shard_map/ppermute | solution.py:213
  78.0 15.6 %collective-permute-done.16.refs_3_.refs_2_ = bf16[32,112,128]{2,1,0:T(8,128)(2,1)S(1)} collective-permute-done((bf16[32,112,128]{2,1,0:T(8,128)(2,1)S(1)}, bf16[32,112,128]{2,1,0:T(8,128)(2,1)S(1)}, u32[]{:S(2)}, u32[]{:S(2)}) %collective-permute-start.16) | collective-permute-done | bytes 917536 | tf_op jit(solution)/shard_map/ppermute | solution.py:199
  93.6 0.0 collective-permute-done.17.refs_4_.refs_3_
  93.6 1.0 collective-permute-start.18
  94.6 2.3 %collective-permute-start.19 = (bf16[8,112,128]{2,1,0:T(8,128)(2,1)S(1)}, bf16[8,112,128]{2,1,0:T(8,128)(2,1)S(1)}, u32[]{:S(2)}, u32[]{:S(2)}) collective-permute-start(bf16[8,112,128]{2,1,0:T(8,128)(2,1)S(1)} %slice.227), channel_id=1, source_target_pairs={{0,3},{1,0},{2,1},{3,2},{4,7},{5,4},{6,5},{7,6},{8,11},{9,8},{10,9... | collective-permute-start | bytes 688136 | tf_op jit(solution)/shard_map/ppermute | solution.py:199
  96.9 0.0 collective-permute-done.20.refs_1_
  96.9 0.0 collective-permute-done.21.refs_2_
  97.0 0.1 collective-permute-done.22.refs_3_
  97.1 1.9 %place.3.refs_5_ = bf16[7168,512]{1,0:T(8,128)(2,1)} custom-call(s32[84]{0:T(128)S(1)} %pad_add_fusion.tables, bf16[16,112,128]{2,1,0:T(8,128)(2,1)S(1)} %get-tuple-element.62.refs_0_, bf16[16,112,128]{2,1,0:T(8,128)(2,1)S(1)} %collective-permute-done.20.refs_1_, bf16[16,112,128]{2,1,0:T(8,128)(2,1)S(1)} %collective-permute-done.21.refs_2_, ...), custom_call_target="tpu_custom_call" | custom-call | bytes 3670016 | tf_op jit(solution)/shard_map/place/pallas_call | solution.py:149
  99.0 2.7 %place.4.refs_6_ = bf16[7168,512]{1,0:T(8,128)(2,1)} custom-call(s32[84]{0:T(128)S(1)} %pad_add_fusion.tables, bf16[32,112,128]{2,1,0:T(8,128)(2,1)S(1)} %bitcast.24, bf16[32,112,128]{2,1,0:T(8,128)(2,1)S(1)} %collective-permute-done.14.refs_1_, bf16[32,112,128]{2,1,0:T(8,128)(2,1)S(1)} %collective-permute-done.15.refs_2_, ...), custom_call_target="tpu_custom_call", output_to_operand_aliasing={{}: (6, {})} | custom-call | bytes 7340032 | tf_op jit(solution)/shard_map/place/pallas_call | solution.py:149
  101.7 0.0 collective-permute-done.19.refs_5_
  101.7 1.9 %place.5 = bf16[7168,512]{1,0:T(8,128)(2,1)} custom-call(s32[84]{0:T(128)S(1)} %pad_add_fusion.tables, bf16[8,112,128]{2,1,0:T(8,128)(2,1)S(1)} %collective-permute-done.8.refs_0_, bf16[8,112,128]{2,1,0:T(8,128)(2,1)S(1)} %collective-permute-done.9.refs_1_, ...), custom_call_target="tpu_custom_call", output_to_operand_aliasing={{}: (7, {})} | custom-call | bytes 3670016 | tf_op jit(solution)/shard_map/place/pallas_call | solution.py:149
  (34 shorter events, 0.5 us)
Async XLA Ops:
  0.0 3.3 %collective-permute-start = (bf16[4,112,512]{2,1,0:T(8,128)(2,1)}, bf16[4,112,512]{2,1,0:T(8,128)(2,1)S(1)}, u32[]{:S(2)}, u32[]{:S(2)}) collective-permute-start(bf16[4,112,512]{2,1,0:T(8,128)(2,1)} %refs_0_.1), channel_id=1, source_target_pairs={{0,4},{4,0},{8,12},{12,8},{16,20},{20,16},{24,28},{28,24},{32,36},... | collective-permute-start | bytes 1376264 | tf_op jit(solution)/shard_map/ppermute | solution.py:67
  0.0 3.3 %collective-permute-start.1 = (bf16[4,112,512]{2,1,0:T(8,128)(2,1)}, bf16[4,112,512]{2,1,0:T(8,128)(2,1)S(1)}, u32[]{:S(2)}, u32[]{:S(2)}) collective-permute-start(bf16[4,112,512]{2,1,0:T(8,128)(2,1)} %refs_1_.1), channel_id=1, source_target_pairs={{0,4},{4,0},{8,12},{12,8},{16,20},{20,16},{24,28},{28,24},{32,36},... | collective-permute-start | bytes 1376264 | tf_op jit(solution)/shard_map/ppermute | solution.py:68
  0.5 2.7 %collective-permute-start.2 = (f32[112]{0:T(128)}, f32[112]{0:T(128)S(1)}, u32[]{:S(2)}, u32[]{:S(2)}) collective-permute-start(f32[112]{0:T(128)} %param.8), channel_id=1, source_target_pairs={{0,4},{4,0},{8,12},{12,8},{16,20},{20,16},{24,28},{28,24},{32,36},... | collective-permute-start | bytes 1352 | tf_op jit(solution)/shard_map/ppermute | solution.py:69
  3.3 1.0 copy-start
  4.3 1.0 copy-start.1
  8.2 13.9 %collective-permute-start.3 = (bf16[8,112,128]{2,1,0:T(8,128)(2,1)S(1)}, bf16[8,112,128]{2,1,0:T(8,128)(2,1)S(1)}, u32[]{:S(2)}, u32[]{:S(2)}) collective-permute-start(bf16[8,112,128]{2,1,0:T(8,128)(2,1)S(1)} %pad_maximum_fusion.4), channel_id=1, source_target_pairs={{0,8},{4,12},{8,16},{12,20},{16,24},{20,28},{24,32},{28,36},{32,40... | collective-permute-start | bytes 688136 | tf_op jit(solution)/shard_map/ppermute | solution.py:195
  10.2 11.9 %collective-permute-start.4 = (bf16[8,112,128]{2,1,0:T(8,128)(2,1)S(1)}, bf16[8,112,128]{2,1,0:T(8,128)(2,1)S(1)}, u32[]{:S(2)}, u32[]{:S(2)}) collective-permute-start(bf16[8,112,128]{2,1,0:T(8,128)(2,1)S(1)} %pad_maximum_fusion.5), channel_id=1, source_target_pairs={{0,56},{4,60},{8,0},{12,4},{16,8},{20,12},{24,16},{28,20},{32,24},... | collective-permute-start | bytes 688136 | tf_op jit(solution)/shard_map/ppermute | solution.py:195
  10.3 37.0 %all-to-all-start = ((bf16[16,2,112,128]{3,2,1,0:T(8,128)(2,1)}), bf16[16,2,112,128]{3,2,1,0:T(8,128)(2,1)S(1)}, u32[]{:S(2)}, u32[]{:S(2)}) async-start(bf16[16,2,112,128]{3,2,1,0:T(8,128)(2,1)} %get-tuple-element.48), calls=%async_computation | async-start | bytes 1835008 | tf_op jit(solution)/shard_map/all_to_all | solution.py:202
  22.2 15.8 %collective-permute-start.11 = (bf16[16,112,128]{2,1,0:T(8,128)(2,1)S(1)}, bf16[16,112,128]{2,1,0:T(8,128)(2,1)S(1)}, u32[]{:S(2)}, u32[]{:S(2)}) collective-permute-start(bf16[16,112,128]{2,1,0:T(8,128)(2,1)S(1)} %pad_maximum_fusion.3), channel_id=1, source_target_pairs={{0,3},{1,0},{2,1},{3,2},{4,7},{5,4},{6,5},{7,6},{8,11},{9,8},{10,9... | collective-permute-start | bytes 1376264 | tf_op jit(solution)/shard_map/ppermute | solution.py:199
  25.3 12.7 %collective-permute-start.10 = (bf16[16,112,128]{2,1,0:T(8,128)(2,1)S(1)}, bf16[16,112,128]{2,1,0:T(8,128)(2,1)S(1)}, u32[]{:S(2)}, u32[]{:S(2)}) collective-permute-start(bf16[16,112,128]{2,1,0:T(8,128)(2,1)S(1)} %pad_maximum_fusion.3), channel_id=1, source_target_pairs={{0,1},{1,2},{2,3},{3,0},{4,5},{5,6},{6,7},{7,4},{8,9},{9,10},{10,1... | collective-permute-start | bytes 1376264 | tf_op jit(solution)/shard_map/ppermute | solution.py:199
  25.3 7.3 %collective-permute-start.5 = (bf16[2,2,112,128]{3,2,1,0:T(8,128)(2,1)S(1)}, bf16[2,2,112,128]{3,2,1,0:T(8,128)(2,1)S(1)}, u32[]{:S(2)}, u32[]{:S(2)}) collective-permute-start(bf16[2,2,112,128]{3,2,1,0:T(8,128)(2,1)S(1)} %get-tuple-element.43), channel_id=1, source_target_pairs={{0,64},{4,68},{8,72},{12,76},{16,80},{20,84},{24,88},{28,92},{32,9... | collective-permute-start | bytes 344072 | tf_op jit(solution)/shard_map/ppermute | solution.py:190
  26.8 14.6 %collective-permute-start.6 = (bf16[2,2,112,128]{3,2,1,0:T(8,128)(2,1)S(1)}, bf16[2,2,112,128]{3,2,1,0:T(8,128)(2,1)S(1)}, u32[]{:S(2)}, u32[]{:S(2)}) collective-permute-start(bf16[2,2,112,128]{3,2,1,0:T(8,128)(2,1)S(1)} %get-tuple-element.44), channel_id=1, source_target_pairs={{0,128},{4,132},{8,136},{12,140},{16,144},{20,148},{24,152},{28,15... | collective-permute-start | bytes 344072 | tf_op jit(solution)/shard_map/ppermute | solution.py:190
  29.4 12.0 %collective-permute-start.7 = (bf16[2,2,112,128]{3,2,1,0:T(8,128)(2,1)S(1)}, bf16[2,2,112,128]{3,2,1,0:T(8,128)(2,1)S(1)}, u32[]{:S(2)}, u32[]{:S(2)}) collective-permute-start(bf16[2,2,112,128]{3,2,1,0:T(8,128)(2,1)S(1)} %get-tuple-element.45), channel_id=1, source_target_pairs={{0,192},{4,196},{8,200},{12,204},{16,208},{20,212},{24,216},{28,22... | collective-permute-start | bytes 344072 | tf_op jit(solution)/shard_map/ppermute | solution.py:190
  38.1 7.3 %collective-permute-start.12 = (bf16[8,112,128]{2,1,0:T(8,128)(2,1)S(1)}, bf16[8,112,128]{2,1,0:T(8,128)(2,1)S(1)}, u32[]{:S(2)}, u32[]{:S(2)}) collective-permute-start(bf16[8,112,128]{2,1,0:T(8,128)(2,1)S(1)} %slice.222), channel_id=1, source_target_pairs={{0,1},{1,2},{2,3},{3,0},{4,5},{5,6},{6,7},{7,4},{8,9},{9,10},{10,1... | collective-permute-start | bytes 688136 | tf_op jit(solution)/shard_map/ppermute | solution.py:199
  38.2 7.2 %collective-permute-start.13 = (bf16[8,112,128]{2,1,0:T(8,128)(2,1)S(1)}, bf16[8,112,128]{2,1,0:T(8,128)(2,1)S(1)}, u32[]{:S(2)}, u32[]{:S(2)}) collective-permute-start(bf16[8,112,128]{2,1,0:T(8,128)(2,1)S(1)} %slice.223), channel_id=1, source_target_pairs={{0,3},{1,0},{2,1},{3,2},{4,7},{5,4},{6,5},{7,6},{8,11},{9,8},{10,9... | collective-permute-start | bytes 688136 | tf_op jit(solution)/shard_map/ppermute | solution.py:199
  47.3 23.4 %collective-permute-start.14 = (bf16[32,112,128]{2,1,0:T(8,128)(2,1)S(1)}, bf16[32,112,128]{2,1,0:T(8,128)(2,1)S(1)}, u32[]{:S(2)}, u32[]{:S(2)}) collective-permute-start(bf16[32,112,128]{2,1,0:T(8,128)(2,1)S(1)} %bitcast.22), channel_id=1, source_target_pairs={{0,1},{1,2},{2,3},{3,0},{4,5},{5,6},{6,7},{7,4},{8,9},{9,10},{10,1... | collective-permute-start | bytes 2752520 | tf_op jit(solution)/shard_map/ppermute | solution.py:199
  48.8 21.9 %collective-permute-start.15 = (bf16[32,112,128]{2,1,0:T(8,128)(2,1)S(1)}, bf16[32,112,128]{2,1,0:T(8,128)(2,1)S(1)}, u32[]{:S(2)}, u32[]{:S(2)}) collective-permute-start(bf16[32,112,128]{2,1,0:T(8,128)(2,1)S(1)} %bitcast.23), channel_id=1, source_target_pairs={{0,3},{1,0},{2,1},{3,2},{4,7},{5,4},{6,5},{7,6},{8,11},{9,8},{10,9... | collective-permute-start | bytes 2752520 | tf_op jit(solution)/shard_map/ppermute | solution.py:199
  50.6 20.2 %collective-permute-start.8 = (bf16[8,112,128]{2,1,0:T(8,128)(2,1)S(1)}, bf16[8,112,128]{2,1,0:T(8,128)(2,1)S(1)}, u32[]{:S(2)}, u32[]{:S(2)}) collective-permute-start(bf16[8,112,128]{2,1,0:T(8,128)(2,1)S(1)} %bitcast.26), channel_id=1, source_target_pairs={{0,24},{4,28},{8,32},{12,36},{16,40},{20,44},{24,48},{28,52},{32,5... | collective-permute-start | bytes 688136 | tf_op jit(solution)/shard_map/ppermute | solution.py:195
  52.9 17.9 %collective-permute-start.9 = (bf16[8,112,128]{2,1,0:T(8,128)(2,1)S(1)}, bf16[8,112,128]{2,1,0:T(8,128)(2,1)S(1)}, u32[]{:S(2)}, u32[]{:S(2)}) collective-permute-start(bf16[8,112,128]{2,1,0:T(8,128)(2,1)S(1)} %bitcast.25), channel_id=1, source_target_pairs={{0,40},{4,44},{8,48},{12,52},{16,56},{20,60},{24,0},{28,4},{32,8},... | collective-permute-start | bytes 688136 | tf_op jit(solution)/shard_map/ppermute | solution.py:195
  70.7 3.6 %copy-start.2 = (bf16[16,112,128]{2,1,0:T(8,128)(2,1)S(1)}, bf16[16,112,128]{2,1,0:T(8,128)(2,1)}, u32[]{:S(2)}) copy-start(bf16[16,112,128]{2,1,0:T(8,128)(2,1)} %get-tuple-element.81) | copy-start | bytes 1376260
  70.7 3.6 %copy-start.3 = (bf16[16,112,128]{2,1,0:T(8,128)(2,1)S(1)}, bf16[16,112,128]{2,1,0:T(8,128)(2,1)}, u32[]{:S(2)}) copy-start(bf16[16,112,128]{2,1,0:T(8,128)(2,1)} %get-tuple-element.82) | copy-start | bytes 1376260
  70.7 3.5 %copy-start.4 = (bf16[16,112,128]{2,1,0:T(8,128)(2,1)S(1)}, bf16[16,112,128]{2,1,0:T(8,128)(2,1)}, u32[]{:S(2)}) copy-start(bf16[16,112,128]{2,1,0:T(8,128)(2,1)} %get-tuple-element.83) | copy-start | bytes 1376260
  71.0 22.6 %collective-permute-start.16 = (bf16[32,112,128]{2,1,0:T(8,128)(2,1)S(1)}, bf16[32,112,128]{2,1,0:T(8,128)(2,1)S(1)}, u32[]{:S(2)}, u32[]{:S(2)}) collective-permute-start(bf16[32,112,128]{2,1,0:T(8,128)(2,1)S(1)} %get-tuple-element.55), channel_id=1, source_target_pairs={{0,1},{1,2},{2,3},{3,0},{4,5},{5,6},{6,7},{7,4},{8,9},{9,10},{10,1... | collective-permute-start | bytes 2752520 | tf_op jit(solution)/shard_map/ppermute | solution.py:199
  72.5 21.1 %collective-permute-start.17 = (bf16[32,112,128]{2,1,0:T(8,128)(2,1)S(1)}, bf16[32,112,128]{2,1,0:T(8,128)(2,1)S(1)}, u32[]{:S(2)}, u32[]{:S(2)}) collective-permute-start(bf16[32,112,128]{2,1,0:T(8,128)(2,1)S(1)} %get-tuple-element.56), channel_id=1, source_target_pairs={{0,3},{1,0},{2,1},{3,2},{4,7},{5,4},{6,5},{7,6},{8,11},{9,8},{10,9... | collective-permute-start | bytes 2752520 | tf_op jit(solution)/shard_map/ppermute | solution.py:199
  74.4 22.5 %collective-permute-start.20 = (bf16[16,112,128]{2,1,0:T(8,128)(2,1)S(1)}, bf16[16,112,128]{2,1,0:T(8,128)(2,1)S(1)}, u32[]{:S(2)}, u32[]{:S(2)}) collective-permute-start(bf16[16,112,128]{2,1,0:T(8,128)(2,1)S(1)} %get-tuple-element.61), channel_id=1, source_target_pairs={{0,64},{4,68},{8,72},{12,76},{16,80},{20,84},{24,88},{28,92},{32,9... | collective-permute-start | bytes 1376264 | tf_op jit(solution)/shard_map/ppermute | solution.py:213
  74.5 22.5 %collective-permute-start.21 = (bf16[16,112,128]{2,1,0:T(8,128)(2,1)S(1)}, bf16[16,112,128]{2,1,0:T(8,128)(2,1)S(1)}, u32[]{:S(2)}, u32[]{:S(2)}) collective-permute-start(bf16[16,112,128]{2,1,0:T(8,128)(2,1)S(1)} %get-tuple-element.60), channel_id=1, source_target_pairs={{0,128},{4,132},{8,136},{12,140},{16,144},{20,148},{24,152},{28,15... | collective-permute-start | bytes 1376264 | tf_op jit(solution)/shard_map/ppermute | solution.py:213
  76.8 20.3 %collective-permute-start.22 = (bf16[16,112,128]{2,1,0:T(8,128)(2,1)S(1)}, bf16[16,112,128]{2,1,0:T(8,128)(2,1)S(1)}, u32[]{:S(2)}, u32[]{:S(2)}) collective-permute-start(bf16[16,112,128]{2,1,0:T(8,128)(2,1)S(1)} %get-tuple-element.59), channel_id=1, source_target_pairs={{0,192},{4,196},{8,200},{12,204},{16,208},{20,212},{24,216},{28,22... | collective-permute-start | bytes 1376264 | tf_op jit(solution)/shard_map/ppermute | solution.py:213
  93.6 8.1 %collective-permute-start.18 = (bf16[8,112,128]{2,1,0:T(8,128)(2,1)S(1)}, bf16[8,112,128]{2,1,0:T(8,128)(2,1)S(1)}, u32[]{:S(2)}, u32[]{:S(2)}) collective-permute-start(bf16[8,112,128]{2,1,0:T(8,128)(2,1)S(1)} %slice.226), channel_id=1, source_target_pairs={{0,1},{1,2},{2,3},{3,0},{4,5},{5,6},{6,7},{7,4},{8,9},{9,10},{10,1... | collective-permute-start | bytes 688136 | tf_op jit(solution)/shard_map/ppermute | solution.py:199
  94.6 7.1 %collective-permute-start.19 = (bf16[8,112,128]{2,1,0:T(8,128)(2,1)S(1)}, bf16[8,112,128]{2,1,0:T(8,128)(2,1)S(1)}, u32[]{:S(2)}, u32[]{:S(2)}) collective-permute-start(bf16[8,112,128]{2,1,0:T(8,128)(2,1)S(1)} %slice.227), channel_id=1, source_target_pairs={{0,3},{1,0},{2,1},{3,2},{4,7},{5,4},{6,5},{7,6},{8,11},{9,8},{10,9... | collective-permute-start | bytes 688136 | tf_op jit(solution)/shard_map/ppermute | solution.py:199

commit v4 on v3

--- a/solution.py
+++ b/solution.py
@@ -22,32 +22,51 @@
     return lax.optimization_barrier((list(arrays), done))[0]
 
 
+def slot_owner(replica_slots, replica_count):
+    shape = (SLOTS,) + replica_slots.shape
+    slot, expert, place_in_list = (lax.broadcasted_iota(jnp.int32, shape, k) for k in range(3))
+    live = jnp.clip(replica_count[None, :, None] - place_in_list, 0, 1)
+    return jnp.sum(jnp.where(replica_slots[None] == slot, live * expert, 0), axis=(1, 2))
+
+
 def pick_matrix(core):
-    unit = lax.broadcasted_iota(jnp.int32, (1024, 512), 0)
-    column = lax.broadcasted_iota(jnp.int32, (1024, 512), 1)
-    lane = column % 128
-    wanted = (lane % 2) * 512 + 8 * (lane // 2) + 2 * (column // 128) + core
-    return (unit == wanted).astype(BF16)
-
-
-def prepare_kernel(tables, *refs):
-    sources, (gain, gain_far, matrix), outs = refs[:4], refs[4:7], refs[7:-2]
-    picked, owner = refs[-2:]
+    shape = (2, 512, 256)
+    half, row, column = (lax.broadcasted_iota(jnp.int32, shape, k) for k in range(3))
+    lane = column % 64
+    residue = (column // 64) ^ half
+    wanted = (lane % 2) * 256 + 8 * (lane // 2) + 2 * residue + core
+    return (row == wanted).astype(BF16)
+
+
+def fold_rows(weights, gain):
+    return (weights.astype(jnp.float32) * gain[None, :, None]).astype(BF16)
+
+
+def prepare_kernel(owner, *refs):
+    sources, (gain_far, matrix), outs, picked = refs[:4], refs[4:6], refs[6:-1], refs[-1]
     experts, rows = sources[0].shape[:2]
     x, z, _ = place()
-    for e in range(experts):
-        for k in range(4):
-            @pl.when(k < tables[16 + e])
-            def _():
-                owner[tables[4 * e + k]] = e
-    for side, scale in enumerate((gain, gain_far)):
+    low = lax.broadcasted_iota(jnp.int32, (rows, 128), 1) < 64
+    for side in range(2):
         gate, up = (ref[...].reshape(experts * rows, 512) for ref in sources[2 * side : 2 * side + 2])
-        got = jnp.dot(gate, matrix[:512, :], preferred_element_type=jnp.float32)
-        got += jnp.dot(up, matrix[512:, :], preferred_element_type=jnp.float32)
+        halves = []
+        for h in range(2):
+            got = jnp.dot(
+                gate[:, 256 * h : 256 * h + 256], matrix[h, :256, :], preferred_element_type=jnp.float32
+            )
+            halves.append(got + jnp.dot(
+                up[:, 256 * h : 256 * h + 256], matrix[h, 256:, :], preferred_element_type=jnp.float32
+            ))
         for e in range(experts):
-            part = (got[e * rows : (e + 1) * rows] * scale[...]).astype(BF16)
-            for zl in range(4):
-                picked[e * 4 + zl, side] = part[:, zl * 128 : (zl + 1) * 128]
+            for pair in range(2):
+                first, second = (
+                    half[e * rows : (e + 1) * rows, pair * 128 : pair * 128 + 128] for half in halves
+                )
+                if side:
+                    first, second = first * gain_far[...], second * gain_far[...]
+                picked[e * 4 + 2 * pair, side] = jnp.where(low, first, second).astype(BF16)
+                other = pltpu.roll(jnp.where(low, second, first), 64, 1)
+                picked[e * 4 + 2 * pair + 1, side] = other.astype(BF16)
     for g, group in enumerate(GROUPS):
         for k, dz in enumerate(group):
             zt = (z + dz) % NZ
@@ -61,7 +80,7 @@
             outs[-1][xt * (NZ // 2) + k] = picked[owner[xt * 2 + zt // 4] * 4 + zt % 4]
 
 
-def prepare(gate, up, gain, matrix, tables):
+def prepare(gate, up, gain, matrix, owner):
     rows = gate.shape[1]
     flip = [(i, i ^ 1) for i in range(2 * NX * NZ)]
     gate_far = lax.ppermute(gate, "fsdp", flip)
@@ -75,17 +94,15 @@
     outs = pl.pallas_call(
         prepare_kernel,
         out_shape=shapes,
-        in_specs=[smem] + [vmem] * 7,
+        in_specs=[smem] + [vmem] * 6,
         out_specs=[vmem] * len(shapes),
         scratch_shapes=[
             pltpu.VMEM((16, 2, rows, 128), BF16),
-            pltpu.SMEM((SLOTS,), jnp.int32),
         ],
         compiler_params=pltpu.CompilerParams(vmem_limit_bytes=16 * 1024 * 1024),
         name="prepare",
     )(
-        tables, gate, up, gate_far, up_far,
-        gain.reshape(rows, 1), gain_far.reshape(rows, 1), matrix,
+        owner, fold_rows(gate, gain), fold_rows(up, gain), gate_far, up_far, gain_far.reshape(rows, 1), matrix,
     )
     return [outs[g * NX : (g + 1) * NX] for g in range(len(GROUPS))], outs[-1]
 
@@ -117,7 +134,7 @@
     return [(array, index) for index in range(start, stop)]
 
 
-def place_kernel(blocks, arrays, tables, *refs):
+def place_kernel(blocks, arrays, matching, *refs):
     held = refs[:arrays]
     out, built, sems = refs[-3:]
     rows = built.shape[1]
@@ -132,7 +149,7 @@
             source = xs * NZ + (2 * dz + z % 2)
         else:
             source = (x - dx) % NX * NZ + (z - dz) % NZ
-        block = tables[20 + source * 2 + (core ^ side)]
+        block = matching[source * 2 + (core ^ side)]
         row = pl.multiple_of(block * rows, 16)
         save = pltpu.make_async_copy(built.at[at], out.at[pl.ds(row, rows)], sems.at[at])
         save.start()
@@ -141,10 +158,10 @@
         save.wait()
 
 
-def place_blocks(out, tables, devices, arrays, blocks):
+def place_blocks(out, matching, devices, arrays, blocks):
     rows = arrays[0].shape[1]
     vmem, anywhere = pl.BlockSpec(memory_space=pltpu.VMEM), pl.BlockSpec(memory_space=pl.ANY)
-    args = [tables, *arrays] + ([] if out is None else [out])
+    args = [matching, *arrays] + ([] if out is None else [out])
     total = len(blocks) * rows * 512 * 2
     return pl.pallas_call(
         functools.partial(place_kernel, blocks, len(arrays)),
@@ -168,8 +185,8 @@
     rows = gate.shape[1]
     _, _, core = place()
     matrix = pick_matrix(core)
-    tables = jnp.concatenate([replica_slots.reshape(16), replica_count, matching])
-    parts, even = prepare(gate, up, norm_gain, matrix, tables)
+    owner = slot_owner(replica_slots, replica_count)
+    parts, even = prepare(gate, up, norm_gain, matrix, owner)
 
     def along_x(dx):
         return [(i, ((i // 16 + dx) % NX) * 16 + i % 16) for i in range(devices)]
@@ -218,18 +235,18 @@
         (dz, side, None, dx, tuple((dx, step * 4 + 2 * k + side) for step in range(NY)))
         for dx in range(NX) for k, dz in enumerate(GROUPS[0]) for side in range(2)
     ]
-    out = place_blocks(None, tables, devices, bundles, late)
     evens = [
         (at // 2 % 4, at % 2, at // 8, None, ((0, at), (2, at), (3, 16 + at) if at < 16 else (4, at), (1, at)))
         for at in range(32)
     ]
-    out = place_blocks(out, tables, devices, [own, le, re, l3, r3], evens)
+    out = place_blocks(None, matching, devices, [own, le, re, l3, r3], evens)
+    out = place_blocks(out, matching, devices, bundles, late)
     odds = [
         (GROUPS[1][at // 8], at % 2, None, at % 8 // 2,
          ((at // 8, at % 8), (3, at), (4, at) if at < 8 else (5, at - 8), (2, at)))
         for at in range(16)
     ]
-    out = place_blocks(out, tables, devices, [*own3, l3, r3, l4, r4], odds)
+    out = place_blocks(out, matching, devices, [*own3, l3, r3, l4, r4], odds)
     return out[None]
 
 

time: 104 us -> 101 us (0.971)
  waiting for transfers between devices: 40.1 us -> 37.2 us
  local copies, waits for them, and re-layouts: 7.37 us -> 5.73 us
  other arithmetic: 1.45 us -> 2.81 us
    ppermute x5, waiting for transfers between devices: 37.8 us -> 32.2 us  [cross_y(): lax.ppermute(pair[0], 'rep', along_y(1))]
    ppermute x5, starting transfers between devices: 4.15 us -> 7.51 us  [cross_y(): lax.ppermute(pair[0], 'rep', along_y(1))]
    ppermute x5, starting transfers between devices: 12.1 us -> 8.98 us  [cross_y(): lax.ppermute(pair[1], 'rep', along_y(-1))]
    all_to_all x1, waiting for transfers between devices: 1.91 us -> 4.23 us  [local(): lax.all_to_all(even, 'fsdp', 0, 0, tiled=True, axis_index_groups=same_par...]
    reshape x2 -> x0, local copies, waits for them, and re-layouts: 1.52 us -> none  [the longest x1 0.77 us: local(): replica_slots.reshape(16)]
    convert_element_type x1 -> x2, other arithmetic: 0.37 us -> 1.7 us  [the longest x1 1.52 us: fold_rows(): return (weights.astype(jnp.float32) * gain[None, :, None]).astype(BF16)]
    unnamed x17 -> x9, local copies, waits for them, and re-layouts: 5.5 us -> 4.74 us
  transfers between devices with their start and end apart: 24 -> 24, of which waited for: 7 -> 7; matrix products, arithmetic and copies ran while one was open for 6% -> 8% of each run, Pallas kernels for 4% -> 5%
where the time goes in v4:
time: 101 us
  starting transfers between devices  46.1 us (46%)
  waiting for transfers between devices  37.2 us (37%)
  Pallas kernels  8.89 us (9%)
  local copies, waits for them, and re-layouts  5.73 us (6%)
  other arithmetic  2.81 us (3%)
    ppermute x5, waiting for transfers between devices, cross_y(): lax.ppermute(pair[0], 'rep', along_y(1))  32.2 us
    all_to_all x1, starting transfers between devices, local(): lax.all_to_all(even, 'fsdp', 0, 0, tiled=True, axis_index_groups=same_par...  11.9 us
    ppermute x5, starting transfers between devices, cross_y(): lax.ppermute(pair[1], 'rep', along_y(-1))  8.98 us
    ppermute x5, starting transfers between devices, cross_y(): lax.ppermute(pair[0], 'rep', along_y(1))  7.51 us
    ppermute x4, starting transfers between devices, cross_z(): return [lax.ppermute(p, 'fsdp', along_z(dz)) for dz, p in zip(dzs, pieces)]  7.4 us
    pallas_call x3, Pallas kernels, place_blocks(): pl.pallas_call(functools.partial(place_kernel, blocks, len(arrays)), out_...  6.57 us
    ppermute x3, starting transfers between devices, cross_x(): lax.ppermute(pieces[dx], 'fsdp', along_x(dx))  5.6 us
    unnamed x9, local copies, waits for them, and re-layouts  4.74 us
  transfers between devices with their start and end apart: 24, of which 7 were waited for; matrix products, arithmetic and copies ran while one was open for 8% of the time, Pallas kernels for 5%

profile of v4, /device:TPU:64, one launch (start us, length us, event | category | flops | bytes accessed | tf_op | source)
XLA Modules:
  0.0 101.2 jit_solution(16704100396801122665)
XLA Ops:
  0.0 0.0 collective-permute-start
  0.0 0.5 collective-permute-start.1
  0.5 0.0 collective-permute-start.2
  0.5 1.5 %multiply_convert_fusion = (bf16[4,112,512]{2,1,0:T(8,128)(2,1)S(1)}, bf16[4,112,512]{2,1,0:T(8,128)(2,1)S(1)}) fusion(bf16[4,112,512]{2,1,0:T(8,128)(2,1)} %param.7, f32[112]{0:T(128)} %param.8, bf16[4,112,512]{2,1,0:T(8,128)(2,1)} %param.6), kind=kLoop, calls=%fused_computation.22 | loop fusion | flops 1376256 | bytes 1835456 | tf_op jit(solution)/shard_map/convert_element_type | solution.py:42
  2.1 0.2 fusion.10.refs_5_
  2.3 0.8 select_reduce_fusion.owner
  3.1 0.0 collective-permute-done.2
  3.1 0.1 copy.10.refs_4_
  3.2 0.0 collective-permute-done.refs_2_
  3.2 0.0 collective-permute-done.1.refs_3_
  3.2 2.3 %prepare.1 = (bf16[2,2,112,128]{3,2,1,0:T(8,128)(2,1)S(1)}, bf16[2,2,112,128]{3,2,1,0:T(8,128)(2,1)S(1)}, bf16[2,2,112,128]{3,2,1,0:T(8,128)(2,1)S(1)}, bf16[2,2...) custom-call(s32[8]{0:T(128)S(1)} %select_reduce_fusion.owner, ...), custom_call_target="tpu_custom_call" | custom-call | tf_op jit(solution)/shard_map/prepare/pallas_call | solution.py:94
  5.7 2.0 %collective-permute-start.3 = (bf16[8,112,128]{2,1,0:T(8,128)(2,1)S(1)}, bf16[8,112,128]{2,1,0:T(8,128)(2,1)S(1)}, u32[]{:S(2)}, u32[]{:S(2)}) collective-permute-start(bf16[8,112,128]{2,1,0:T(8,128)(2,1)S(1)} %pad_maximum_fusion.4), channel_id=1, source_target_pairs={{0,8},{4,12},{8,16},{12,20},{16,24},{20,28},{24,32},{28,36},{32,40... | collective-permute-start | bytes 688136 | tf_op jit(solution)/shard_map/ppermute | solution.py:212
  7.6 0.1 collective-permute-start.4
  7.8 11.9 %all-to-all-start = ((bf16[16,2,112,128]{3,2,1,0:T(8,128)(2,1)}), bf16[16,2,112,128]{3,2,1,0:T(8,128)(2,1)S(1)}, u32[]{:S(2)}, u32[]{:S(2)}) async-start(bf16[16,2,112,128]{3,2,1,0:T(8,128)(2,1)} %get-tuple-element.48), calls=%async_computation | async-start | bytes 1835008 | tf_op jit(solution)/shard_map/all_to_all | solution.py:219
  19.7 0.0 collective-permute-done.3
  19.7 0.0 collective-permute-done.4
  19.8 1.7 %collective-permute-start.10 = (bf16[16,112,128]{2,1,0:T(8,128)(2,1)S(1)}, bf16[16,112,128]{2,1,0:T(8,128)(2,1)S(1)}, u32[]{:S(2)}, u32[]{:S(2)}) collective-permute-start(bf16[16,112,128]{2,1,0:T(8,128)(2,1)S(1)} %pad_maximum_fusion.3), channel_id=1, source_target_pairs={{0,1},{1,2},{2,3},{3,0},{4,5},{5,6},{6,7},{7,4},{8,9},{9,10},{10,1... | collective-permute-start | bytes 1376264 | tf_op jit(solution)/shard_map/ppermute | solution.py:216
  21.4 1.7 %collective-permute-start.11 = (bf16[16,112,128]{2,1,0:T(8,128)(2,1)S(1)}, bf16[16,112,128]{2,1,0:T(8,128)(2,1)S(1)}, u32[]{:S(2)}, u32[]{:S(2)}) collective-permute-start(bf16[16,112,128]{2,1,0:T(8,128)(2,1)S(1)} %pad_maximum_fusion.3), channel_id=1, source_target_pairs={{0,3},{1,0},{2,1},{3,2},{4,7},{5,4},{6,5},{7,6},{8,11},{9,8},{10,9... | collective-permute-start | bytes 1376264 | tf_op jit(solution)/shard_map/ppermute | solution.py:216
  23.1 1.5 %collective-permute-start.5 = (bf16[2,2,112,128]{3,2,1,0:T(8,128)(2,1)S(1)}, bf16[2,2,112,128]{3,2,1,0:T(8,128)(2,1)S(1)}, u32[]{:S(2)}, u32[]{:S(2)}) collective-permute-start(bf16[2,2,112,128]{3,2,1,0:T(8,128)(2,1)S(1)} %get-tuple-element.43), channel_id=1, source_target_pairs={{0,64},{4,68},{8,72},{12,76},{16,80},{20,84},{24,88},{28,92},{32,9... | collective-permute-start | bytes 344072 | tf_op jit(solution)/shard_map/ppermute | solution.py:207
  24.5 2.7 %collective-permute-start.6 = (bf16[2,2,112,128]{3,2,1,0:T(8,128)(2,1)S(1)}, bf16[2,2,112,128]{3,2,1,0:T(8,128)(2,1)S(1)}, u32[]{:S(2)}, u32[]{:S(2)}) collective-permute-start(bf16[2,2,112,128]{3,2,1,0:T(8,128)(2,1)S(1)} %get-tuple-element.44), channel_id=1, source_target_pairs={{0,128},{4,132},{8,136},{12,140},{16,144},{20,148},{24,152},{28,15... | collective-permute-start | bytes 344072 | tf_op jit(solution)/shard_map/ppermute | solution.py:207
  27.2 1.5 %collective-permute-start.7 = (bf16[2,2,112,128]{3,2,1,0:T(8,128)(2,1)S(1)}, bf16[2,2,112,128]{3,2,1,0:T(8,128)(2,1)S(1)}, u32[]{:S(2)}, u32[]{:S(2)}) collective-permute-start(bf16[2,2,112,128]{3,2,1,0:T(8,128)(2,1)S(1)} %get-tuple-element.45), channel_id=1, source_target_pairs={{0,192},{4,196},{8,200},{12,204},{16,208},{20,212},{24,216},{28,22... | collective-permute-start | bytes 344072 | tf_op jit(solution)/shard_map/ppermute | solution.py:207
  28.7 0.7 constant_dynamic-update-slice_fusion.31
  29.3 0.7 constant_dynamic-update-slice_fusion.30
  30.0 0.3 collective-permute-done.5
  30.4 2.6 %collective-permute-done.10 = bf16[16,112,128]{2,1,0:T(8,128)(2,1)S(1)} collective-permute-done((bf16[16,112,128]{2,1,0:T(8,128)(2,1)S(1)}, bf16[16,112,128]{2,1,0:T(8,128)(2,1)S(1)}, u32[]{:S(2)}, u32[]{:S(2)}) %collective-permute-start.10) | collective-permute-done | bytes 458784 | tf_op jit(solution)/shard_map/ppermute | solution.py:216
  32.9 0.0 collective-permute-done.11
  33.0 1.6 %collective-permute-start.12 = (bf16[8,112,128]{2,1,0:T(8,128)(2,1)S(1)}, bf16[8,112,128]{2,1,0:T(8,128)(2,1)S(1)}, u32[]{:S(2)}, u32[]{:S(2)}) collective-permute-start(bf16[8,112,128]{2,1,0:T(8,128)(2,1)S(1)} %slice.222), channel_id=1, source_target_pairs={{0,1},{1,2},{2,3},{3,0},{4,5},{5,6},{6,7},{7,4},{8,9},{9,10},{10,1... | collective-permute-start | bytes 688136 | tf_op jit(solution)/shard_map/ppermute | solution.py:216
  34.6 1.7 %collective-permute-start.13 = (bf16[8,112,128]{2,1,0:T(8,128)(2,1)S(1)}, bf16[8,112,128]{2,1,0:T(8,128)(2,1)S(1)}, u32[]{:S(2)}, u32[]{:S(2)}) collective-permute-start(bf16[8,112,128]{2,1,0:T(8,128)(2,1)S(1)} %slice.223), channel_id=1, source_target_pairs={{0,3},{1,0},{2,1},{3,2},{4,7},{5,4},{6,5},{7,6},{8,11},{9,8},{10,9... | collective-permute-start | bytes 688136 | tf_op jit(solution)/shard_map/ppermute | solution.py:216
  36.3 0.0 collective-permute-done.6
  36.3 0.0 collective-permute-done.7
  36.3 4.0 %collective-permute-done.12 = bf16[8,112,128]{2,1,0:T(8,128)(2,1)S(1)} collective-permute-done((bf16[8,112,128]{2,1,0:T(8,128)(2,1)S(1)}, bf16[8,112,128]{2,1,0:T(8,128)(2,1)S(1)}, u32[]{:S(2)}, u32[]{:S(2)}) %collective-permute-start.12) | collective-permute-done | bytes 229408 | tf_op jit(solution)/shard_map/ppermute | solution.py:216
  40.3 0.3 collective-permute-done.13
  40.6 4.2 %all-to-all-done = bf16[16,2,112,128]{3,2,1,0:T(8,128)(2,1)S(1)} async-done(((bf16[16,2,112,128]{3,2,1,0:T(8,128)(2,1)}), bf16[16,2,112,128]{3,2,1,0:T(8,128)(2,1)S(1)}, u32[]{:S(2)}, u32[]{:S(2)}) %all-to-all-start) | async-done | bytes 917536 | tf_op jit(solution)/shard_map/all_to_all | solution.py:219
  44.9 1.5 %collective-permute-start.14 = (bf16[32,112,128]{2,1,0:T(8,128)(2,1)S(1)}, bf16[32,112,128]{2,1,0:T(8,128)(2,1)S(1)}, u32[]{:S(2)}, u32[]{:S(2)}) collective-permute-start(bf16[32,112,128]{2,1,0:T(8,128)(2,1)S(1)} %bitcast.21), channel_id=1, source_target_pairs={{0,1},{1,2},{2,3},{3,0},{4,5},{5,6},{6,7},{7,4},{8,9},{9,10},{10,1... | collective-permute-start | bytes 2752520 | tf_op jit(solution)/shard_map/ppermute | solution.py:216
  46.4 1.7 %collective-permute-start.15 = (bf16[32,112,128]{2,1,0:T(8,128)(2,1)S(1)}, bf16[32,112,128]{2,1,0:T(8,128)(2,1)S(1)}, u32[]{:S(2)}, u32[]{:S(2)}) collective-permute-start(bf16[32,112,128]{2,1,0:T(8,128)(2,1)S(1)} %bitcast.22), channel_id=1, source_target_pairs={{0,3},{1,0},{2,1},{3,2},{4,7},{5,4},{6,5},{7,6},{8,11},{9,8},{10,9... | collective-permute-start | bytes 2752520 | tf_op jit(solution)/shard_map/ppermute | solution.py:216
  48.2 2.3 %collective-permute-start.8 = (bf16[8,112,128]{2,1,0:T(8,128)(2,1)S(1)}, bf16[8,112,128]{2,1,0:T(8,128)(2,1)S(1)}, u32[]{:S(2)}, u32[]{:S(2)}) collective-permute-start(bf16[8,112,128]{2,1,0:T(8,128)(2,1)S(1)} %bitcast.25), channel_id=1, source_target_pairs={{0,24},{4,28},{8,32},{12,36},{16,40},{20,44},{24,48},{28,52},{32,5... | collective-permute-start | bytes 688136 | tf_op jit(solution)/shard_map/ppermute | solution.py:212
  50.5 3.0 %collective-permute-start.9 = (bf16[8,112,128]{2,1,0:T(8,128)(2,1)S(1)}, bf16[8,112,128]{2,1,0:T(8,128)(2,1)S(1)}, u32[]{:S(2)}, u32[]{:S(2)}) collective-permute-start(bf16[8,112,128]{2,1,0:T(8,128)(2,1)S(1)} %bitcast.24), channel_id=1, source_target_pairs={{0,40},{4,44},{8,48},{12,52},{16,56},{20,60},{24,0},{28,4},{32,8},... | collective-permute-start | bytes 688136 | tf_op jit(solution)/shard_map/ppermute | solution.py:212
  53.5 0.7 constant_dynamic-update-slice_fusion.29
  54.2 0.7 constant_dynamic-update-slice_fusion.28
  54.8 0.7 constant_dynamic-update-slice_fusion.27
  55.5 12.7 %collective-permute-done.14.refs_1_ = bf16[32,112,128]{2,1,0:T(8,128)(2,1)S(1)} collective-permute-done((bf16[32,112,128]{2,1,0:T(8,128)(2,1)S(1)}, bf16[32,112,128]{2,1,0:T(8,128)(2,1)S(1)}, u32[]{:S(2)}, u32[]{:S(2)}) %collective-permute-start.14) | collective-permute-done | bytes 917536 | tf_op jit(solution)/shard_map/ppermute | solution.py:216
  68.3 0.0 collective-permute-done.15.refs_2_
  68.3 0.0 collective-permute-done.8.refs_0_
  68.3 0.0 collective-permute-done.9.refs_1_
  68.3 0.1 pad_maximum_fusion.2
  68.5 1.6 %collective-permute-start.16 = (bf16[32,112,128]{2,1,0:T(8,128)(2,1)S(1)}, bf16[32,112,128]{2,1,0:T(8,128)(2,1)S(1)}, u32[]{:S(2)}, u32[]{:S(2)}) collective-permute-start(bf16[32,112,128]{2,1,0:T(8,128)(2,1)S(1)} %get-tuple-element.55), channel_id=1, source_target_pairs={{0,1},{1,2},{2,3},{3,0},{4,5},{5,6},{6,7},{7,4},{8,9},{9,10},{10,1... | collective-permute-start | bytes 2752520 | tf_op jit(solution)/shard_map/ppermute | solution.py:216
  70.1 1.7 %collective-permute-start.17 = (bf16[32,112,128]{2,1,0:T(8,128)(2,1)S(1)}, bf16[32,112,128]{2,1,0:T(8,128)(2,1)S(1)}, u32[]{:S(2)}, u32[]{:S(2)}) collective-permute-start(bf16[32,112,128]{2,1,0:T(8,128)(2,1)S(1)} %get-tuple-element.56), channel_id=1, source_target_pairs={{0,3},{1,0},{2,1},{3,2},{4,7},{5,4},{6,5},{7,6},{8,11},{9,8},{10,9... | collective-permute-start | bytes 2752520 | tf_op jit(solution)/shard_map/ppermute | solution.py:216
  71.8 0.7 constant_dynamic-update-slice_fusion.26
  72.5 0.7 constant_dynamic-update-slice_fusion.25
  73.1 0.7 constant_dynamic-update-slice_fusion.24
  73.8 0.1 collective-permute-start.20
  73.9 2.9 %collective-permute-start.21 = (bf16[16,112,128]{2,1,0:T(8,128)(2,1)}, bf16[16,112,128]{2,1,0:T(8,128)(2,1)S(1)}, u32[]{:S(2)}, u32[]{:S(2)}) collective-permute-start(bf16[16,112,128]{2,1,0:T(8,128)(2,1)} %get-tuple-element.60), channel_id=1, source_target_pairs={{0,128},{4,132},{8,136},{12,140},{16,144},{20,148},{24,152},{28,15... | collective-permute-start | bytes 1376264 | tf_op jit(solution)/shard_map/ppermute | solution.py:230
  76.9 1.2 %collective-permute-start.22 = (bf16[16,112,128]{2,1,0:T(8,128)(2,1)}, bf16[16,112,128]{2,1,0:T(8,128)(2,1)S(1)}, u32[]{:S(2)}, u32[]{:S(2)}) collective-permute-start(bf16[16,112,128]{2,1,0:T(8,128)(2,1)} %get-tuple-element.59), channel_id=1, source_target_pairs={{0,192},{4,196},{8,200},{12,204},{16,208},{20,212},{24,216},{28,22... | collective-permute-start | bytes 1376264 | tf_op jit(solution)/shard_map/ppermute | solution.py:230
  78.0 13.0 %collective-permute-done.16.refs_3_.refs_2_ = bf16[32,112,128]{2,1,0:T(8,128)(2,1)S(1)} collective-permute-done((bf16[32,112,128]{2,1,0:T(8,128)(2,1)S(1)}, bf16[32,112,128]{2,1,0:T(8,128)(2,1)S(1)}, u32[]{:S(2)}, u32[]{:S(2)}) %collective-permute-start.16) | collective-permute-done | bytes 917536 | tf_op jit(solution)/shard_map/ppermute | solution.py:216
  91.0 0.0 collective-permute-done.17.refs_4_.refs_3_
  91.1 1.1 %collective-permute-start.18 = (bf16[8,112,128]{2,1,0:T(8,128)(2,1)S(1)}, bf16[8,112,128]{2,1,0:T(8,128)(2,1)S(1)}, u32[]{:S(2)}, u32[]{:S(2)}) collective-permute-start(bf16[8,112,128]{2,1,0:T(8,128)(2,1)S(1)} %slice.226), channel_id=1, source_target_pairs={{0,1},{1,2},{2,3},{3,0},{4,5},{5,6},{6,7},{7,4},{8,9},{9,10},{10,1... | collective-permute-start | bytes 688136 | tf_op jit(solution)/shard_map/ppermute | solution.py:216
  92.1 2.3 %collective-permute-start.19 = (bf16[8,112,128]{2,1,0:T(8,128)(2,1)S(1)}, bf16[8,112,128]{2,1,0:T(8,128)(2,1)S(1)}, u32[]{:S(2)}, u32[]{:S(2)}) collective-permute-start(bf16[8,112,128]{2,1,0:T(8,128)(2,1)S(1)} %slice.227), channel_id=1, source_target_pairs={{0,3},{1,0},{2,1},{3,2},{4,7},{5,4},{6,5},{7,6},{8,11},{9,8},{10,9... | collective-permute-start | bytes 688136 | tf_op jit(solution)/shard_map/ppermute | solution.py:216
  94.4 2.7 %place.3.refs_4_ = bf16[7168,512]{1,0:T(8,128)(2,1)} custom-call(s32[64]{0:T(128)S(1)} %copy-done, bf16[32,112,128]{2,1,0:T(8,128)(2,1)S(1)} %bitcast.23, bf16[32,112,128]{2,1,0:T(8,128)(2,1)S(1)} %collective-permute-done.14.refs_1_, bf16[32,112,128]{2,1,0:T(8,128)(2,1)S(1)} %collective-permute-done.15.refs_2_, ...), custom_call_target="tpu_custom_call" | custom-call | bytes 7340032 | tf_op jit(solution)/shard_map/place/pallas_call | solution.py:166
  97.1 0.0 collective-permute-done.20.refs_1_
  97.1 0.0 collective-permute-done.21.refs_2_
  97.1 0.0 collective-permute-done.22.refs_3_
  97.1 1.9 %place.4.refs_6_ = bf16[7168,512]{1,0:T(8,128)(2,1)} custom-call(s32[64]{0:T(128)S(1)} %copy-done, bf16[16,112,128]{2,1,0:T(8,128)(2,1)S(1)} %get-tuple-element.62.refs_0_, bf16[16,112,128]{2,1,0:T(8,128)(2,1)S(1)} %collective-permute-done.20.refs_1_, bf16[16,112,128]{2,1,0:T(8,128)(2,1)S(1)} %collective-permute-done.21.refs_2_, ...), custom_call_target="tpu_custom_call", output_to_operand_aliasing={{}: (5, {})} | custom-call | bytes 3670016 | tf_op jit(solution)/shard_map/place/pallas_call | solution.py:166
  99.1 0.0 collective-permute-done.18.refs_4_
  99.1 1.9 %place.5 = bf16[7168,512]{1,0:T(8,128)(2,1)} custom-call(s32[64]{0:T(128)S(1)} %copy-done, bf16[8,112,128]{2,1,0:T(8,128)(2,1)S(1)} %collective-permute-done.8.refs_0_, bf16[8,112,128]{2,1,0:T(8,128)(2,1)S(1)} %collective-permute-done.9.refs_1_, bf16[32,112,128]{2,1,0:T(8,128)(2,1)S(1)} %collective-permute-done.16.refs_3_.refs_2_, ...), custom_call_target="tpu_custom_call", output_to_operand_aliasing={{}: (7, {})} | custom-call | bytes 3670016 | tf_op jit(solution)/shard_map/place/pallas_call | solution.py:166
  (25 shorter events, 0.4 us)
Async XLA Ops:
  0.0 3.2 %collective-permute-start = (bf16[4,112,512]{2,1,0:T(8,128)(2,1)}, bf16[4,112,512]{2,1,0:T(8,128)(2,1)S(1)}, u32[]{:S(2)}, u32[]{:S(2)}) collective-permute-start(bf16[4,112,512]{2,1,0:T(8,128)(2,1)} %param.6), channel_id=1, source_target_pairs={{0,4},{4,0},{8,12},{12,8},{16,20},{20,16},{24,28},{28,24},{32,36},... | collective-permute-start | bytes 1376264 | tf_op jit(solution)/shard_map/ppermute | solution.py:86
  0.0 3.2 %collective-permute-start.1 = (bf16[4,112,512]{2,1,0:T(8,128)(2,1)}, bf16[4,112,512]{2,1,0:T(8,128)(2,1)S(1)}, u32[]{:S(2)}, u32[]{:S(2)}) collective-permute-start(bf16[4,112,512]{2,1,0:T(8,128)(2,1)} %param.7), channel_id=1, source_target_pairs={{0,4},{4,0},{8,12},{12,8},{16,20},{20,16},{24,28},{28,24},{32,36},... | collective-permute-start | bytes 1376264 | tf_op jit(solution)/shard_map/ppermute | solution.py:87
  0.5 2.5 %collective-permute-start.2 = (f32[112]{0:T(128)}, f32[112]{0:T(128)S(1)}, u32[]{:S(2)}, u32[]{:S(2)}) collective-permute-start(f32[112]{0:T(128)} %param.8), channel_id=1, source_target_pairs={{0,4},{4,0},{8,12},{12,8},{16,20},{20,16},{24,28},{28,24},{32,36},... | collective-permute-start | bytes 1352 | tf_op jit(solution)/shard_map/ppermute | solution.py:88
  5.7 14.0 %collective-permute-start.3 = (bf16[8,112,128]{2,1,0:T(8,128)(2,1)S(1)}, bf16[8,112,128]{2,1,0:T(8,128)(2,1)S(1)}, u32[]{:S(2)}, u32[]{:S(2)}) collective-permute-start(bf16[8,112,128]{2,1,0:T(8,128)(2,1)S(1)} %pad_maximum_fusion.4), channel_id=1, source_target_pairs={{0,8},{4,12},{8,16},{12,20},{16,24},{20,28},{24,32},{28,36},{32,40... | collective-permute-start | bytes 688136 | tf_op jit(solution)/shard_map/ppermute | solution.py:212
  7.6 12.1 %collective-permute-start.4 = (bf16[8,112,128]{2,1,0:T(8,128)(2,1)S(1)}, bf16[8,112,128]{2,1,0:T(8,128)(2,1)S(1)}, u32[]{:S(2)}, u32[]{:S(2)}) collective-permute-start(bf16[8,112,128]{2,1,0:T(8,128)(2,1)S(1)} %pad_maximum_fusion.5), channel_id=1, source_target_pairs={{0,56},{4,60},{8,0},{12,4},{16,8},{20,12},{24,16},{28,20},{32,24},... | collective-permute-start | bytes 688136 | tf_op jit(solution)/shard_map/ppermute | solution.py:212
  7.8 86.6 %copy-start = (s32[64]{0:T(128)S(1)}, s32[64]{0:T(128)}, u32[]{:S(2)}) copy-start(s32[64]{0:T(128)} %matching.5) | copy-start | bytes 772
  7.8 37.1 %all-to-all-start = ((bf16[16,2,112,128]{3,2,1,0:T(8,128)(2,1)}), bf16[16,2,112,128]{3,2,1,0:T(8,128)(2,1)S(1)}, u32[]{:S(2)}, u32[]{:S(2)}) async-start(bf16[16,2,112,128]{3,2,1,0:T(8,128)(2,1)} %get-tuple-element.48), calls=%async_computation | async-start | bytes 1835008 | tf_op jit(solution)/shard_map/all_to_all | solution.py:219
  19.8 13.2 %collective-permute-start.10 = (bf16[16,112,128]{2,1,0:T(8,128)(2,1)S(1)}, bf16[16,112,128]{2,1,0:T(8,128)(2,1)S(1)}, u32[]{:S(2)}, u32[]{:S(2)}) collective-permute-start(bf16[16,112,128]{2,1,0:T(8,128)(2,1)S(1)} %pad_maximum_fusion.3), channel_id=1, source_target_pairs={{0,1},{1,2},{2,3},{3,0},{4,5},{5,6},{6,7},{7,4},{8,9},{9,10},{10,1... | collective-permute-start | bytes 1376264 | tf_op jit(solution)/shard_map/ppermute | solution.py:216
  21.4 11.5 %collective-permute-start.11 = (bf16[16,112,128]{2,1,0:T(8,128)(2,1)S(1)}, bf16[16,112,128]{2,1,0:T(8,128)(2,1)S(1)}, u32[]{:S(2)}, u32[]{:S(2)}) collective-permute-start(bf16[16,112,128]{2,1,0:T(8,128)(2,1)S(1)} %pad_maximum_fusion.3), channel_id=1, source_target_pairs={{0,3},{1,0},{2,1},{3,2},{4,7},{5,4},{6,5},{7,6},{8,11},{9,8},{10,9... | collective-permute-start | bytes 1376264 | tf_op jit(solution)/shard_map/ppermute | solution.py:216
  23.1 7.3 %collective-permute-start.5 = (bf16[2,2,112,128]{3,2,1,0:T(8,128)(2,1)S(1)}, bf16[2,2,112,128]{3,2,1,0:T(8,128)(2,1)S(1)}, u32[]{:S(2)}, u32[]{:S(2)}) collective-permute-start(bf16[2,2,112,128]{3,2,1,0:T(8,128)(2,1)S(1)} %get-tuple-element.43), channel_id=1, source_target_pairs={{0,64},{4,68},{8,72},{12,76},{16,80},{20,84},{24,88},{28,92},{32,9... | collective-permute-start | bytes 344072 | tf_op jit(solution)/shard_map/ppermute | solution.py:207
  24.5 11.8 %collective-permute-start.6 = (bf16[2,2,112,128]{3,2,1,0:T(8,128)(2,1)S(1)}, bf16[2,2,112,128]{3,2,1,0:T(8,128)(2,1)S(1)}, u32[]{:S(2)}, u32[]{:S(2)}) collective-permute-start(bf16[2,2,112,128]{3,2,1,0:T(8,128)(2,1)S(1)} %get-tuple-element.44), channel_id=1, source_target_pairs={{0,128},{4,132},{8,136},{12,140},{16,144},{20,148},{24,152},{28,15... | collective-permute-start | bytes 344072 | tf_op jit(solution)/shard_map/ppermute | solution.py:207
  27.2 9.1 %collective-permute-start.7 = (bf16[2,2,112,128]{3,2,1,0:T(8,128)(2,1)S(1)}, bf16[2,2,112,128]{3,2,1,0:T(8,128)(2,1)S(1)}, u32[]{:S(2)}, u32[]{:S(2)}) collective-permute-start(bf16[2,2,112,128]{3,2,1,0:T(8,128)(2,1)S(1)} %get-tuple-element.45), channel_id=1, source_target_pairs={{0,192},{4,196},{8,200},{12,204},{16,208},{20,212},{24,216},{28,22... | collective-permute-start | bytes 344072 | tf_op jit(solution)/shard_map/ppermute | solution.py:207
  33.0 7.3 %collective-permute-start.12 = (bf16[8,112,128]{2,1,0:T(8,128)(2,1)S(1)}, bf16[8,112,128]{2,1,0:T(8,128)(2,1)S(1)}, u32[]{:S(2)}, u32[]{:S(2)}) collective-permute-start(bf16[8,112,128]{2,1,0:T(8,128)(2,1)S(1)} %slice.222), channel_id=1, source_target_pairs={{0,1},{1,2},{2,3},{3,0},{4,5},{5,6},{6,7},{7,4},{8,9},{9,10},{10,1... | collective-permute-start | bytes 688136 | tf_op jit(solution)/shard_map/ppermute | solution.py:216
  34.6 6.0 %collective-permute-start.13 = (bf16[8,112,128]{2,1,0:T(8,128)(2,1)S(1)}, bf16[8,112,128]{2,1,0:T(8,128)(2,1)S(1)}, u32[]{:S(2)}, u32[]{:S(2)}) collective-permute-start(bf16[8,112,128]{2,1,0:T(8,128)(2,1)S(1)} %slice.223), channel_id=1, source_target_pairs={{0,3},{1,0},{2,1},{3,2},{4,7},{5,4},{6,5},{7,6},{8,11},{9,8},{10,9... | collective-permute-start | bytes 688136 | tf_op jit(solution)/shard_map/ppermute | solution.py:216
  44.9 23.4 %collective-permute-start.14 = (bf16[32,112,128]{2,1,0:T(8,128)(2,1)S(1)}, bf16[32,112,128]{2,1,0:T(8,128)(2,1)S(1)}, u32[]{:S(2)}, u32[]{:S(2)}) collective-permute-start(bf16[32,112,128]{2,1,0:T(8,128)(2,1)S(1)} %bitcast.21), channel_id=1, source_target_pairs={{0,1},{1,2},{2,3},{3,0},{4,5},{5,6},{6,7},{7,4},{8,9},{9,10},{10,1... | collective-permute-start | bytes 2752520 | tf_op jit(solution)/shard_map/ppermute | solution.py:216
  46.4 21.9 %collective-permute-start.15 = (bf16[32,112,128]{2,1,0:T(8,128)(2,1)S(1)}, bf16[32,112,128]{2,1,0:T(8,128)(2,1)S(1)}, u32[]{:S(2)}, u32[]{:S(2)}) collective-permute-start(bf16[32,112,128]{2,1,0:T(8,128)(2,1)S(1)} %bitcast.22), channel_id=1, source_target_pairs={{0,3},{1,0},{2,1},{3,2},{4,7},{5,4},{6,5},{7,6},{8,11},{9,8},{10,9... | collective-permute-start | bytes 2752520 | tf_op jit(solution)/shard_map/ppermute | solution.py:216
  48.2 20.1 %collective-permute-start.8 = (bf16[8,112,128]{2,1,0:T(8,128)(2,1)S(1)}, bf16[8,112,128]{2,1,0:T(8,128)(2,1)S(1)}, u32[]{:S(2)}, u32[]{:S(2)}) collective-permute-start(bf16[8,112,128]{2,1,0:T(8,128)(2,1)S(1)} %bitcast.25), channel_id=1, source_target_pairs={{0,24},{4,28},{8,32},{12,36},{16,40},{20,44},{24,48},{28,52},{32,5... | collective-permute-start | bytes 688136 | tf_op jit(solution)/shard_map/ppermute | solution.py:212
  50.5 17.9 %collective-permute-start.9 = (bf16[8,112,128]{2,1,0:T(8,128)(2,1)S(1)}, bf16[8,112,128]{2,1,0:T(8,128)(2,1)S(1)}, u32[]{:S(2)}, u32[]{:S(2)}) collective-permute-start(bf16[8,112,128]{2,1,0:T(8,128)(2,1)S(1)} %bitcast.24), channel_id=1, source_target_pairs={{0,40},{4,44},{8,48},{12,52},{16,56},{20,60},{24,0},{28,4},{32,8},... | collective-permute-start | bytes 688136 | tf_op jit(solution)/shard_map/ppermute | solution.py:212
  68.5 22.6 %collective-permute-start.16 = (bf16[32,112,128]{2,1,0:T(8,128)(2,1)S(1)}, bf16[32,112,128]{2,1,0:T(8,128)(2,1)S(1)}, u32[]{:S(2)}, u32[]{:S(2)}) collective-permute-start(bf16[32,112,128]{2,1,0:T(8,128)(2,1)S(1)} %get-tuple-element.55), channel_id=1, source_target_pairs={{0,1},{1,2},{2,3},{3,0},{4,5},{5,6},{6,7},{7,4},{8,9},{9,10},{10,1... | collective-permute-start | bytes 2752520 | tf_op jit(solution)/shard_map/ppermute | solution.py:216
  70.1 21.0 %collective-permute-start.17 = (bf16[32,112,128]{2,1,0:T(8,128)(2,1)S(1)}, bf16[32,112,128]{2,1,0:T(8,128)(2,1)S(1)}, u32[]{:S(2)}, u32[]{:S(2)}) collective-permute-start(bf16[32,112,128]{2,1,0:T(8,128)(2,1)S(1)} %get-tuple-element.56), channel_id=1, source_target_pairs={{0,3},{1,0},{2,1},{3,2},{4,7},{5,4},{6,5},{7,6},{8,11},{9,8},{10,9... | collective-permute-start | bytes 2752520 | tf_op jit(solution)/shard_map/ppermute | solution.py:216
  73.8 23.3 %collective-permute-start.20 = (bf16[16,112,128]{2,1,0:T(8,128)(2,1)}, bf16[16,112,128]{2,1,0:T(8,128)(2,1)S(1)}, u32[]{:S(2)}, u32[]{:S(2)}) collective-permute-start(bf16[16,112,128]{2,1,0:T(8,128)(2,1)} %get-tuple-element.61), channel_id=1, source_target_pairs={{0,64},{4,68},{8,72},{12,76},{16,80},{20,84},{24,88},{28,92},{32,9... | collective-permute-start | bytes 1376264 | tf_op jit(solution)/shard_map/ppermute | solution.py:230
  73.9 23.1 %collective-permute-start.21 = (bf16[16,112,128]{2,1,0:T(8,128)(2,1)}, bf16[16,112,128]{2,1,0:T(8,128)(2,1)S(1)}, u32[]{:S(2)}, u32[]{:S(2)}) collective-permute-start(bf16[16,112,128]{2,1,0:T(8,128)(2,1)} %get-tuple-element.60), channel_id=1, source_target_pairs={{0,128},{4,132},{8,136},{12,140},{16,144},{20,148},{24,152},{28,15... | collective-permute-start | bytes 1376264 | tf_op jit(solution)/shard_map/ppermute | solution.py:230
  76.9 20.2 %collective-permute-start.22 = (bf16[16,112,128]{2,1,0:T(8,128)(2,1)}, bf16[16,112,128]{2,1,0:T(8,128)(2,1)S(1)}, u32[]{:S(2)}, u32[]{:S(2)}) collective-permute-start(bf16[16,112,128]{2,1,0:T(8,128)(2,1)} %get-tuple-element.59), channel_id=1, source_target_pairs={{0,192},{4,196},{8,200},{12,204},{16,208},{20,212},{24,216},{28,22... | collective-permute-start | bytes 1376264 | tf_op jit(solution)/shard_map/ppermute | solution.py:230
  91.1 8.0 %collective-permute-start.18 = (bf16[8,112,128]{2,1,0:T(8,128)(2,1)S(1)}, bf16[8,112,128]{2,1,0:T(8,128)(2,1)S(1)}, u32[]{:S(2)}, u32[]{:S(2)}) collective-permute-start(bf16[8,112,128]{2,1,0:T(8,128)(2,1)S(1)} %slice.226), channel_id=1, source_target_pairs={{0,1},{1,2},{2,3},{3,0},{4,5},{5,6},{6,7},{7,4},{8,9},{9,10},{10,1... | collective-permute-start | bytes 688136 | tf_op jit(solution)/shard_map/ppermute | solution.py:216
  92.1 6.9 %collective-permute-start.19 = (bf16[8,112,128]{2,1,0:T(8,128)(2,1)S(1)}, bf16[8,112,128]{2,1,0:T(8,128)(2,1)S(1)}, u32[]{:S(2)}, u32[]{:S(2)}) collective-permute-start(bf16[8,112,128]{2,1,0:T(8,128)(2,1)S(1)} %slice.227), channel_id=1, source_target_pairs={{0,3},{1,0},{2,1},{3,2},{4,7},{5,4},{6,5},{7,6},{8,11},{9,8},{10,9... | collective-permute-start | bytes 688136 | tf_op jit(solution)/shard_map/ppermute | solution.py:216

commit v5 on v4

--- a/solution.py
+++ b/solution.py
@@ -228,7 +228,7 @@
         bundle += [h1[0][here[0]], h1[1][here[0]]] + [l1[h] for h in here]
         bundle = jnp.concatenate(bundle)
         bundles.append(lax.ppermute(bundle, "fsdp", along_x(dx)) if dx else bundle)
-    own3 = cross_z((3, 5), cross_x(1, *own1))
+    own3 = cross_z((3, 5), cross_x(1, *h1))
     l3, r3 = cross_y(own3 + [le[:16]], own3 + [re[16:]])
     l4, r4 = cross_y([l3[:8]], [r3[8:16]])
     late = [

time: 101 us -> 101 us (level)
    all_to_all x1, waiting for transfers between devices: 4.23 us -> 0.01 us  [local(): lax.all_to_all(even, 'fsdp', 0, 0, tiled=True, axis_index_groups=same_par...]
    ppermute x5, waiting for transfers between devices: 0.35 us -> 2.08 us  [cross_y(): lax.ppermute(pair[1], 'rep', along_y(-1))]
    ppermute x5, waiting for transfers between devices: 32.2 us -> 33.5 us  [cross_y(): lax.ppermute(pair[0], 'rep', along_y(1))]
  transfers between devices with their start and end apart: 24 -> 24, of which waited for: 7 -> 8; matrix products, arithmetic and copies ran while one was open for 8% -> 8% of each run, Pallas kernels for 5% -> 5%
where the time goes in v5:
time: 101 us
  starting transfers between devices  46.3 us (46%)
  waiting for transfers between devices  36.9 us (37%)
  Pallas kernels  8.88 us (9%)
  local copies, waits for them, and re-layouts  5.73 us (6%)
  other arithmetic  2.82 us (3%)
    ppermute x5, waiting for transfers between devices, cross_y(): lax.ppermute(pair[0], 'rep', along_y(1))  33.5 us
    all_to_all x1, starting transfers between devices, local(): lax.all_to_all(even, 'fsdp', 0, 0, tiled=True, axis_index_groups=same_par...  11.9 us
    ppermute x5, starting transfers between devices, cross_y(): lax.ppermute(pair[1], 'rep', along_y(-1))  9.64 us
    ppermute x4, starting transfers between devices, cross_z(): return [lax.ppermute(p, 'fsdp', along_z(dz)) for dz, p in zip(dzs, pieces)]  7.4 us
    ppermute x5, starting transfers between devices, cross_y(): lax.ppermute(pair[0], 'rep', along_y(1))  6.92 us
    pallas_call x3, Pallas kernels, place_blocks(): pl.pallas_call(functools.partial(place_kernel, blocks, len(arrays)), out_...  6.57 us
    ppermute x3, starting transfers between devices, cross_x(): lax.ppermute(pieces[dx], 'fsdp', along_x(dx))  5.6 us
    unnamed x9, local copies, waits for them, and re-layouts  4.74 us
  transfers between devices with their start and end apart: 24, of which 8 were waited for; matrix products, arithmetic and copies ran while one was open for 8% of the time, Pallas kernels for 5%

profile of v5, /device:TPU:64, one launch (start us, length us, event | category | flops | bytes accessed | tf_op | source)
XLA Modules:
  0.0 101.1 jit_solution(4261030264834989678)
XLA Ops:
  0.0 0.0 collective-permute-start
  0.0 0.5 collective-permute-start.1
  0.5 0.0 collective-permute-start.2
  0.5 1.5 %multiply_convert_fusion = (bf16[4,112,512]{2,1,0:T(8,128)(2,1)S(1)}, bf16[4,112,512]{2,1,0:T(8,128)(2,1)S(1)}) fusion(bf16[4,112,512]{2,1,0:T(8,128)(2,1)} %param.7, f32[112]{0:T(128)} %param.8, bf16[4,112,512]{2,1,0:T(8,128)(2,1)} %param.6), kind=kLoop, calls=%fused_computation.22 | loop fusion | flops 1376256 | bytes 1835456 | tf_op jit(solution)/shard_map/convert_element_type | solution.py:42
  2.1 0.2 fusion.10.refs_5_
  2.3 0.8 select_reduce_fusion.owner
  3.1 0.0 collective-permute-done.2
  3.1 0.1 copy.10.refs_4_
  3.2 0.0 collective-permute-done.refs_2_
  3.2 0.0 collective-permute-done.1.refs_3_
  3.2 2.3 %prepare.1 = (bf16[2,2,112,128]{3,2,1,0:T(8,128)(2,1)S(1)}, bf16[2,2,112,128]{3,2,1,0:T(8,128)(2,1)S(1)}, bf16[2,2,112,128]{3,2,1,0:T(8,128)(2,1)S(1)}, bf16[2,2...) custom-call(s32[8]{0:T(128)S(1)} %select_reduce_fusion.owner, ...), custom_call_target="tpu_custom_call" | custom-call | tf_op jit(solution)/shard_map/prepare/pallas_call | solution.py:94
  5.6 2.0 %collective-permute-start.3 = (bf16[8,112,128]{2,1,0:T(8,128)(2,1)S(1)}, bf16[8,112,128]{2,1,0:T(8,128)(2,1)S(1)}, u32[]{:S(2)}, u32[]{:S(2)}) collective-permute-start(bf16[8,112,128]{2,1,0:T(8,128)(2,1)S(1)} %pad_maximum_fusion.4), channel_id=1, source_target_pairs={{0,8},{4,12},{8,16},{12,20},{16,24},{20,28},{24,32},{28,36},{32,40... | collective-permute-start | bytes 688136 | tf_op jit(solution)/shard_map/ppermute | solution.py:212
  7.6 0.1 collective-permute-start.4
  7.8 11.9 %all-to-all-start = ((bf16[16,2,112,128]{3,2,1,0:T(8,128)(2,1)}), bf16[16,2,112,128]{3,2,1,0:T(8,128)(2,1)S(1)}, u32[]{:S(2)}, u32[]{:S(2)}) async-start(bf16[16,2,112,128]{3,2,1,0:T(8,128)(2,1)} %get-tuple-element.52), calls=%async_computation | async-start | bytes 1835008 | tf_op jit(solution)/shard_map/all_to_all | solution.py:219
  19.7 0.0 collective-permute-done.3
  19.7 0.0 collective-permute-done.4
  19.8 1.7 %collective-permute-start.5 = (bf16[16,112,128]{2,1,0:T(8,128)(2,1)S(1)}, bf16[16,112,128]{2,1,0:T(8,128)(2,1)S(1)}, u32[]{:S(2)}, u32[]{:S(2)}) collective-permute-start(bf16[16,112,128]{2,1,0:T(8,128)(2,1)S(1)} %pad_maximum_fusion.3), channel_id=1, source_target_pairs={{0,1},{1,2},{2,3},{3,0},{4,5},{5,6},{6,7},{7,4},{8,9},{9,10},{10,1... | collective-permute-start | bytes 1376264 | tf_op jit(solution)/shard_map/ppermute | solution.py:216
  21.4 1.7 %collective-permute-start.6 = (bf16[16,112,128]{2,1,0:T(8,128)(2,1)S(1)}, bf16[16,112,128]{2,1,0:T(8,128)(2,1)S(1)}, u32[]{:S(2)}, u32[]{:S(2)}) collective-permute-start(bf16[16,112,128]{2,1,0:T(8,128)(2,1)S(1)} %pad_maximum_fusion.3), channel_id=1, source_target_pairs={{0,3},{1,0},{2,1},{3,2},{4,7},{5,4},{6,5},{7,6},{8,11},{9,8},{10,9... | collective-permute-start | bytes 1376264 | tf_op jit(solution)/shard_map/ppermute | solution.py:216
  23.1 0.7 constant_dynamic-update-slice_fusion.31
  23.7 0.7 constant_dynamic-update-slice_fusion.30
  24.4 8.5 %collective-permute-done.5 = bf16[16,112,128]{2,1,0:T(8,128)(2,1)S(1)} collective-permute-done((bf16[16,112,128]{2,1,0:T(8,128)(2,1)S(1)}, bf16[16,112,128]{2,1,0:T(8,128)(2,1)S(1)}, u32[]{:S(2)}, u32[]{:S(2)}) %collective-permute-start.5) | collective-permute-done | bytes 458784 | tf_op jit(solution)/shard_map/ppermute | solution.py:216
  32.9 0.0 collective-permute-done.6
  33.0 1.6 %collective-permute-start.7 = (bf16[8,112,128]{2,1,0:T(8,128)(2,1)S(1)}, bf16[8,112,128]{2,1,0:T(8,128)(2,1)S(1)}, u32[]{:S(2)}, u32[]{:S(2)}) collective-permute-start(bf16[8,112,128]{2,1,0:T(8,128)(2,1)S(1)} %slice.216), channel_id=1, source_target_pairs={{0,1},{1,2},{2,3},{3,0},{4,5},{5,6},{6,7},{7,4},{8,9},{9,10},{10,1... | collective-permute-start | bytes 688136 | tf_op jit(solution)/shard_map/ppermute | solution.py:216
  34.6 1.7 %collective-permute-start.8 = (bf16[8,112,128]{2,1,0:T(8,128)(2,1)S(1)}, bf16[8,112,128]{2,1,0:T(8,128)(2,1)S(1)}, u32[]{:S(2)}, u32[]{:S(2)}) collective-permute-start(bf16[8,112,128]{2,1,0:T(8,128)(2,1)S(1)} %slice.217), channel_id=1, source_target_pairs={{0,3},{1,0},{2,1},{3,2},{4,7},{5,4},{6,5},{7,6},{8,11},{9,8},{10,9... | collective-permute-start | bytes 688136 | tf_op jit(solution)/shard_map/ppermute | solution.py:216
  36.3 0.7 constant_dynamic-update-slice_fusion.29
  37.0 0.7 constant_dynamic-update-slice_fusion.28
  37.6 2.6 %collective-permute-done.7 = bf16[8,112,128]{2,1,0:T(8,128)(2,1)S(1)} collective-permute-done((bf16[8,112,128]{2,1,0:T(8,128)(2,1)S(1)}, bf16[8,112,128]{2,1,0:T(8,128)(2,1)S(1)}, u32[]{:S(2)}, u32[]{:S(2)}) %collective-permute-start.7) | collective-permute-done | bytes 229408 | tf_op jit(solution)/shard_map/ppermute | solution.py:216
  40.3 0.3 collective-permute-done.8
  40.6 1.5 %collective-permute-start.9 = (bf16[2,2,112,128]{3,2,1,0:T(8,128)(2,1)S(1)}, bf16[2,2,112,128]{3,2,1,0:T(8,128)(2,1)S(1)}, u32[]{:S(2)}, u32[]{:S(2)}) collective-permute-start(bf16[2,2,112,128]{3,2,1,0:T(8,128)(2,1)S(1)} %get-tuple-element.47), channel_id=1, source_target_pairs={{0,64},{4,68},{8,72},{12,76},{16,80},{20,84},{24,88},{28,92},{32,9... | collective-permute-start | bytes 344072 | tf_op jit(solution)/shard_map/ppermute | solution.py:207
  42.1 2.7 %collective-permute-start.10 = (bf16[2,2,112,128]{3,2,1,0:T(8,128)(2,1)S(1)}, bf16[2,2,112,128]{3,2,1,0:T(8,128)(2,1)S(1)}, u32[]{:S(2)}, u32[]{:S(2)}) collective-permute-start(bf16[2,2,112,128]{3,2,1,0:T(8,128)(2,1)S(1)} %get-tuple-element.48), channel_id=1, source_target_pairs={{0,128},{4,132},{8,136},{12,140},{16,144},{20,148},{24,152},{28,15... | collective-permute-start | bytes 344072 | tf_op jit(solution)/shard_map/ppermute | solution.py:207
  44.8 1.5 %collective-permute-start.11 = (bf16[2,2,112,128]{3,2,1,0:T(8,128)(2,1)S(1)}, bf16[2,2,112,128]{3,2,1,0:T(8,128)(2,1)S(1)}, u32[]{:S(2)}, u32[]{:S(2)}) collective-permute-start(bf16[2,2,112,128]{3,2,1,0:T(8,128)(2,1)S(1)} %get-tuple-element.49), channel_id=1, source_target_pairs={{0,192},{4,196},{8,200},{12,204},{16,208},{20,212},{24,216},{28,22... | collective-permute-start | bytes 344072 | tf_op jit(solution)/shard_map/ppermute | solution.py:207
  46.2 1.3 %collective-permute-done.9 = bf16[2,2,112,128]{3,2,1,0:T(8,128)(2,1)S(1)} collective-permute-done((bf16[2,2,112,128]{3,2,1,0:T(8,128)(2,1)S(1)}, bf16[2,2,112,128]{3,2,1,0:T(8,128)(2,1)S(1)}, u32[]{:S(2)}, u32[]{:S(2)}) %collective-permute-start.9) | collective-permute-done | bytes 114720 | tf_op jit(solution)/shard_map/ppermute | solution.py:207
  47.6 0.0 all-to-all-done
  47.6 1.4 %collective-permute-start.14 = (bf16[32,112,128]{2,1,0:T(8,128)(2,1)S(1)}, bf16[32,112,128]{2,1,0:T(8,128)(2,1)S(1)}, u32[]{:S(2)}, u32[]{:S(2)}) collective-permute-start(bf16[32,112,128]{2,1,0:T(8,128)(2,1)S(1)} %bitcast.21), channel_id=1, source_target_pairs={{0,1},{1,2},{2,3},{3,0},{4,5},{5,6},{6,7},{7,4},{8,9},{9,10},{10,1... | collective-permute-start | bytes 2752520 | tf_op jit(solution)/shard_map/ppermute | solution.py:216
  49.0 1.9 %collective-permute-start.15 = (bf16[32,112,128]{2,1,0:T(8,128)(2,1)S(1)}, bf16[32,112,128]{2,1,0:T(8,128)(2,1)S(1)}, u32[]{:S(2)}, u32[]{:S(2)}) collective-permute-start(bf16[32,112,128]{2,1,0:T(8,128)(2,1)S(1)} %bitcast.22), channel_id=1, source_target_pairs={{0,3},{1,0},{2,1},{3,2},{4,7},{5,4},{6,5},{7,6},{8,11},{9,8},{10,9... | collective-permute-start | bytes 2752520 | tf_op jit(solution)/shard_map/ppermute | solution.py:216
  50.9 0.0 collective-permute-done.10
  50.9 0.0 collective-permute-done.11
  51.0 2.1 %collective-permute-start.12 = (bf16[8,112,128]{2,1,0:T(8,128)(2,1)S(1)}, bf16[8,112,128]{2,1,0:T(8,128)(2,1)S(1)}, u32[]{:S(2)}, u32[]{:S(2)}) collective-permute-start(bf16[8,112,128]{2,1,0:T(8,128)(2,1)S(1)} %bitcast.25), channel_id=1, source_target_pairs={{0,24},{4,28},{8,32},{12,36},{16,40},{20,44},{24,48},{28,52},{32,5... | collective-permute-start | bytes 688136 | tf_op jit(solution)/shard_map/ppermute | solution.py:212
  53.2 3.2 %collective-permute-start.13 = (bf16[8,112,128]{2,1,0:T(8,128)(2,1)S(1)}, bf16[8,112,128]{2,1,0:T(8,128)(2,1)S(1)}, u32[]{:S(2)}, u32[]{:S(2)}) collective-permute-start(bf16[8,112,128]{2,1,0:T(8,128)(2,1)S(1)} %bitcast.24), channel_id=1, source_target_pairs={{0,40},{4,44},{8,48},{12,52},{16,56},{20,60},{24,0},{28,4},{32,8},... | collective-permute-start | bytes 688136 | tf_op jit(solution)/shard_map/ppermute | solution.py:212
  56.3 0.7 constant_dynamic-update-slice_fusion.27
  57.0 11.6 %collective-permute-done.14.refs_1_ = bf16[32,112,128]{2,1,0:T(8,128)(2,1)S(1)} collective-permute-done((bf16[32,112,128]{2,1,0:T(8,128)(2,1)S(1)}, bf16[32,112,128]{2,1,0:T(8,128)(2,1)S(1)}, u32[]{:S(2)}, u32[]{:S(2)}) %collective-permute-start.14) | collective-permute-done | bytes 917536 | tf_op jit(solution)/shard_map/ppermute | solution.py:216
  68.7 0.2 collective-permute-done.15.refs_2_
  68.9 0.0 collective-permute-done.12.refs_0_
  68.9 0.0 collective-permute-done.13.refs_1_
  68.9 0.1 pad_maximum_fusion.2
  69.0 1.8 %collective-permute-start.16 = (bf16[32,112,128]{2,1,0:T(8,128)(2,1)S(1)}, bf16[32,112,128]{2,1,0:T(8,128)(2,1)S(1)}, u32[]{:S(2)}, u32[]{:S(2)}) collective-permute-start(bf16[32,112,128]{2,1,0:T(8,128)(2,1)S(1)} %get-tuple-element.55), channel_id=1, source_target_pairs={{0,1},{1,2},{2,3},{3,0},{4,5},{5,6},{6,7},{7,4},{8,9},{9,10},{10,1... | collective-permute-start | bytes 2752520 | tf_op jit(solution)/shard_map/ppermute | solution.py:216
  70.9 1.5 %collective-permute-start.17 = (bf16[32,112,128]{2,1,0:T(8,128)(2,1)S(1)}, bf16[32,112,128]{2,1,0:T(8,128)(2,1)S(1)}, u32[]{:S(2)}, u32[]{:S(2)}) collective-permute-start(bf16[32,112,128]{2,1,0:T(8,128)(2,1)S(1)} %get-tuple-element.56), channel_id=1, source_target_pairs={{0,3},{1,0},{2,1},{3,2},{4,7},{5,4},{6,5},{7,6},{8,11},{9,8},{10,9... | collective-permute-start | bytes 2752520 | tf_op jit(solution)/shard_map/ppermute | solution.py:216
  72.4 0.7 constant_dynamic-update-slice_fusion.26
  73.0 0.7 constant_dynamic-update-slice_fusion.25
  73.7 0.7 constant_dynamic-update-slice_fusion.24
  74.4 0.4 collective-permute-start.20
  74.8 2.7 %collective-permute-start.21 = (bf16[16,112,128]{2,1,0:T(8,128)(2,1)}, bf16[16,112,128]{2,1,0:T(8,128)(2,1)S(1)}, u32[]{:S(2)}, u32[]{:S(2)}) collective-permute-start(bf16[16,112,128]{2,1,0:T(8,128)(2,1)} %get-tuple-element.60), channel_id=1, source_target_pairs={{0,128},{4,132},{8,136},{12,140},{16,144},{20,148},{24,152},{28,15... | collective-permute-start | bytes 1376264 | tf_op jit(solution)/shard_map/ppermute | solution.py:230
  77.5 1.2 %collective-permute-start.22 = (bf16[16,112,128]{2,1,0:T(8,128)(2,1)}, bf16[16,112,128]{2,1,0:T(8,128)(2,1)S(1)}, u32[]{:S(2)}, u32[]{:S(2)}) collective-permute-start(bf16[16,112,128]{2,1,0:T(8,128)(2,1)} %get-tuple-element.59), channel_id=1, source_target_pairs={{0,192},{4,196},{8,200},{12,204},{16,208},{20,212},{24,216},{28,22... | collective-permute-start | bytes 1376264 | tf_op jit(solution)/shard_map/ppermute | solution.py:230
  78.7 10.7 %collective-permute-done.16.refs_3_.refs_2_ = bf16[32,112,128]{2,1,0:T(8,128)(2,1)S(1)} collective-permute-done((bf16[32,112,128]{2,1,0:T(8,128)(2,1)S(1)}, bf16[32,112,128]{2,1,0:T(8,128)(2,1)S(1)}, u32[]{:S(2)}, u32[]{:S(2)}) %collective-permute-start.16) | collective-permute-done | bytes 917536 | tf_op jit(solution)/shard_map/ppermute | solution.py:216
  89.4 1.6 %collective-permute-done.17.refs_4_.refs_3_ = bf16[32,112,128]{2,1,0:T(8,128)(2,1)S(1)} collective-permute-done((bf16[32,112,128]{2,1,0:T(8,128)(2,1)S(1)}, bf16[32,112,128]{2,1,0:T(8,128)(2,1)S(1)}, u32[]{:S(2)}, u32[]{:S(2)}) %collective-permute-start.17) | collective-permute-done | bytes 917536 | tf_op jit(solution)/shard_map/ppermute | solution.py:216
  91.0 0.4 collective-permute-start.18
  91.4 2.9 %collective-permute-start.19 = (bf16[8,112,128]{2,1,0:T(8,128)(2,1)S(1)}, bf16[8,112,128]{2,1,0:T(8,128)(2,1)S(1)}, u32[]{:S(2)}, u32[]{:S(2)}) collective-permute-start(bf16[8,112,128]{2,1,0:T(8,128)(2,1)S(1)} %slice.227), channel_id=1, source_target_pairs={{0,3},{1,0},{2,1},{3,2},{4,7},{5,4},{6,5},{7,6},{8,11},{9,8},{10,9... | collective-permute-start | bytes 688136 | tf_op jit(solution)/shard_map/ppermute | solution.py:216
  94.3 2.7 %place.3.refs_4_ = bf16[7168,512]{1,0:T(8,128)(2,1)} custom-call(s32[64]{0:T(128)S(1)} %copy-done, bf16[32,112,128]{2,1,0:T(8,128)(2,1)S(1)} %bitcast.23, bf16[32,112,128]{2,1,0:T(8,128)(2,1)S(1)} %collective-permute-done.14.refs_1_, bf16[32,112,128]{2,1,0:T(8,128)(2,1)S(1)} %collective-permute-done.15.refs_2_, ...), custom_call_target="tpu_custom_call" | custom-call | bytes 7340032 | tf_op jit(solution)/shard_map/place/pallas_call | solution.py:166
  97.0 0.0 collective-permute-done.20.refs_1_
  97.0 0.0 collective-permute-done.22.refs_3_
  97.0 1.9 %place.4.refs_6_ = bf16[7168,512]{1,0:T(8,128)(2,1)} custom-call(s32[64]{0:T(128)S(1)} %copy-done, bf16[16,112,128]{2,1,0:T(8,128)(2,1)S(1)} %get-tuple-element.62.refs_0_, bf16[16,112,128]{2,1,0:T(8,128)(2,1)S(1)} %collective-permute-done.20.refs_1_, bf16[16,112,128]{2,1,0:T(8,128)(2,1)S(1)} %collective-permute-done.21.refs_2_, ...), custom_call_target="tpu_custom_call", output_to_operand_aliasing={{}: (5, {})} | custom-call | bytes 3670016 | tf_op jit(solution)/shard_map/place/pallas_call | solution.py:166
  99.0 0.0 collective-permute-done.18.refs_4_
  99.0 0.0 collective-permute-done.19.refs_5_
  99.0 1.9 %place.5 = bf16[7168,512]{1,0:T(8,128)(2,1)} custom-call(s32[64]{0:T(128)S(1)} %copy-done, bf16[8,112,128]{2,1,0:T(8,128)(2,1)S(1)} %collective-permute-done.12.refs_0_, bf16[8,112,128]{2,1,0:T(8,128)(2,1)S(1)} %collective-permute-done.13.refs_1_, bf16[32,112,128]{2,1,0:T(8,128)(2,1)S(1)} %collective-permute-done.16.refs_3_.refs_2_, ...), custom_call_target="tpu_custom_call", output_to_operand_aliasing={{}: (7, {})} | custom-call | bytes 3670016 | tf_op jit(solution)/shard_map/place/pallas_call | solution.py:166
  (25 shorter events, 0.4 us)
Async XLA Ops:
  0.0 3.2 %collective-permute-start = (bf16[4,112,512]{2,1,0:T(8,128)(2,1)}, bf16[4,112,512]{2,1,0:T(8,128)(2,1)S(1)}, u32[]{:S(2)}, u32[]{:S(2)}) collective-permute-start(bf16[4,112,512]{2,1,0:T(8,128)(2,1)} %param.6), channel_id=1, source_target_pairs={{0,4},{4,0},{8,12},{12,8},{16,20},{20,16},{24,28},{28,24},{32,36},... | collective-permute-start | bytes 1376264 | tf_op jit(solution)/shard_map/ppermute | solution.py:86
  0.0 3.2 %collective-permute-start.1 = (bf16[4,112,512]{2,1,0:T(8,128)(2,1)}, bf16[4,112,512]{2,1,0:T(8,128)(2,1)S(1)}, u32[]{:S(2)}, u32[]{:S(2)}) collective-permute-start(bf16[4,112,512]{2,1,0:T(8,128)(2,1)} %param.7), channel_id=1, source_target_pairs={{0,4},{4,0},{8,12},{12,8},{16,20},{20,16},{24,28},{28,24},{32,36},... | collective-permute-start | bytes 1376264 | tf_op jit(solution)/shard_map/ppermute | solution.py:87
  0.5 2.5 %collective-permute-start.2 = (f32[112]{0:T(128)}, f32[112]{0:T(128)S(1)}, u32[]{:S(2)}, u32[]{:S(2)}) collective-permute-start(f32[112]{0:T(128)} %param.8), channel_id=1, source_target_pairs={{0,4},{4,0},{8,12},{12,8},{16,20},{20,16},{24,28},{28,24},{32,36},... | collective-permute-start | bytes 1352 | tf_op jit(solution)/shard_map/ppermute | solution.py:88
  5.6 14.0 %collective-permute-start.3 = (bf16[8,112,128]{2,1,0:T(8,128)(2,1)S(1)}, bf16[8,112,128]{2,1,0:T(8,128)(2,1)S(1)}, u32[]{:S(2)}, u32[]{:S(2)}) collective-permute-start(bf16[8,112,128]{2,1,0:T(8,128)(2,1)S(1)} %pad_maximum_fusion.4), channel_id=1, source_target_pairs={{0,8},{4,12},{8,16},{12,20},{16,24},{20,28},{24,32},{28,36},{32,40... | collective-permute-start | bytes 688136 | tf_op jit(solution)/shard_map/ppermute | solution.py:212
  7.6 12.1 %collective-permute-start.4 = (bf16[8,112,128]{2,1,0:T(8,128)(2,1)S(1)}, bf16[8,112,128]{2,1,0:T(8,128)(2,1)S(1)}, u32[]{:S(2)}, u32[]{:S(2)}) collective-permute-start(bf16[8,112,128]{2,1,0:T(8,128)(2,1)S(1)} %pad_maximum_fusion.5), channel_id=1, source_target_pairs={{0,56},{4,60},{8,0},{12,4},{16,8},{20,12},{24,16},{28,20},{32,24},... | collective-permute-start | bytes 688136 | tf_op jit(solution)/shard_map/ppermute | solution.py:212
  7.8 86.6 %copy-start = (s32[64]{0:T(128)S(1)}, s32[64]{0:T(128)}, u32[]{:S(2)}) copy-start(s32[64]{0:T(128)} %matching.5) | copy-start | bytes 772
  7.8 39.8 %all-to-all-start = ((bf16[16,2,112,128]{3,2,1,0:T(8,128)(2,1)}), bf16[16,2,112,128]{3,2,1,0:T(8,128)(2,1)S(1)}, u32[]{:S(2)}, u32[]{:S(2)}) async-start(bf16[16,2,112,128]{3,2,1,0:T(8,128)(2,1)} %get-tuple-element.52), calls=%async_computation | async-start | bytes 1835008 | tf_op jit(solution)/shard_map/all_to_all | solution.py:219
  19.8 13.2 %collective-permute-start.5 = (bf16[16,112,128]{2,1,0:T(8,128)(2,1)S(1)}, bf16[16,112,128]{2,1,0:T(8,128)(2,1)S(1)}, u32[]{:S(2)}, u32[]{:S(2)}) collective-permute-start(bf16[16,112,128]{2,1,0:T(8,128)(2,1)S(1)} %pad_maximum_fusion.3), channel_id=1, source_target_pairs={{0,1},{1,2},{2,3},{3,0},{4,5},{5,6},{6,7},{7,4},{8,9},{9,10},{10,1... | collective-permute-start | bytes 1376264 | tf_op jit(solution)/shard_map/ppermute | solution.py:216
  21.4 11.5 %collective-permute-start.6 = (bf16[16,112,128]{2,1,0:T(8,128)(2,1)S(1)}, bf16[16,112,128]{2,1,0:T(8,128)(2,1)S(1)}, u32[]{:S(2)}, u32[]{:S(2)}) collective-permute-start(bf16[16,112,128]{2,1,0:T(8,128)(2,1)S(1)} %pad_maximum_fusion.3), channel_id=1, source_target_pairs={{0,3},{1,0},{2,1},{3,2},{4,7},{5,4},{6,5},{7,6},{8,11},{9,8},{10,9... | collective-permute-start | bytes 1376264 | tf_op jit(solution)/shard_map/ppermute | solution.py:216
  33.0 7.3 %collective-permute-start.7 = (bf16[8,112,128]{2,1,0:T(8,128)(2,1)S(1)}, bf16[8,112,128]{2,1,0:T(8,128)(2,1)S(1)}, u32[]{:S(2)}, u32[]{:S(2)}) collective-permute-start(bf16[8,112,128]{2,1,0:T(8,128)(2,1)S(1)} %slice.216), channel_id=1, source_target_pairs={{0,1},{1,2},{2,3},{3,0},{4,5},{5,6},{6,7},{7,4},{8,9},{9,10},{10,1... | collective-permute-start | bytes 688136 | tf_op jit(solution)/shard_map/ppermute | solution.py:216
  34.6 6.0 %collective-permute-start.8 = (bf16[8,112,128]{2,1,0:T(8,128)(2,1)S(1)}, bf16[8,112,128]{2,1,0:T(8,128)(2,1)S(1)}, u32[]{:S(2)}, u32[]{:S(2)}) collective-permute-start(bf16[8,112,128]{2,1,0:T(8,128)(2,1)S(1)} %slice.217), channel_id=1, source_target_pairs={{0,3},{1,0},{2,1},{3,2},{4,7},{5,4},{6,5},{7,6},{8,11},{9,8},{10,9... | collective-permute-start | bytes 688136 | tf_op jit(solution)/shard_map/ppermute | solution.py:216
  40.6 6.9 %collective-permute-start.9 = (bf16[2,2,112,128]{3,2,1,0:T(8,128)(2,1)S(1)}, bf16[2,2,112,128]{3,2,1,0:T(8,128)(2,1)S(1)}, u32[]{:S(2)}, u32[]{:S(2)}) collective-permute-start(bf16[2,2,112,128]{3,2,1,0:T(8,128)(2,1)S(1)} %get-tuple-element.47), channel_id=1, source_target_pairs={{0,64},{4,68},{8,72},{12,76},{16,80},{20,84},{24,88},{28,92},{32,9... | collective-permute-start | bytes 344072 | tf_op jit(solution)/shard_map/ppermute | solution.py:207
  42.1 8.8 %collective-permute-start.10 = (bf16[2,2,112,128]{3,2,1,0:T(8,128)(2,1)S(1)}, bf16[2,2,112,128]{3,2,1,0:T(8,128)(2,1)S(1)}, u32[]{:S(2)}, u32[]{:S(2)}) collective-permute-start(bf16[2,2,112,128]{3,2,1,0:T(8,128)(2,1)S(1)} %get-tuple-element.48), channel_id=1, source_target_pairs={{0,128},{4,132},{8,136},{12,140},{16,144},{20,148},{24,152},{28,15... | collective-permute-start | bytes 344072 | tf_op jit(solution)/shard_map/ppermute | solution.py:207
  44.8 6.2 %collective-permute-start.11 = (bf16[2,2,112,128]{3,2,1,0:T(8,128)(2,1)S(1)}, bf16[2,2,112,128]{3,2,1,0:T(8,128)(2,1)S(1)}, u32[]{:S(2)}, u32[]{:S(2)}) collective-permute-start(bf16[2,2,112,128]{3,2,1,0:T(8,128)(2,1)S(1)} %get-tuple-element.49), channel_id=1, source_target_pairs={{0,192},{4,196},{8,200},{12,204},{16,208},{20,212},{24,216},{28,22... | collective-permute-start | bytes 344072 | tf_op jit(solution)/shard_map/ppermute | solution.py:207
  47.6 21.0 %collective-permute-start.14 = (bf16[32,112,128]{2,1,0:T(8,128)(2,1)S(1)}, bf16[32,112,128]{2,1,0:T(8,128)(2,1)S(1)}, u32[]{:S(2)}, u32[]{:S(2)}) collective-permute-start(bf16[32,112,128]{2,1,0:T(8,128)(2,1)S(1)} %bitcast.21), channel_id=1, source_target_pairs={{0,1},{1,2},{2,3},{3,0},{4,5},{5,6},{6,7},{7,4},{8,9},{9,10},{10,1... | collective-permute-start | bytes 2752520 | tf_op jit(solution)/shard_map/ppermute | solution.py:216
  49.0 19.8 %collective-permute-start.15 = (bf16[32,112,128]{2,1,0:T(8,128)(2,1)S(1)}, bf16[32,112,128]{2,1,0:T(8,128)(2,1)S(1)}, u32[]{:S(2)}, u32[]{:S(2)}) collective-permute-start(bf16[32,112,128]{2,1,0:T(8,128)(2,1)S(1)} %bitcast.22), channel_id=1, source_target_pairs={{0,3},{1,0},{2,1},{3,2},{4,7},{5,4},{6,5},{7,6},{8,11},{9,8},{10,9... | collective-permute-start | bytes 2752520 | tf_op jit(solution)/shard_map/ppermute | solution.py:216
  51.0 17.8 %collective-permute-start.12 = (bf16[8,112,128]{2,1,0:T(8,128)(2,1)S(1)}, bf16[8,112,128]{2,1,0:T(8,128)(2,1)S(1)}, u32[]{:S(2)}, u32[]{:S(2)}) collective-permute-start(bf16[8,112,128]{2,1,0:T(8,128)(2,1)S(1)} %bitcast.25), channel_id=1, source_target_pairs={{0,24},{4,28},{8,32},{12,36},{16,40},{20,44},{24,48},{28,52},{32,5... | collective-permute-start | bytes 688136 | tf_op jit(solution)/shard_map/ppermute | solution.py:212
  53.2 15.7 %collective-permute-start.13 = (bf16[8,112,128]{2,1,0:T(8,128)(2,1)S(1)}, bf16[8,112,128]{2,1,0:T(8,128)(2,1)S(1)}, u32[]{:S(2)}, u32[]{:S(2)}) collective-permute-start(bf16[8,112,128]{2,1,0:T(8,128)(2,1)S(1)} %bitcast.24), channel_id=1, source_target_pairs={{0,40},{4,44},{8,48},{12,52},{16,56},{20,60},{24,0},{28,4},{32,8},... | collective-permute-start | bytes 688136 | tf_op jit(solution)/shard_map/ppermute | solution.py:212
  69.0 20.4 %collective-permute-start.16 = (bf16[32,112,128]{2,1,0:T(8,128)(2,1)S(1)}, bf16[32,112,128]{2,1,0:T(8,128)(2,1)S(1)}, u32[]{:S(2)}, u32[]{:S(2)}) collective-permute-start(bf16[32,112,128]{2,1,0:T(8,128)(2,1)S(1)} %get-tuple-element.55), channel_id=1, source_target_pairs={{0,1},{1,2},{2,3},{3,0},{4,5},{5,6},{6,7},{7,4},{8,9},{9,10},{10,1... | collective-permute-start | bytes 2752520 | tf_op jit(solution)/shard_map/ppermute | solution.py:216
  70.9 20.1 %collective-permute-start.17 = (bf16[32,112,128]{2,1,0:T(8,128)(2,1)S(1)}, bf16[32,112,128]{2,1,0:T(8,128)(2,1)S(1)}, u32[]{:S(2)}, u32[]{:S(2)}) collective-permute-start(bf16[32,112,128]{2,1,0:T(8,128)(2,1)S(1)} %get-tuple-element.56), channel_id=1, source_target_pairs={{0,3},{1,0},{2,1},{3,2},{4,7},{5,4},{6,5},{7,6},{8,11},{9,8},{10,9... | collective-permute-start | bytes 2752520 | tf_op jit(solution)/shard_map/ppermute | solution.py:216
  74.4 22.6 %collective-permute-start.20 = (bf16[16,112,128]{2,1,0:T(8,128)(2,1)}, bf16[16,112,128]{2,1,0:T(8,128)(2,1)S(1)}, u32[]{:S(2)}, u32[]{:S(2)}) collective-permute-start(bf16[16,112,128]{2,1,0:T(8,128)(2,1)} %get-tuple-element.61), channel_id=1, source_target_pairs={{0,64},{4,68},{8,72},{12,76},{16,80},{20,84},{24,88},{28,92},{32,9... | collective-permute-start | bytes 1376264 | tf_op jit(solution)/shard_map/ppermute | solution.py:230
  74.8 22.2 %collective-permute-start.21 = (bf16[16,112,128]{2,1,0:T(8,128)(2,1)}, bf16[16,112,128]{2,1,0:T(8,128)(2,1)S(1)}, u32[]{:S(2)}, u32[]{:S(2)}) collective-permute-start(bf16[16,112,128]{2,1,0:T(8,128)(2,1)} %get-tuple-element.60), channel_id=1, source_target_pairs={{0,128},{4,132},{8,136},{12,140},{16,144},{20,148},{24,152},{28,15... | collective-permute-start | bytes 1376264 | tf_op jit(solution)/shard_map/ppermute | solution.py:230
  77.5 19.6 %collective-permute-start.22 = (bf16[16,112,128]{2,1,0:T(8,128)(2,1)}, bf16[16,112,128]{2,1,0:T(8,128)(2,1)S(1)}, u32[]{:S(2)}, u32[]{:S(2)}) collective-permute-start(bf16[16,112,128]{2,1,0:T(8,128)(2,1)} %get-tuple-element.59), channel_id=1, source_target_pairs={{0,192},{4,196},{8,200},{12,204},{16,208},{20,212},{24,216},{28,22... | collective-permute-start | bytes 1376264 | tf_op jit(solution)/shard_map/ppermute | solution.py:230
  91.0 8.0 %collective-permute-start.18 = (bf16[8,112,128]{2,1,0:T(8,128)(2,1)S(1)}, bf16[8,112,128]{2,1,0:T(8,128)(2,1)S(1)}, u32[]{:S(2)}, u32[]{:S(2)}) collective-permute-start(bf16[8,112,128]{2,1,0:T(8,128)(2,1)S(1)} %slice.226), channel_id=1, source_target_pairs={{0,1},{1,2},{2,3},{3,0},{4,5},{5,6},{6,7},{7,4},{8,9},{9,10},{10,1... | collective-permute-start | bytes 688136 | tf_op jit(solution)/shard_map/ppermute | solution.py:216
  91.4 7.6 %collective-permute-start.19 = (bf16[8,112,128]{2,1,0:T(8,128)(2,1)S(1)}, bf16[8,112,128]{2,1,0:T(8,128)(2,1)S(1)}, u32[]{:S(2)}, u32[]{:S(2)}) collective-permute-start(bf16[8,112,128]{2,1,0:T(8,128)(2,1)S(1)} %slice.227), channel_id=1, source_target_pairs={{0,3},{1,0},{2,1},{3,2},{4,7},{5,4},{6,5},{7,6},{8,11},{9,8},{10,9... | collective-permute-start | bytes 688136 | tf_op jit(solution)/shard_map/ppermute | solution.py:216

commit v6 on v4

--- a/solution.py
+++ b/solution.py
@@ -240,13 +240,13 @@
         for at in range(32)
     ]
     out = place_blocks(None, matching, devices, [own, le, re, l3, r3], evens)
-    out = place_blocks(out, matching, devices, bundles, late)
     odds = [
         (GROUPS[1][at // 8], at % 2, None, at % 8 // 2,
          ((at // 8, at % 8), (3, at), (4, at) if at < 8 else (5, at - 8), (2, at)))
         for at in range(16)
     ]
-    out = place_blocks(out, matching, devices, [*own3, l3, r3, l4, r4], odds)
+    late = [(dz, side, xs, dx, tuple((k + 6, at) for k, at in parts)) for dz, side, xs, dx, parts in late]
+    out = place_blocks(out, matching, devices, [*own3, l3, r3, l4, r4, *bundles], late + odds)
     return out[None]
 
 

time: 101 us -> 102 us (level); the launches traced: 101 us -> 101 us
  waiting for transfers between devices: 37.2 us -> 39.6 us
  starting transfers between devices: 46.1 us -> 44.3 us
  Pallas kernels: 8.89 us -> 7.69 us
    ppermute x5, waiting for transfers between devices: 32.2 us -> 39 us  [cross_y(): lax.ppermute(pair[0], 'rep', along_y(1))]
    all_to_all x1, waiting for transfers between devices: 4.23 us -> 0.01 us  [local(): lax.all_to_all(even, 'fsdp', 0, 0, tiled=True, axis_index_groups=same_par...]
    ppermute x3, starting transfers between devices: 4.21 us -> 2.31 us  [local(): bundles.append(lax.ppermute(bundle, 'fsdp', along_x(dx)) if dx else bundle)]
    pallas_call x3 -> x2, Pallas kernels: 6.57 us -> 5.37 us  [place_blocks(): pl.pallas_call(functools.partial(place_kernel, blocks, len(arrays)), out_...]
  transfers between devices with their start and end apart: 24 -> 24, of which waited for: 7 -> 7; matrix products, arithmetic and copies ran while one was open for 8% -> 8% of each run, Pallas kernels for 5% -> 3%
where the time goes in v6:
time: 102 us; the launch traced here: 101 us
  starting transfers between devices  44.3 us (43%)
  waiting for transfers between devices  39.6 us (39%)
  Pallas kernels  7.69 us (8%)
  local copies, waits for them, and re-layouts  5.73 us (6%)
  other arithmetic  2.81 us (3%)
    ppermute x5, waiting for transfers between devices, cross_y(): lax.ppermute(pair[0], 'rep', along_y(1))  39 us
    all_to_all x1, starting transfers between devices, local(): lax.all_to_all(even, 'fsdp', 0, 0, tiled=True, axis_index_groups=same_par...  11.9 us
    ppermute x5, starting transfers between devices, cross_y(): lax.ppermute(pair[1], 'rep', along_y(-1))  9.11 us
    ppermute x4, starting transfers between devices, cross_z(): return [lax.ppermute(p, 'fsdp', along_z(dz)) for dz, p in zip(dzs, pieces)]  7.4 us
    ppermute x5, starting transfers between devices, cross_y(): lax.ppermute(pair[0], 'rep', along_y(1))  7.38 us
    ppermute x3, starting transfers between devices, cross_x(): lax.ppermute(pieces[dx], 'fsdp', along_x(dx))  5.68 us
    pallas_call x2, Pallas kernels, place_blocks(): pl.pallas_call(functools.partial(place_kernel, blocks, len(arrays)), out_...  5.37 us
    unnamed x9, local copies, waits for them, and re-layouts  4.74 us
  transfers between devices with their start and end apart: 24, of which 7 were waited for; matrix products, arithmetic and copies ran while one was open for 8% of the time, Pallas kernels for 3%

profile of v6, /device:TPU:64, one launch (start us, length us, event | category | flops | bytes accessed | tf_op | source)
XLA Modules:
  0.0 100.6 jit_solution(1222120589496720576)
XLA Ops:
  0.0 0.0 collective-permute-start.2
  0.0 0.5 collective-permute-start
  0.5 0.0 collective-permute-start.1
  0.5 1.5 %multiply_convert_fusion = (bf16[4,112,512]{2,1,0:T(8,128)(2,1)S(1)}, bf16[4,112,512]{2,1,0:T(8,128)(2,1)S(1)}) fusion(bf16[4,112,512]{2,1,0:T(8,128)(2,1)} %param.7, f32[112]{0:T(128)} %param.8, bf16[4,112,512]{2,1,0:T(8,128)(2,1)} %param.6), kind=kLoop, calls=%fused_computation.22 | loop fusion | flops 1376256 | bytes 1835456 | tf_op jit(solution)/shard_map/convert_element_type | solution.py:42
  2.1 0.2 fusion.10.refs_5_
  2.3 0.8 select_reduce_fusion.owner
  3.1 0.0 collective-permute-done.2
  3.1 0.1 copy.9.refs_4_
  3.2 0.0 collective-permute-done.refs_2_
  3.2 0.0 collective-permute-done.1.refs_3_
  3.2 2.3 %prepare.1 = (bf16[2,2,112,128]{3,2,1,0:T(8,128)(2,1)S(1)}, bf16[2,2,112,128]{3,2,1,0:T(8,128)(2,1)S(1)}, bf16[2,2,112,128]{3,2,1,0:T(8,128)(2,1)S(1)}, bf16[2,2...) custom-call(s32[8]{0:T(128)S(1)} %select_reduce_fusion.owner, ...), custom_call_target="tpu_custom_call" | custom-call | tf_op jit(solution)/shard_map/prepare/pallas_call | solution.py:94
  5.7 2.0 %collective-permute-start.3 = (bf16[8,112,128]{2,1,0:T(8,128)(2,1)S(1)}, bf16[8,112,128]{2,1,0:T(8,128)(2,1)S(1)}, u32[]{:S(2)}, u32[]{:S(2)}) collective-permute-start(bf16[8,112,128]{2,1,0:T(8,128)(2,1)S(1)} %pad_maximum_fusion.4), channel_id=1, source_target_pairs={{0,8},{4,12},{8,16},{12,20},{16,24},{20,28},{24,32},{28,36},{32,40... | collective-permute-start | bytes 688136 | tf_op jit(solution)/shard_map/ppermute | solution.py:212
  7.6 0.1 collective-permute-start.4
  7.8 11.9 %all-to-all-start = ((bf16[16,2,112,128]{3,2,1,0:T(8,128)(2,1)}), bf16[16,2,112,128]{3,2,1,0:T(8,128)(2,1)S(1)}, u32[]{:S(2)}, u32[]{:S(2)}) async-start(bf16[16,2,112,128]{3,2,1,0:T(8,128)(2,1)} %get-tuple-element.48), calls=%async_computation | async-start | bytes 1835008 | tf_op jit(solution)/shard_map/all_to_all | solution.py:219
  19.7 0.0 collective-permute-done.3
  19.7 0.0 collective-permute-done.4
  19.7 1.5 %collective-permute-start.5 = (bf16[2,2,112,128]{3,2,1,0:T(8,128)(2,1)S(1)}, bf16[2,2,112,128]{3,2,1,0:T(8,128)(2,1)S(1)}, u32[]{:S(2)}, u32[]{:S(2)}) collective-permute-start(bf16[2,2,112,128]{3,2,1,0:T(8,128)(2,1)S(1)} %get-tuple-element.43), channel_id=1, source_target_pairs={{0,64},{4,68},{8,72},{12,76},{16,80},{20,84},{24,88},{28,92},{32,9... | collective-permute-start | bytes 344072 | tf_op jit(solution)/shard_map/ppermute | solution.py:207
  21.2 2.7 %collective-permute-start.6 = (bf16[2,2,112,128]{3,2,1,0:T(8,128)(2,1)S(1)}, bf16[2,2,112,128]{3,2,1,0:T(8,128)(2,1)S(1)}, u32[]{:S(2)}, u32[]{:S(2)}) collective-permute-start(bf16[2,2,112,128]{3,2,1,0:T(8,128)(2,1)S(1)} %get-tuple-element.44), channel_id=1, source_target_pairs={{0,128},{4,132},{8,136},{12,140},{16,144},{20,148},{24,152},{28,15... | collective-permute-start | bytes 344072 | tf_op jit(solution)/shard_map/ppermute | solution.py:207
  23.9 1.5 %collective-permute-start.7 = (bf16[2,2,112,128]{3,2,1,0:T(8,128)(2,1)S(1)}, bf16[2,2,112,128]{3,2,1,0:T(8,128)(2,1)S(1)}, u32[]{:S(2)}, u32[]{:S(2)}) collective-permute-start(bf16[2,2,112,128]{3,2,1,0:T(8,128)(2,1)S(1)} %get-tuple-element.45), channel_id=1, source_target_pairs={{0,192},{4,196},{8,200},{12,204},{16,208},{20,212},{24,216},{28,22... | collective-permute-start | bytes 344072 | tf_op jit(solution)/shard_map/ppermute | solution.py:207
  25.4 1.7 %collective-permute-start.10 = (bf16[16,112,128]{2,1,0:T(8,128)(2,1)S(1)}, bf16[16,112,128]{2,1,0:T(8,128)(2,1)S(1)}, u32[]{:S(2)}, u32[]{:S(2)}) collective-permute-start(bf16[16,112,128]{2,1,0:T(8,128)(2,1)S(1)} %pad_maximum_fusion.3), channel_id=1, source_target_pairs={{0,1},{1,2},{2,3},{3,0},{4,5},{5,6},{6,7},{7,4},{8,9},{9,10},{10,1... | collective-permute-start | bytes 1376264 | tf_op jit(solution)/shard_map/ppermute | solution.py:216
  27.1 1.7 %collective-permute-start.11 = (bf16[16,112,128]{2,1,0:T(8,128)(2,1)S(1)}, bf16[16,112,128]{2,1,0:T(8,128)(2,1)S(1)}, u32[]{:S(2)}, u32[]{:S(2)}) collective-permute-start(bf16[16,112,128]{2,1,0:T(8,128)(2,1)S(1)} %pad_maximum_fusion.3), channel_id=1, source_target_pairs={{0,3},{1,0},{2,1},{3,2},{4,7},{5,4},{6,5},{7,6},{8,11},{9,8},{10,9... | collective-permute-start | bytes 1376264 | tf_op jit(solution)/shard_map/ppermute | solution.py:216
  28.7 0.7 constant_dynamic-update-slice_fusion.31
  29.4 0.7 constant_dynamic-update-slice_fusion.30
  30.1 0.0 collective-permute-done.5
  30.1 7.6 %collective-permute-done.10 = bf16[16,112,128]{2,1,0:T(8,128)(2,1)S(1)} collective-permute-done((bf16[16,112,128]{2,1,0:T(8,128)(2,1)S(1)}, bf16[16,112,128]{2,1,0:T(8,128)(2,1)S(1)}, u32[]{:S(2)}, u32[]{:S(2)}) %collective-permute-start.10) | collective-permute-done | bytes 458784 | tf_op jit(solution)/shard_map/ppermute | solution.py:216
  37.8 0.0 collective-permute-done.11
  37.8 1.6 %collective-permute-start.12 = (bf16[8,112,128]{2,1,0:T(8,128)(2,1)S(1)}, bf16[8,112,128]{2,1,0:T(8,128)(2,1)S(1)}, u32[]{:S(2)}, u32[]{:S(2)}) collective-permute-start(bf16[8,112,128]{2,1,0:T(8,128)(2,1)S(1)} %slice.222), channel_id=1, source_target_pairs={{0,1},{1,2},{2,3},{3,0},{4,5},{5,6},{6,7},{7,4},{8,9},{9,10},{10,1... | collective-permute-start | bytes 688136 | tf_op jit(solution)/shard_map/ppermute | solution.py:216
  39.4 1.7 %collective-permute-start.13 = (bf16[8,112,128]{2,1,0:T(8,128)(2,1)S(1)}, bf16[8,112,128]{2,1,0:T(8,128)(2,1)S(1)}, u32[]{:S(2)}, u32[]{:S(2)}) collective-permute-start(bf16[8,112,128]{2,1,0:T(8,128)(2,1)S(1)} %slice.223), channel_id=1, source_target_pairs={{0,3},{1,0},{2,1},{3,2},{4,7},{5,4},{6,5},{7,6},{8,11},{9,8},{10,9... | collective-permute-start | bytes 688136 | tf_op jit(solution)/shard_map/ppermute | solution.py:216
  41.1 0.0 collective-permute-done.6
  41.1 0.0 collective-permute-done.7
  41.2 4.0 %collective-permute-done.12 = bf16[8,112,128]{2,1,0:T(8,128)(2,1)S(1)} collective-permute-done((bf16[8,112,128]{2,1,0:T(8,128)(2,1)S(1)}, bf16[8,112,128]{2,1,0:T(8,128)(2,1)S(1)}, u32[]{:S(2)}, u32[]{:S(2)}) %collective-permute-start.12) | collective-permute-done | bytes 229408 | tf_op jit(solution)/shard_map/ppermute | solution.py:216
  45.1 0.4 collective-permute-done.13
  45.5 0.0 all-to-all-done
  45.5 1.3 %collective-permute-start.14 = (bf16[32,112,128]{2,1,0:T(8,128)(2,1)S(1)}, bf16[32,112,128]{2,1,0:T(8,128)(2,1)S(1)}, u32[]{:S(2)}, u32[]{:S(2)}) collective-permute-start(bf16[32,112,128]{2,1,0:T(8,128)(2,1)S(1)} %bitcast.21), channel_id=1, source_target_pairs={{0,1},{1,2},{2,3},{3,0},{4,5},{5,6},{6,7},{7,4},{8,9},{9,10},{10,1... | collective-permute-start | bytes 2752520 | tf_op jit(solution)/shard_map/ppermute | solution.py:216
  46.8 2.0 %collective-permute-start.15 = (bf16[32,112,128]{2,1,0:T(8,128)(2,1)S(1)}, bf16[32,112,128]{2,1,0:T(8,128)(2,1)S(1)}, u32[]{:S(2)}, u32[]{:S(2)}) collective-permute-start(bf16[32,112,128]{2,1,0:T(8,128)(2,1)S(1)} %bitcast.22), channel_id=1, source_target_pairs={{0,3},{1,0},{2,1},{3,2},{4,7},{5,4},{6,5},{7,6},{8,11},{9,8},{10,9... | collective-permute-start | bytes 2752520 | tf_op jit(solution)/shard_map/ppermute | solution.py:216
  48.8 3.1 %collective-permute-start.8 = (bf16[8,112,128]{2,1,0:T(8,128)(2,1)S(1)}, bf16[8,112,128]{2,1,0:T(8,128)(2,1)S(1)}, u32[]{:S(2)}, u32[]{:S(2)}) collective-permute-start(bf16[8,112,128]{2,1,0:T(8,128)(2,1)S(1)} %bitcast.25), channel_id=1, source_target_pairs={{0,24},{4,28},{8,32},{12,36},{16,40},{20,44},{24,48},{28,52},{32,5... | collective-permute-start | bytes 688136 | tf_op jit(solution)/shard_map/ppermute | solution.py:212
  51.9 2.2 %collective-permute-start.9 = (bf16[8,112,128]{2,1,0:T(8,128)(2,1)S(1)}, bf16[8,112,128]{2,1,0:T(8,128)(2,1)S(1)}, u32[]{:S(2)}, u32[]{:S(2)}) collective-permute-start(bf16[8,112,128]{2,1,0:T(8,128)(2,1)S(1)} %bitcast.24), channel_id=1, source_target_pairs={{0,40},{4,44},{8,48},{12,52},{16,56},{20,60},{24,0},{28,4},{32,8},... | collective-permute-start | bytes 688136 | tf_op jit(solution)/shard_map/ppermute | solution.py:212
  54.1 0.7 constant_dynamic-update-slice_fusion.29
  54.8 0.7 constant_dynamic-update-slice_fusion.28
  55.4 0.7 constant_dynamic-update-slice_fusion.27
  56.1 12.1 %collective-permute-done.14.refs_1_ = bf16[32,112,128]{2,1,0:T(8,128)(2,1)S(1)} collective-permute-done((bf16[32,112,128]{2,1,0:T(8,128)(2,1)S(1)}, bf16[32,112,128]{2,1,0:T(8,128)(2,1)S(1)}, u32[]{:S(2)}, u32[]{:S(2)}) %collective-permute-start.14) | collective-permute-done | bytes 917536 | tf_op jit(solution)/shard_map/ppermute | solution.py:216
  68.3 0.0 collective-permute-done.15.refs_2_
  68.3 0.0 collective-permute-done.8.refs_0_
  68.3 0.0 collective-permute-done.9.refs_1_
  68.3 0.1 pad_maximum_fusion.2
  68.5 1.6 %collective-permute-start.16 = (bf16[32,112,128]{2,1,0:T(8,128)(2,1)S(1)}, bf16[32,112,128]{2,1,0:T(8,128)(2,1)S(1)}, u32[]{:S(2)}, u32[]{:S(2)}) collective-permute-start(bf16[32,112,128]{2,1,0:T(8,128)(2,1)S(1)} %get-tuple-element.55), channel_id=1, source_target_pairs={{0,1},{1,2},{2,3},{3,0},{4,5},{5,6},{6,7},{7,4},{8,9},{9,10},{10,1... | collective-permute-start | bytes 2752520 | tf_op jit(solution)/shard_map/ppermute | solution.py:216
  70.1 1.7 %collective-permute-start.17 = (bf16[32,112,128]{2,1,0:T(8,128)(2,1)S(1)}, bf16[32,112,128]{2,1,0:T(8,128)(2,1)S(1)}, u32[]{:S(2)}, u32[]{:S(2)}) collective-permute-start(bf16[32,112,128]{2,1,0:T(8,128)(2,1)S(1)} %get-tuple-element.56), channel_id=1, source_target_pairs={{0,3},{1,0},{2,1},{3,2},{4,7},{5,4},{6,5},{7,6},{8,11},{9,8},{10,9... | collective-permute-start | bytes 2752520 | tf_op jit(solution)/shard_map/ppermute | solution.py:216
  71.8 0.7 constant_dynamic-update-slice_fusion.26
  72.5 0.7 constant_dynamic-update-slice_fusion.25
  73.1 0.7 constant_dynamic-update-slice_fusion.24
  73.8 0.9 collective-permute-start.22
  74.7 1.0 collective-permute-start.21
  75.7 0.4 collective-permute-start.20
  76.1 14.2 %collective-permute-done.16.refs_3_.refs_2_ = bf16[32,112,128]{2,1,0:T(8,128)(2,1)S(1)} collective-permute-done((bf16[32,112,128]{2,1,0:T(8,128)(2,1)S(1)}, bf16[32,112,128]{2,1,0:T(8,128)(2,1)S(1)}, u32[]{:S(2)}, u32[]{:S(2)}) %collective-permute-start.16) | collective-permute-done | bytes 917536 | tf_op jit(solution)/shard_map/ppermute | solution.py:216
  90.4 0.0 collective-permute-done.17.refs_4_.refs_3_
  90.4 1.2 %collective-permute-start.18 = (bf16[8,112,128]{2,1,0:T(8,128)(2,1)S(1)}, bf16[8,112,128]{2,1,0:T(8,128)(2,1)S(1)}, u32[]{:S(2)}, u32[]{:S(2)}) collective-permute-start(bf16[8,112,128]{2,1,0:T(8,128)(2,1)S(1)} %slice.226), channel_id=1, source_target_pairs={{0,1},{1,2},{2,3},{3,0},{4,5},{5,6},{6,7},{7,4},{8,9},{9,10},{10,1... | collective-permute-start | bytes 688136 | tf_op jit(solution)/shard_map/ppermute | solution.py:216
  91.6 2.1 %collective-permute-start.19 = (bf16[8,112,128]{2,1,0:T(8,128)(2,1)S(1)}, bf16[8,112,128]{2,1,0:T(8,128)(2,1)S(1)}, u32[]{:S(2)}, u32[]{:S(2)}) collective-permute-start(bf16[8,112,128]{2,1,0:T(8,128)(2,1)S(1)} %slice.227), channel_id=1, source_target_pairs={{0,3},{1,0},{2,1},{3,2},{4,7},{5,4},{6,5},{7,6},{8,11},{9,8},{10,9... | collective-permute-start | bytes 688136 | tf_op jit(solution)/shard_map/ppermute | solution.py:216
  93.7 2.7 %place.2.refs_10_ = bf16[7168,512]{1,0:T(8,128)(2,1)} custom-call(s32[64]{0:T(128)S(1)} %copy-done, bf16[32,112,128]{2,1,0:T(8,128)(2,1)S(1)} %bitcast.23, bf16[32,112,128]{2,1,0:T(8,128)(2,1)S(1)} %collective-permute-done.14.refs_1_, bf16[32,112,128]{2,1,0:T(8,128)(2,1)S(1)} %collective-permute-done.15.refs_2_, ...), custom_call_target="tpu_custom_call" | custom-call | bytes 7340032 | tf_op jit(solution)/shard_map/place/pallas_call | solution.py:166
  96.4 0.0 collective-permute-done.22.refs_9_
  96.4 0.0 collective-permute-done.21.refs_8_
  96.4 0.2 collective-permute-done.20.refs_7_
  96.6 1.1 %collective-permute-done.18.refs_4_ = bf16[8,112,128]{2,1,0:T(8,128)(2,1)S(1)} collective-permute-done((bf16[8,112,128]{2,1,0:T(8,128)(2,1)S(1)}, bf16[8,112,128]{2,1,0:T(8,128)(2,1)S(1)}, u32[]{:S(2)}, u32[]{:S(2)}) %collective-permute-start.18) | collective-permute-done | bytes 229408 | tf_op jit(solution)/shard_map/ppermute | solution.py:216
  97.7 0.0 collective-permute-done.19.refs_5_
  97.7 2.7 %place.3 = bf16[7168,512]{1,0:T(8,128)(2,1)} custom-call(s32[64]{0:T(128)S(1)} %copy-done, bf16[8,112,128]{2,1,0:T(8,128)(2,1)S(1)} %collective-permute-done.8.refs_0_, bf16[8,112,128]{2,1,0:T(8,128)(2,1)S(1)} %collective-permute-done.9.refs_1_, bf16[32,112,128]{2,1,0:T(8,128)(2,1)S(1)} %collective-permute-done.16.refs_3_.refs_2_, ...), custom_call_target="tpu_custom_call", output_to_operand_aliasing={{}: (11, {})} | custom-call | bytes 7340032 | tf_op jit(solution)/shard_map/place/pallas_call | solution.py:166
  (24 shorter events, 0.4 us)
Async XLA Ops:
  0.0 3.1 %collective-permute-start.2 = (f32[112]{0:T(128)}, f32[112]{0:T(128)S(1)}, u32[]{:S(2)}, u32[]{:S(2)}) collective-permute-start(f32[112]{0:T(128)} %param.8), channel_id=1, source_target_pairs={{0,4},{4,0},{8,12},{12,8},{16,20},{20,16},{24,28},{28,24},{32,36},... | collective-permute-start | bytes 1352 | tf_op jit(solution)/shard_map/ppermute | solution.py:88
  0.0 3.2 %collective-permute-start = (bf16[4,112,512]{2,1,0:T(8,128)(2,1)}, bf16[4,112,512]{2,1,0:T(8,128)(2,1)S(1)}, u32[]{:S(2)}, u32[]{:S(2)}) collective-permute-start(bf16[4,112,512]{2,1,0:T(8,128)(2,1)} %param.6), channel_id=1, source_target_pairs={{0,4},{4,0},{8,12},{12,8},{16,20},{20,16},{24,28},{28,24},{32,36},... | collective-permute-start | bytes 1376264 | tf_op jit(solution)/shard_map/ppermute | solution.py:86
  0.5 2.7 %collective-permute-start.1 = (bf16[4,112,512]{2,1,0:T(8,128)(2,1)}, bf16[4,112,512]{2,1,0:T(8,128)(2,1)S(1)}, u32[]{:S(2)}, u32[]{:S(2)}) collective-permute-start(bf16[4,112,512]{2,1,0:T(8,128)(2,1)} %param.7), channel_id=1, source_target_pairs={{0,4},{4,0},{8,12},{12,8},{16,20},{20,16},{24,28},{28,24},{32,36},... | collective-permute-start | bytes 1376264 | tf_op jit(solution)/shard_map/ppermute | solution.py:87
  5.7 14.0 %collective-permute-start.3 = (bf16[8,112,128]{2,1,0:T(8,128)(2,1)S(1)}, bf16[8,112,128]{2,1,0:T(8,128)(2,1)S(1)}, u32[]{:S(2)}, u32[]{:S(2)}) collective-permute-start(bf16[8,112,128]{2,1,0:T(8,128)(2,1)S(1)} %pad_maximum_fusion.4), channel_id=1, source_target_pairs={{0,8},{4,12},{8,16},{12,20},{16,24},{20,28},{24,32},{28,36},{32,40... | collective-permute-start | bytes 688136 | tf_op jit(solution)/shard_map/ppermute | solution.py:212
  7.6 12.1 %collective-permute-start.4 = (bf16[8,112,128]{2,1,0:T(8,128)(2,1)S(1)}, bf16[8,112,128]{2,1,0:T(8,128)(2,1)S(1)}, u32[]{:S(2)}, u32[]{:S(2)}) collective-permute-start(bf16[8,112,128]{2,1,0:T(8,128)(2,1)S(1)} %pad_maximum_fusion.5), channel_id=1, source_target_pairs={{0,56},{4,60},{8,0},{12,4},{16,8},{20,12},{24,16},{28,20},{32,24},... | collective-permute-start | bytes 688136 | tf_op jit(solution)/shard_map/ppermute | solution.py:212
  7.8 86.0 %copy-start = (s32[64]{0:T(128)S(1)}, s32[64]{0:T(128)}, u32[]{:S(2)}) copy-start(s32[64]{0:T(128)} %matching.3) | copy-start | bytes 772
  7.8 37.7 %all-to-all-start = ((bf16[16,2,112,128]{3,2,1,0:T(8,128)(2,1)}), bf16[16,2,112,128]{3,2,1,0:T(8,128)(2,1)S(1)}, u32[]{:S(2)}, u32[]{:S(2)}) async-start(bf16[16,2,112,128]{3,2,1,0:T(8,128)(2,1)} %get-tuple-element.48), calls=%async_computation | async-start | bytes 1835008 | tf_op jit(solution)/shard_map/all_to_all | solution.py:219
  19.7 10.4 %collective-permute-start.5 = (bf16[2,2,112,128]{3,2,1,0:T(8,128)(2,1)S(1)}, bf16[2,2,112,128]{3,2,1,0:T(8,128)(2,1)S(1)}, u32[]{:S(2)}, u32[]{:S(2)}) collective-permute-start(bf16[2,2,112,128]{3,2,1,0:T(8,128)(2,1)S(1)} %get-tuple-element.43), channel_id=1, source_target_pairs={{0,64},{4,68},{8,72},{12,76},{16,80},{20,84},{24,88},{28,92},{32,9... | collective-permute-start | bytes 344072 | tf_op jit(solution)/shard_map/ppermute | solution.py:207
  21.2 19.9 %collective-permute-start.6 = (bf16[2,2,112,128]{3,2,1,0:T(8,128)(2,1)S(1)}, bf16[2,2,112,128]{3,2,1,0:T(8,128)(2,1)S(1)}, u32[]{:S(2)}, u32[]{:S(2)}) collective-permute-start(bf16[2,2,112,128]{3,2,1,0:T(8,128)(2,1)S(1)} %get-tuple-element.44), channel_id=1, source_target_pairs={{0,128},{4,132},{8,136},{12,140},{16,144},{20,148},{24,152},{28,15... | collective-permute-start | bytes 344072 | tf_op jit(solution)/shard_map/ppermute | solution.py:207
  23.9 17.2 %collective-permute-start.7 = (bf16[2,2,112,128]{3,2,1,0:T(8,128)(2,1)S(1)}, bf16[2,2,112,128]{3,2,1,0:T(8,128)(2,1)S(1)}, u32[]{:S(2)}, u32[]{:S(2)}) collective-permute-start(bf16[2,2,112,128]{3,2,1,0:T(8,128)(2,1)S(1)} %get-tuple-element.45), channel_id=1, source_target_pairs={{0,192},{4,196},{8,200},{12,204},{16,208},{20,212},{24,216},{28,22... | collective-permute-start | bytes 344072 | tf_op jit(solution)/shard_map/ppermute | solution.py:207
  25.4 12.3 %collective-permute-start.10 = (bf16[16,112,128]{2,1,0:T(8,128)(2,1)S(1)}, bf16[16,112,128]{2,1,0:T(8,128)(2,1)S(1)}, u32[]{:S(2)}, u32[]{:S(2)}) collective-permute-start(bf16[16,112,128]{2,1,0:T(8,128)(2,1)S(1)} %pad_maximum_fusion.3), channel_id=1, source_target_pairs={{0,1},{1,2},{2,3},{3,0},{4,5},{5,6},{6,7},{7,4},{8,9},{9,10},{10,1... | collective-permute-start | bytes 1376264 | tf_op jit(solution)/shard_map/ppermute | solution.py:216
  27.1 10.7 %collective-permute-start.11 = (bf16[16,112,128]{2,1,0:T(8,128)(2,1)S(1)}, bf16[16,112,128]{2,1,0:T(8,128)(2,1)S(1)}, u32[]{:S(2)}, u32[]{:S(2)}) collective-permute-start(bf16[16,112,128]{2,1,0:T(8,128)(2,1)S(1)} %pad_maximum_fusion.3), channel_id=1, source_target_pairs={{0,3},{1,0},{2,1},{3,2},{4,7},{5,4},{6,5},{7,6},{8,11},{9,8},{10,9... | collective-permute-start | bytes 1376264 | tf_op jit(solution)/shard_map/ppermute | solution.py:216
  37.8 7.3 %collective-permute-start.12 = (bf16[8,112,128]{2,1,0:T(8,128)(2,1)S(1)}, bf16[8,112,128]{2,1,0:T(8,128)(2,1)S(1)}, u32[]{:S(2)}, u32[]{:S(2)}) collective-permute-start(bf16[8,112,128]{2,1,0:T(8,128)(2,1)S(1)} %slice.222), channel_id=1, source_target_pairs={{0,1},{1,2},{2,3},{3,0},{4,5},{5,6},{6,7},{7,4},{8,9},{9,10},{10,1... | collective-permute-start | bytes 688136 | tf_op jit(solution)/shard_map/ppermute | solution.py:216
  39.4 6.0 %collective-permute-start.13 = (bf16[8,112,128]{2,1,0:T(8,128)(2,1)S(1)}, bf16[8,112,128]{2,1,0:T(8,128)(2,1)S(1)}, u32[]{:S(2)}, u32[]{:S(2)}) collective-permute-start(bf16[8,112,128]{2,1,0:T(8,128)(2,1)S(1)} %slice.223), channel_id=1, source_target_pairs={{0,3},{1,0},{2,1},{3,2},{4,7},{5,4},{6,5},{7,6},{8,11},{9,8},{10,9... | collective-permute-start | bytes 688136 | tf_op jit(solution)/shard_map/ppermute | solution.py:216
  45.5 22.7 %collective-permute-start.14 = (bf16[32,112,128]{2,1,0:T(8,128)(2,1)S(1)}, bf16[32,112,128]{2,1,0:T(8,128)(2,1)S(1)}, u32[]{:S(2)}, u32[]{:S(2)}) collective-permute-start(bf16[32,112,128]{2,1,0:T(8,128)(2,1)S(1)} %bitcast.21), channel_id=1, source_target_pairs={{0,1},{1,2},{2,3},{3,0},{4,5},{5,6},{6,7},{7,4},{8,9},{9,10},{10,1... | collective-permute-start | bytes 2752520 | tf_op jit(solution)/shard_map/ppermute | solution.py:216
  46.8 21.5 %collective-permute-start.15 = (bf16[32,112,128]{2,1,0:T(8,128)(2,1)S(1)}, bf16[32,112,128]{2,1,0:T(8,128)(2,1)S(1)}, u32[]{:S(2)}, u32[]{:S(2)}) collective-permute-start(bf16[32,112,128]{2,1,0:T(8,128)(2,1)S(1)} %bitcast.22), channel_id=1, source_target_pairs={{0,3},{1,0},{2,1},{3,2},{4,7},{5,4},{6,5},{7,6},{8,11},{9,8},{10,9... | collective-permute-start | bytes 2752520 | tf_op jit(solution)/shard_map/ppermute | solution.py:216
  48.8 19.5 %collective-permute-start.8 = (bf16[8,112,128]{2,1,0:T(8,128)(2,1)S(1)}, bf16[8,112,128]{2,1,0:T(8,128)(2,1)S(1)}, u32[]{:S(2)}, u32[]{:S(2)}) collective-permute-start(bf16[8,112,128]{2,1,0:T(8,128)(2,1)S(1)} %bitcast.25), channel_id=1, source_target_pairs={{0,24},{4,28},{8,32},{12,36},{16,40},{20,44},{24,48},{28,52},{32,5... | collective-permute-start | bytes 688136 | tf_op jit(solution)/shard_map/ppermute | solution.py:212
  51.9 16.5 %collective-permute-start.9 = (bf16[8,112,128]{2,1,0:T(8,128)(2,1)S(1)}, bf16[8,112,128]{2,1,0:T(8,128)(2,1)S(1)}, u32[]{:S(2)}, u32[]{:S(2)}) collective-permute-start(bf16[8,112,128]{2,1,0:T(8,128)(2,1)S(1)} %bitcast.24), channel_id=1, source_target_pairs={{0,40},{4,44},{8,48},{12,52},{16,56},{20,60},{24,0},{28,4},{32,8},... | collective-permute-start | bytes 688136 | tf_op jit(solution)/shard_map/ppermute | solution.py:212
  68.5 21.9 %collective-permute-start.16 = (bf16[32,112,128]{2,1,0:T(8,128)(2,1)S(1)}, bf16[32,112,128]{2,1,0:T(8,128)(2,1)S(1)}, u32[]{:S(2)}, u32[]{:S(2)}) collective-permute-start(bf16[32,112,128]{2,1,0:T(8,128)(2,1)S(1)} %get-tuple-element.55), channel_id=1, source_target_pairs={{0,1},{1,2},{2,3},{3,0},{4,5},{5,6},{6,7},{7,4},{8,9},{9,10},{10,1... | collective-permute-start | bytes 2752520 | tf_op jit(solution)/shard_map/ppermute | solution.py:216
  70.1 20.3 %collective-permute-start.17 = (bf16[32,112,128]{2,1,0:T(8,128)(2,1)S(1)}, bf16[32,112,128]{2,1,0:T(8,128)(2,1)S(1)}, u32[]{:S(2)}, u32[]{:S(2)}) collective-permute-start(bf16[32,112,128]{2,1,0:T(8,128)(2,1)S(1)} %get-tuple-element.56), channel_id=1, source_target_pairs={{0,3},{1,0},{2,1},{3,2},{4,7},{5,4},{6,5},{7,6},{8,11},{9,8},{10,9... | collective-permute-start | bytes 2752520 | tf_op jit(solution)/shard_map/ppermute | solution.py:216
  73.8 22.6 %collective-permute-start.22 = (bf16[16,112,128]{2,1,0:T(8,128)(2,1)}, bf16[16,112,128]{2,1,0:T(8,128)(2,1)S(1)}, u32[]{:S(2)}, u32[]{:S(2)}) collective-permute-start(bf16[16,112,128]{2,1,0:T(8,128)(2,1)} %get-tuple-element.59), channel_id=1, source_target_pairs={{0,192},{4,196},{8,200},{12,204},{16,208},{20,212},{24,216},{28,22... | collective-permute-start | bytes 1376264 | tf_op jit(solution)/shard_map/ppermute | solution.py:230
  74.7 21.7 %collective-permute-start.21 = (bf16[16,112,128]{2,1,0:T(8,128)(2,1)}, bf16[16,112,128]{2,1,0:T(8,128)(2,1)S(1)}, u32[]{:S(2)}, u32[]{:S(2)}) collective-permute-start(bf16[16,112,128]{2,1,0:T(8,128)(2,1)} %get-tuple-element.60), channel_id=1, source_target_pairs={{0,128},{4,132},{8,136},{12,140},{16,144},{20,148},{24,152},{28,15... | collective-permute-start | bytes 1376264 | tf_op jit(solution)/shard_map/ppermute | solution.py:230
  75.7 20.9 %collective-permute-start.20 = (bf16[16,112,128]{2,1,0:T(8,128)(2,1)}, bf16[16,112,128]{2,1,0:T(8,128)(2,1)S(1)}, u32[]{:S(2)}, u32[]{:S(2)}) collective-permute-start(bf16[16,112,128]{2,1,0:T(8,128)(2,1)} %get-tuple-element.61), channel_id=1, source_target_pairs={{0,64},{4,68},{8,72},{12,76},{16,80},{20,84},{24,88},{28,92},{32,9... | collective-permute-start | bytes 1376264 | tf_op jit(solution)/shard_map/ppermute | solution.py:230
  90.4 7.3 %collective-permute-start.18 = (bf16[8,112,128]{2,1,0:T(8,128)(2,1)S(1)}, bf16[8,112,128]{2,1,0:T(8,128)(2,1)S(1)}, u32[]{:S(2)}, u32[]{:S(2)}) collective-permute-start(bf16[8,112,128]{2,1,0:T(8,128)(2,1)S(1)} %slice.226), channel_id=1, source_target_pairs={{0,1},{1,2},{2,3},{3,0},{4,5},{5,6},{6,7},{7,4},{8,9},{9,10},{10,1... | collective-permute-start | bytes 688136 | tf_op jit(solution)/shard_map/ppermute | solution.py:216
  91.6 6.1 %collective-permute-start.19 = (bf16[8,112,128]{2,1,0:T(8,128)(2,1)S(1)}, bf16[8,112,128]{2,1,0:T(8,128)(2,1)S(1)}, u32[]{:S(2)}, u32[]{:S(2)}) collective-permute-start(bf16[8,112,128]{2,1,0:T(8,128)(2,1)S(1)} %slice.227), channel_id=1, source_target_pairs={{0,3},{1,0},{2,1},{3,2},{4,7},{5,4},{6,5},{7,6},{8,11},{9,8},{10,9... | collective-permute-start | bytes 688136 | tf_op jit(solution)/shard_map/ppermute | solution.py:216
